TPU v7x, 32 devices: a whole 2x2x4 slice. The times are simulated.
32 devices in a mesh: batch: 2 (over core), seq: 4 (over y, x), head: 4 (over z).
Axes of the slice: x: 2, y: 2, z: 4, core: 2. Of those that a mesh axis runs over, the one named last changes fastest.
Arguments:
- tokens: bfloat16 [4096, 1024], P(('batch', 'seq', 'head')), may hold values from -6 to 6
- doc_ids: int32 [4096], P(('batch', 'seq')), may hold values from 0 to 2, as said below
- norm_gain: float32 [1024], replicated, may hold values from 0.1 to 1.9
- w_query: bfloat16 [1024, 1024], P(None, 'head'), may hold values from -0.1875 to 0.1875
- w_key: bfloat16 [1024, 2048], P(None, 'head'), may hold values from -0.1875 to 0.1875
- w_value: bfloat16 [1024, 2048], P(None, 'head'), may hold values from -0.1875 to 0.1875
- w_beta: bfloat16 [1024, 16], P(None, 'head'), may hold values from -0.1875 to 0.1875
- w_decay: bfloat16 [1024, 8], P(None, 'head'), may hold values from -0.1875 to 0.1875
- w_outgate: bfloat16 [1024, 1024], P(None, 'head'), may hold values from -0.1875 to 0.1875
- conv_query: bfloat16 [4, 1024], P(None, 'head'), may hold values from -3 to 3
- conv_key: bfloat16 [4, 2048], P(None, 'head'), may hold values from -1 to 1
- conv_value: bfloat16 [4, 2048], P(None, 'head'), may hold values from -3 to 3
- decay_log: float32 [8], P('head'), may hold values from -15 to -3
- out_gain: float32 [1024], P('head'), may hold values from 0.1 to 1.9
- w_out: bfloat16 [1024, 1024], P('head'), may hold values from -0.1875 to 0.1875
- mlp_gain: float32 [1024], replicated, may hold values from 0.1 to 1.9
- w_gate: bfloat16 [1024, 2816], replicated, may hold values from -0.1875 to 0.1875
- w_up: bfloat16 [1024, 2816], replicated, may hold values from -0.1875 to 0.1875
- w_down: bfloat16 [2816, 1024], replicated, may hold values from -0.109375 to 0.109375
- cotangent: bfloat16 [4096, 1024], P(('batch', 'seq', 'head')), may hold values from -6 to 6
Outputs:
- block_out: bfloat16 [4096, 1024], P(('batch', 'seq', 'head'))
- grad_tokens: float32 [4096, 1024], P(('batch', 'seq', 'head'))
- grad_norm_gain: float32 [1024], P(('batch', 'seq', 'head'))
- grad_w_query: float32 [1024, 1024], P(('batch', 'seq'), 'head')
- grad_w_key: float32 [1024, 2048], P(('batch', 'seq'), 'head')
- grad_w_value: float32 [1024, 2048], P(('batch', 'seq'), 'head')
- grad_w_beta: float32 [1024, 16], P(('batch', 'seq'), 'head')
- grad_w_decay: float32 [1024, 8], P(('batch', 'seq'), 'head')
- grad_w_outgate: float32 [1024, 1024], P(('batch', 'seq'), 'head')
- grad_conv_query: float32 [4, 1024], P(None, 'head')
- grad_conv_key: float32 [4, 2048], P(None, 'head')
- grad_conv_value: float32 [4, 2048], P(None, 'head')
- grad_decay_log: float32 [8], P('head')
- grad_out_gain: float32 [1024], P('head')
- grad_w_out: float32 [1024, 1024], P('head', ('batch', 'seq'))
- grad_mlp_gain: float32 [1024], P(('batch', 'seq', 'head'))
- grad_w_gate: float32 [1024, 2816], P(('batch', 'seq', 'head'))
- grad_w_up: float32 [1024, 2816], P(('batch', 'seq', 'head'))
- grad_w_down: float32 [2816, 1024], P(None, ('batch', 'seq', 'head'))
Inputs may be any that keep to these rules, and one draw needn't show every extreme that they name: `doc_ids`: each stream of 2048 tokens (one index of batch) is packed: its ids start at 0 and never fall, and one of its documents covers tokens on every segment of the stream.
All inputs are finite; a program needn't handle non-finite values.
Results may differ from a plain program's by a relative error of at most 0.015.
Values may be sent and summed in bfloat16 or wider, within the bound.
No kernel may reach another device: no remote copies, remote signals or barrier semaphores. Data moves between devices by JAX's collectives and lax.ppermute only.
A program may use at most 192 MiB of HBM per device.

v0:
```python
import jax
import jax.numpy as jnp
from jax import lax
from jax.sharding import PartitionSpec as P

SCAN_BLOCK_STEPS = 64


eps = 1e-06
precise = lax.Precision.HIGHEST


def shifted(value, axis, steps):
    count = lax.axis_size(axis)
    initial, last = (max(0, -steps), min(count, count - steps))
    return lax.ppermute(value, axis, [(source, source + steps) for source in range(initial, last)])


def entering(value, axis, join, neutral):
    count, mine = (lax.axis_size(axis), lax.axis_index(axis))
    pieces = jax.tree.map(lambda part: lax.all_gather(part, axis), value)
    so_far = jax.tree.map(
        lambda part, zero: jnp.full_like(part, 0) + jnp.asarray(zero, part.dtype), value, neutral
    )

    def lap(position, so_far):
        longer = join(so_far, jax.tree.map(lambda part: part[position], pieces))
        return jax.tree.map(lambda new, old: jnp.where(position < mine, new, old), longer, so_far)

    return lax.fori_loop(0, count - 1, lap, so_far)


def entering_2(array, axis, join, neutral):
    count = lax.axis_size(axis)
    place = lax.axis_index(axis)
    ahead = count - 1 - place
    gathered = jax.tree.map(
        lambda a, kind: lax.all_gather(a.astype(kind), axis),
        array,
        jax.tree.map(lambda a: jnp.bfloat16 if a.dtype == jnp.float32 else a.dtype, array),
    )
    state = jax.tree.map(lambda a, e: jnp.zeros_like(a) + jnp.asarray(e, a.dtype), array, neutral)

    def one(lap, state):
        source = count - 1 - lap
        return join(
            state,
            jax.tree.map(
                lambda a, own: lax.dynamic_index_in_dim(a, source, 0, False).astype(own.dtype),
                gathered,
                array,
            ),
        )

    return lax.fori_loop(0, ahead, one, state)


def inverse_rms(rows):
    return lax.rsqrt(jnp.mean(rows * rows, -1, keepdims=True) + eps)


def norm_back(grad_normed, rows, scale, gain):
    unit = rows * scale
    scaled = grad_normed * gain
    grad_rows = scale * (scaled - unit * jnp.mean(scaled * unit, -1, keepdims=True))
    return (grad_rows, jnp.sum(grad_normed * unit, 0))


def rows_dot(left, right):
    return lax.dot_general(
        left, right, (((0,), (0,)), ((), ())), preferred_element_type=jnp.float32
    )


def dot_trans(left, right):
    return lax.dot_general(
        left, right, (((1,), (1,)), ((), ())), preferred_element_type=jnp.float32
    )


def doc_masks(own_ids, earlier_ids, conv_rows):
    extended = jnp.concatenate([earlier_ids, own_ids])
    length = own_ids.shape[0]
    return jnp.stack(
        [
            (extended[conv_rows - 1 - delay : conv_rows - 1 - delay + length] == own_ids).astype(
                jnp.float32
            )
            for delay in range(conv_rows)
        ]
    )


def short_conv(rows, rim, kernel, same_document):
    conv_rows = kernel.shape[0]
    length = rows.shape[0]
    extended = jnp.concatenate([rim, rows], 0)
    total = jnp.zeros_like(rows)
    for delay in range(conv_rows):
        offset = conv_rows - 1 - delay
        total = (
            total
            + kernel[delay][None, :]
            * extended[offset : offset + length]
            * same_document[delay][:, None]
        )
    return total


def token_input_rows(
    query_before_conv,
    key_before_conv,
    value_before_conv,
    rim_query,
    rim_key,
    rim_value,
    strength_logit,
    forget_logit,
    query_filter_taps,
    key_filter_taps,
    value_filter_taps,
    forget_rates,
    same_document,
    head_count,
):
    length = query_before_conv.shape[0]
    query_rows = jax.nn.silu(
        short_conv(query_before_conv, rim_query, query_filter_taps, same_document)
    ).reshape(length, head_count, -1)
    head_size = query_rows.shape[-1]
    key = jax.nn.silu(short_conv(key_before_conv, rim_key, key_filter_taps, same_document)).reshape(
        length, head_count, -1, head_size
    )
    key = key * lax.rsqrt(jnp.sum(key * key, -1, keepdims=True) + eps)
    value_rows = jax.nn.silu(
        short_conv(value_before_conv, rim_value, value_filter_taps, same_document)
    ).reshape(length, head_count, -1, head_size)
    write_strength = jax.nn.sigmoid(strength_logit).reshape(length, head_count, -1)
    gate_logarithm = -jnp.exp(forget_rates)[None, :] * jax.nn.softplus(forget_logit)
    return (query_rows, key, value_rows, write_strength, gate_logarithm)


def lower_solve(system, right_side):
    return jax.scipy.linalg.solve_triangular(system, right_side, lower=True)


def delta_rule_sweep(
    query_rows, key, value_rows, write_strength, gate_logarithm, document_index, initial_state
):
    length, step_count, head_size = key.shape
    wide = value_rows.shape[-1]
    block_list = length * step_count // SCAN_BLOCK_STEPS
    opening_step = (jnp.arange(step_count) == 0).astype(jnp.float32)
    last_step = (jnp.arange(step_count) == step_count - 1).astype(jnp.float32)
    keys = key.reshape(block_list, SCAN_BLOCK_STEPS, head_size)
    values = value_rows.reshape(block_list, SCAN_BLOCK_STEPS, wide)
    betas = write_strength.reshape(block_list, SCAN_BLOCK_STEPS)
    forget_factors = (gate_logarithm[:, None] * opening_step[None, :]).reshape(
        block_list, SCAN_BLOCK_STEPS
    )
    queries = (query_rows[:, None, :] * last_step[None, :, None]).reshape(
        block_list, SCAN_BLOCK_STEPS, head_size
    )
    doc_of = (document_index[:, None] + jnp.zeros((1, step_count), jnp.int32)).reshape(
        block_list, SCAN_BLOCK_STEPS
    )
    doc_before = jnp.concatenate([doc_of[:1, :1], doc_of[:-1, -1:]], 0)
    cumulative = jnp.cumsum(forget_factors, 1)
    positions = jnp.arange(SCAN_BLOCK_STEPS)
    lower_tri = positions[:, None] >= positions[None, :]
    strict = positions[:, None] > positions[None, :]
    same_document = (doc_of[:, :, None] == doc_of[:, None, :]) & lower_tri[None]
    spread = jnp.where(
        same_document,
        jnp.exp(jnp.where(lower_tri[None], cumulative[:, :, None] - cumulative[:, None, :], 0.0)),
        0.0,
    )
    carried = jnp.exp(cumulative) * (doc_of == doc_before).astype(jnp.float32)
    key_gram = jnp.einsum("cid,cjd->cij", keys, keys, precision=precise)
    system = jnp.eye(SCAN_BLOCK_STEPS, dtype=jnp.float32)[None] + jnp.where(
        strict[None], betas[:, :, None] * key_gram * spread, 0.0
    )
    right_side = jnp.concatenate(
        [(betas * carried)[:, :, None] * keys, betas[:, :, None] * values], -1
    )
    solved = jax.vmap(lower_solve)(system, right_side)
    mix_keys = solved[:, :, :head_size]
    mix_values = solved[:, :, head_size:]
    scores = jnp.einsum("cid,cjd->cij", queries, keys, precision=precise) * spread
    reaching = queries * carried[:, :, None]
    tail_keys = keys * spread[:, -1, :, None]
    survive = carried[:, -1]

    def advance(carry_state, block_data):
        mix_k, mix_v, block_scores, block_reach, block_tail, block_keep = block_data
        fresh_rows = mix_v - jnp.dot(mix_k, carry_state, precision=precise)
        output_rows = jnp.dot(block_reach, carry_state, precision=precise) + jnp.dot(
            block_scores, fresh_rows, precision=precise
        )
        next_state = block_keep * carry_state + jnp.einsum(
            "jd,jw->dw", block_tail, fresh_rows, precision=precise
        )
        return (next_state, output_rows)

    closing_state, output_rows = lax.scan(
        jax.checkpoint(advance),
        initial_state,
        (mix_keys, mix_values, scores, reaching, tail_keys, survive),
    )
    return (output_rows.reshape(length, step_count, wide)[:, -1], closing_state)


def head_digest(query_rows, key, value_rows, write_strength, gate_logarithm, document_index):
    head_size = key.shape[-1]
    value_size = value_rows.shape[-1]
    padded_rows = jnp.concatenate(
        [value_rows, jnp.zeros(value_rows.shape[:-1] + (head_size,), jnp.float32)], -1
    )
    initial_state = jnp.concatenate(
        [jnp.zeros((head_size, value_size), jnp.float32), jnp.eye(head_size, dtype=jnp.float32)], 1
    )
    output_rows, closing_state = delta_rule_sweep(
        query_rows, key, padded_rows, write_strength, gate_logarithm, document_index, initial_state
    )
    return (
        output_rows[:, :value_size],
        output_rows[:, value_size:],
        closing_state[:, :value_size],
        closing_state[:, value_size:],
    )


def gate_norm(core_out, gate_pre, gain_heads):
    length, head_count, head_size = core_out.shape
    unit = core_out * inverse_rms(core_out)
    gate_rows = gate_pre.reshape(length, head_count, head_size)
    return (unit * gain_heads.reshape(head_count, head_size) * jax.nn.silu(gate_rows)).reshape(
        length, head_count * head_size
    )


def compose(earlier, later):
    return (
        jnp.matmul(later[0], earlier[0], precision=precise),
        jnp.matmul(later[0], earlier[1], precision=precise) + later[1],
    )


def on_device(
    tokens,
    doc_ids,
    norm_gain,
    w_query,
    w_key,
    w_value,
    w_beta,
    w_decay,
    w_outgate,
    conv_query,
    conv_key,
    conv_value,
    decay_log,
    out_gain,
    w_out,
    mlp_gain,
    w_gate,
    w_up,
    w_down,
    cotangent,
):
    head_count = w_decay.shape[1]
    step_count = w_beta.shape[1] // head_count
    head_size = w_query.shape[1] // head_count
    conv_rows = conv_query.shape[0]
    rim_rows = conv_rows - 1
    residual = tokens.astype(jnp.float32)
    scale_in = inverse_rms(residual)
    normed = (residual * scale_in * norm_gain).astype(jnp.bfloat16)
    gathered = lax.all_gather(normed, "head", axis=0, tiled=True)
    weights = jnp.concatenate([w_query, w_key, w_value, w_outgate, w_beta, w_decay], 1)
    projected = jnp.dot(gathered, weights, preferred_element_type=jnp.float32)
    query_cols = head_count * head_size
    pair_cols = head_count * step_count * head_size
    offsets = [
        0,
        query_cols,
        query_cols + pair_cols,
        query_cols + 2 * pair_cols,
        2 * query_cols + 2 * pair_cols,
        2 * query_cols + 2 * pair_cols + head_count * step_count,
        weights.shape[1],
    ]
    query_before_conv = projected[:, offsets[0] : offsets[1]].astype(jnp.bfloat16)
    key_before_conv = projected[:, offsets[1] : offsets[2]].astype(jnp.bfloat16)
    value_before_conv = projected[:, offsets[2] : offsets[3]].astype(jnp.bfloat16)
    gate_pre = projected[:, offsets[3] : offsets[4]]
    strength_logit = projected[:, offsets[4] : offsets[5]]
    forget_logit = projected[:, offsets[5] : offsets[6]]
    rim_query, rim_key, rim_value, rim_ids = shifted(
        (
            query_before_conv[-rim_rows:],
            key_before_conv[-rim_rows:],
            value_before_conv[-rim_rows:],
            doc_ids[-rim_rows:].astype(jnp.bfloat16),
        ),
        "seq",
        1,
    )
    own_ids = doc_ids.astype(jnp.float32)
    same_document = doc_masks(own_ids, rim_ids.astype(jnp.float32), conv_rows)
    joined = same_document[1, 0]

    def local_fn(
        query_in,
        key_in,
        value_in,
        rim_q,
        rim_k,
        rim_v,
        beta_in,
        decay_in,
        taps_query,
        taps_key,
        taps_value,
        forget_rates,
    ):
        return token_input_rows(
            query_in,
            key_in,
            value_in,
            rim_q,
            rim_k,
            rim_v,
            beta_in,
            decay_in,
            taps_query,
            taps_key,
            taps_value,
            forget_rates,
            same_document,
            head_count,
        )

    local_args = (
        query_before_conv.astype(jnp.float32),
        key_before_conv.astype(jnp.float32),
        value_before_conv.astype(jnp.float32),
        rim_query.astype(jnp.float32),
        rim_key.astype(jnp.float32),
        rim_value.astype(jnp.float32),
        strength_logit,
        forget_logit,
        conv_query.astype(jnp.float32),
        conv_key.astype(jnp.float32),
        conv_value.astype(jnp.float32),
        decay_log,
    )
    mixer_inputs, local_back = jax.vjp(local_fn, *local_args)

    def build_digest(query_rows, key, value_rows, write_strength, gate_logarithm):

        def single_head(q_head, k_head, v_head, b_head, g_head):
            return head_digest(q_head, k_head, v_head, b_head, g_head, doc_ids)

        return jax.vmap(single_head, in_axes=1, out_axes=(1, 1, 0, 0))(
            query_rows, key, value_rows, write_strength, gate_logarithm
        )

    summary, core_back = jax.vjp(build_digest, *mixer_inputs)
    base_out, query_reach, end_base, end_map = summary
    identity = jnp.broadcast_to(jnp.eye(head_size, dtype=jnp.float32), end_map.shape)
    zero_state = jnp.zeros_like(end_base)
    before = entering((joined * end_map, end_base), "seq", compose, (identity, zero_state))
    state_in = joined * before[1]
    core_out = base_out + jnp.einsum("lhd,hdv->lhv", query_reach, state_in, precision=precise)
    gated, gate_back = jax.vjp(gate_norm, core_out, gate_pre, out_gain)
    mixed_in = gated.astype(jnp.bfloat16)
    branch = lax.psum_scatter(
        jnp.dot(mixed_in, w_out, preferred_element_type=jnp.float32),
        "head",
        scatter_dimension=0,
        tiled=True,
    )
    middle = residual + branch
    scale_mid = inverse_rms(middle)
    normed_mid = (middle * scale_mid * mlp_gain).astype(jnp.bfloat16)
    gate = jnp.dot(normed_mid, w_gate, preferred_element_type=jnp.float32)
    up = jnp.dot(normed_mid, w_up, preferred_element_type=jnp.float32)
    sigma = jax.nn.sigmoid(gate)
    silu_gate = gate * sigma
    act = (silu_gate * up).astype(jnp.bfloat16)
    block_out = (middle + jnp.dot(act, w_down, preferred_element_type=jnp.float32)).astype(
        jnp.bfloat16
    )
    grad_w_down = rows_dot(act, cotangent)
    grad_act = dot_trans(cotangent, w_down)
    grad_gate = (grad_act * up * sigma * (1.0 + gate * (1.0 - sigma))).astype(jnp.bfloat16)
    grad_up = (grad_act * silu_gate).astype(jnp.bfloat16)
    grad_w_gate = rows_dot(normed_mid, grad_gate)
    grad_w_up = rows_dot(normed_mid, grad_up)
    grad_normed_mid = dot_trans(grad_gate, w_gate) + dot_trans(grad_up, w_up)
    grad_mid_norm, grad_mlp_gain = norm_back(grad_normed_mid, middle, scale_mid, mlp_gain)
    grad_middle = cotangent.astype(jnp.float32) + grad_mid_norm
    grad_branch = grad_middle.astype(jnp.bfloat16)
    piece = lax.all_gather(grad_branch, "head", axis=0, tiled=True)
    grad_rows_all = dot_trans(piece, w_out)
    grad_weight = rows_dot(mixed_in, piece)
    grad_core, grad_gate_pre, grad_out_gain = gate_back(grad_rows_all)
    local_grad = jnp.einsum("lhd,lhv->hdv", query_reach, grad_core, precision=precise)
    grad_reach = jnp.einsum("lhv,hdv->lhd", grad_core, state_in, precision=precise)
    behind = entering_2(
        (joined * jnp.swapaxes(end_map, 1, 2), joined * local_grad),
        "seq",
        compose,
        (identity, zero_state),
    )
    grad_end = behind[1]
    grad_end_map = jnp.einsum("hdv,hev->hde", grad_end, state_in, precision=precise)
    summary_grads = (grad_core, grad_reach, grad_end, grad_end_map)
    grads_core = core_back(summary_grads)
    (
        grad_query_in,
        grad_key_in,
        grad_value_in,
        grad_rim_q,
        grad_rim_k,
        grad_rim_v,
        grad_beta_in,
        grad_decay_in,
        grad_taps_query,
        grad_taps_key,
        grad_taps_value,
        grad_decay_rates,
    ) = local_back(grads_core)
    late_query, late_key, late_value = shifted((grad_rim_q, grad_rim_k, grad_rim_v), "seq", -1)
    grad_query_in = jnp.concatenate(
        [grad_query_in[:-rim_rows], grad_query_in[-rim_rows:] + late_query], 0
    )
    grad_key_in = jnp.concatenate([grad_key_in[:-rim_rows], grad_key_in[-rim_rows:] + late_key], 0)
    grad_value_in = jnp.concatenate(
        [grad_value_in[:-rim_rows], grad_value_in[-rim_rows:] + late_value], 0
    )
    grad_proj = jnp.concatenate(
        [grad_query_in, grad_key_in, grad_value_in, grad_gate_pre, grad_beta_in, grad_decay_in], 1
    ).astype(jnp.bfloat16)
    grad_normed = lax.psum_scatter(
        dot_trans(grad_proj, weights).astype(jnp.bfloat16), "head", scatter_dimension=0, tiled=True
    ).astype(jnp.float32)
    grad_weights = rows_dot(gathered, grad_proj)
    grad_in_norm, grad_norm_gain = norm_back(grad_normed, residual, scale_in, norm_gain)
    grad_tokens = grad_middle + grad_in_norm
    mixer_sums = (
        lax.psum_scatter(
            grad_weights[:, offsets[0] : offsets[1]].astype(jnp.bfloat16),
            ("batch", "seq"),
            scatter_dimension=0,
            tiled=True,
        ).astype(jnp.float32),
        lax.psum_scatter(
            grad_weights[:, offsets[1] : offsets[2]].astype(jnp.bfloat16),
            ("batch", "seq"),
            scatter_dimension=0,
            tiled=True,
        ).astype(jnp.float32),
        lax.psum_scatter(
            grad_weights[:, offsets[2] : offsets[3]].astype(jnp.bfloat16),
            ("batch", "seq"),
            scatter_dimension=0,
            tiled=True,
        ).astype(jnp.float32),
        lax.psum_scatter(
            grad_weights[:, offsets[4] : offsets[5]].astype(jnp.bfloat16),
            ("batch", "seq"),
            scatter_dimension=0,
            tiled=True,
        ).astype(jnp.float32),
        lax.psum_scatter(
            grad_weights[:, offsets[5] : offsets[6]].astype(jnp.bfloat16),
            ("batch", "seq"),
            scatter_dimension=0,
            tiled=True,
        ).astype(jnp.float32),
        lax.psum_scatter(
            grad_weights[:, offsets[3] : offsets[4]].astype(jnp.bfloat16),
            ("batch", "seq"),
            scatter_dimension=0,
            tiled=True,
        ).astype(jnp.float32),
        lax.psum_scatter(
            grad_weight.astype(jnp.bfloat16), ("batch", "seq"), scatter_dimension=1, tiled=True
        ).astype(jnp.float32),
    )
    small_sums = lax.psum(
        (grad_taps_query, grad_taps_key, grad_taps_value, grad_decay_rates, grad_out_gain),
        ("batch", "seq"),
    )
    block_sums = (
        lax.psum_scatter(grad_w_gate, ("batch", "seq", "head"), scatter_dimension=0, tiled=True),
        lax.psum_scatter(grad_w_up, ("batch", "seq", "head"), scatter_dimension=0, tiled=True),
        lax.psum_scatter(grad_w_down, ("batch", "seq", "head"), scatter_dimension=1, tiled=True),
        lax.psum_scatter(grad_norm_gain, ("batch", "seq", "head"), scatter_dimension=0, tiled=True),
        lax.psum_scatter(grad_mlp_gain, ("batch", "seq", "head"), scatter_dimension=0, tiled=True),
    )
    return (
        block_out,
        grad_tokens,
        block_sums[3],
        mixer_sums[0],
        mixer_sums[1],
        mixer_sums[2],
        mixer_sums[3],
        mixer_sums[4],
        mixer_sums[5],
        small_sums[0],
        small_sums[1],
        small_sums[2],
        small_sums[3],
        small_sums[4],
        mixer_sums[6],
        block_sums[4],
        block_sums[0],
        block_sums[1],
        block_sums[2],
    )


def solution(mesh):
    return jax.shard_map(
        on_device,
        mesh=mesh,
        in_specs=(
            P(("batch", "seq", "head"), None),
            P(("batch", "seq")),
            P(),
            P(None, "head"),
            P(None, "head"),
            P(None, "head"),
            P(None, "head"),
            P(None, "head"),
            P(None, "head"),
            P(None, "head"),
            P(None, "head"),
            P(None, "head"),
            P("head"),
            P("head"),
            P("head", None),
            P(),
            P(),
            P(),
            P(),
            P(("batch", "seq", "head"), None),
        ),
        out_specs=(
            P(("batch", "seq", "head"), None),
            P(("batch", "seq", "head"), None),
            P(("batch", "seq", "head")),
            P(("batch", "seq"), "head"),
            P(("batch", "seq"), "head"),
            P(("batch", "seq"), "head"),
            P(("batch", "seq"), "head"),
            P(("batch", "seq"), "head"),
            P(("batch", "seq"), "head"),
            P(None, "head"),
            P(None, "head"),
            P(None, "head"),
            P("head"),
            P("head"),
            P("head", ("batch", "seq")),
            P(("batch", "seq", "head")),
            P(("batch", "seq", "head"), None),
            P(("batch", "seq", "head"), None),
            P(None, ("batch", "seq", "head")),
        ),
        check_vma=False,
    )
```

profile of v0, /device:TPU:0, one launch (start us, length us, event | category | flops | bytes accessed | tf_op | source)
XLA Modules:
  0.0 1970.8 jit_solution(10464062582660077093)
XLA Ops:
  8.2 4.8 collective-permute-start.1
  22.7 6.1 concatenate.47
  32.9 11.5 all-gather.7.cloned.1.call-done
  82.8 158.7 %custom-call.10 = f32[2,16,1,64,64]{3,4,2,1,0:T(8,128)} custom-call(f32[2,16,1,64,64]{4,3,2,1,0:T(8,128)} %get-tuple-element.997), custom_call_target="InvertDiagBlocksLowerTriangular" | custom-call | tf_op jit(solution)/shard_map/jvp(vmap(vmap(jit(_solve_triangular))))/triangular_solve | solution.py:144
  243.2 4.7 fusion.68
  275.6 108.8 %while.68 = (s32[]{:T(128)}, f32[2,128,256]{2,1,0:T(8,128)S(1)}, f32[16,2,64,256]{3,2,1,0:T(8,128)}, f32[16,2,128,256]{3,2,1,0:T(8,128)}, f32[16,2]{1,0:T(8,128)...) while((s32[]{:T(128)}, f32[2,128,256]{2,1,0:T(8,128)S(1)}, ...), condition=%wide.region_4.5_spmd, body=%wide.region_3.4_spmd.sunk | while | flops 176357376 | bytes 2756233 | solution.py:205
  385.7 9.8 all-gather
  395.5 10.7 all-gather.1
  419.6 42.5 %reduce-scatter.27.cloned.1.call-done = f32[128,1024]{1,0:T(8,128)} async-done(((f32[512,1024]{1,0:T(8,128)}), f32[128,1024]{1,0:T(8,128)}) %reduce-scatter.27.cloned.1.call-update) | async-done | bytes 524304 | tf_op jit(solution)/shard_map/reduce_scatter | solution.py:378
  483.4 9.6 all-gather.2
  493.0 13.6 all-gather.9.cloned.1.call-done
  519.5 8.9 all-gather.3
  542.7 269.2 %while.70 = (s32[]{:T(128)}, f32[2,128,256]{2,1,0:T(8,128)S(1)}, f32[16,2,64,128]{3,2,1,0:T(8,128)}, f32[16,2,64,256]{3,2,1,0:T(8,128)}, f32[16,2,64,64]{3,2,0,1...) while((s32[]{:T(128)}, f32[2,128,256]{2,1,0:T(8,128)S(1)}, ...), condition=%wide.region_16.17_spmd, body=%wide.region_14.16_spmd.sunk | while | flops 403111936 | bytes 7143709 | solution.py:205
  812.0 6.7 fusion.38
  832.0 4.2 fusion.63
  903.6 5.1 concatenate.58
  926.3 5.7 convolution_convert_fusion.1
  932.1 5.9 fusion.166
  939.1 5.8 fusion.167
  946.1 5.9 fusion.168
  952.2 4.3 fusion.47
  956.8 29.1 %all-reduce.38 = (f32[4,256]{1,0:T(4,128)}, f32[4,512]{1,0:T(4,128)}, f32[4,512]{1,0:T(4,128)}, f32[2]{0:T(128)}, f32[256]{0:T(256)}) all-reduce(f32[4,256]{1,0:T(4,128)S(1)} %pad_add_fusion.10, f32[4,512]{1,0:T(4,128)S(1)} %pad_add_fusion.9, ...), channel_id=1, replica_groups=mesh['batch'=2,'seq'=4,'head'=4] {'batch','seq'}, use_global_device_ids=true, to_apply=%region_42.43 | all-reduce | flops 5378 | bytes 43024 | tf_op jit(solution)/shard_map/psum | solution.py:493
  988.7 35.9 %reduce-scatter.49.cloned.1.call-done = bf16[128,256]{1,0:T(8,128)(2,1)} async-done(((bf16[1024,256]{1,0:T(8,128)(2,1)}), bf16[128,256]{1,0:T(8,128)(2,1)}) %reduce-scatter.49.cloned.1.call-update) | async-done | bytes 65552
  1026.2 36.1 %reduce-scatter.37.cloned.1.call-done = bf16[128,256]{1,0:T(8,128)(2,1)} async-done(((bf16[1024,256]{1,0:T(8,128)(2,1)}), bf16[128,256]{1,0:T(8,128)(2,1)}) %reduce-scatter.37.cloned.1.call-update) | async-done | bytes 65552
  1064.1 35.8 %reduce-scatter.47.cloned.1.call-done = bf16[128,256]{1,0:T(8,128)(2,1)} async-done(((bf16[1024,256]{1,0:T(8,128)(2,1)}), bf16[128,256]{1,0:T(8,128)(2,1)}) %reduce-scatter.47.cloned.1.call-update) | async-done | bytes 65552
  1101.7 37.5 %reduce-scatter.39.cloned.1.call-done = bf16[128,512]{1,0:T(8,128)(2,1)} async-done(((bf16[1024,512]{1,0:T(8,128)(2,1)}), bf16[128,512]{1,0:T(8,128)(2,1)}) %reduce-scatter.39.cloned.1.call-update) | async-done | bytes 131088
  1141.1 37.2 %reduce-scatter.41.cloned.1.call-done = bf16[128,512]{1,0:T(8,128)(2,1)} async-done(((bf16[1024,512]{1,0:T(8,128)(2,1)}), bf16[128,512]{1,0:T(8,128)(2,1)}) %reduce-scatter.41.cloned.1.call-update) | async-done | bytes 131088
  1180.1 27.6 %reduce-scatter.29.cloned.1.call-done = bf16[128,1024]{1,0:T(8,128)(2,1)} async-done(((bf16[512,1024]{1,0:T(8,128)(2,1)}), bf16[128,1024]{1,0:T(8,128)(2,1)}) %reduce-scatter.29.cloned.1.call-update) | async-done | bytes 262160 | tf_op jit(solution)/shard_map/reduce_scatter | solution.py:446
  1209.0 42.7 %all-reduce.37 = (f32[1024]{0:T(1024)S(1)}, f32[1024]{0:T(1024)S(1)}) all-reduce(f32[1024]{0:T(1024)S(1)} %get-tuple-element.863, f32[1024]{0:T(1024)S(1)} %copy-done.141), channel_id=8, replica_groups=mesh['batch'=2,'seq'=4,'head'=4] {'batch','seq','head'}, use_global_device_ids=true, to_apply=%region_31.32.clone | all-reduce | flops 2048 | bytes 16384
  1254.9 206.4 %reduce-scatter.31.cloned.1.call-done = f32[32,2816]{1,0:T(8,128)} async-done(((f32[1024,2816]{1,0:T(8,128)}), f32[32,2816]{1,0:T(8,128)}) %reduce-scatter.31.cloned.1.call-update) | async-done | bytes 360464 | tf_op jit(solution)/shard_map/reduce_scatter | solution.py:498
  1461.3 251.5 %reduce-scatter.33.cloned.1.call-done = f32[32,2816]{1,0:T(8,128)} async-done(((f32[1024,2816]{1,0:T(8,128)}), f32[32,2816]{1,0:T(8,128)}) %reduce-scatter.33.cloned.1.call-update) | async-done | bytes 360464 | tf_op jit(solution)/shard_map/reduce_scatter | solution.py:499
  1712.7 251.3 %reduce-scatter.35.cloned.1.call-done = f32[2816,32]{0,1:T(8,128)} async-done(((f32[2816,1024]{0,1:T(8,128)}), f32[2816,32]{0,1:T(8,128)}) %reduce-scatter.35.cloned.1.call-update) | async-done | bytes 360464 | tf_op jit(solution)/shard_map/reduce_scatter | solution.py:500
  (1049 shorter events, 643.7 us)
Async XLA Ops:
  7.2 410.1 %copy-start = (bf16[256,1024]{1,0:T(8,128)(2,1)S(1)}, bf16[256,1024]{1,0:T(8,128)(2,1)}, u32[]{:S(2)}) copy-start(bf16[256,1024]{1,0:T(8,128)(2,1)} %param.42) | copy-start | bytes 1572868
  7.2 37.1 %all-gather.7.cloned.1.call-start = ((), (), s32[]{:S(2)}) async-start(), calls=%async_computation.12 | async-start | bytes 1310720 | tf_op jit(solution)/shard_map/all_gather | solution.py:279
  8.2 23.4 %collective-permute-start.1 = (bf16[3]{0:T(256)(128)(2,1)S(1)}, bf16[3]{0:T(256)(128)(2,1)S(1)}, u32[]{:S(2)}, u32[]{:S(2)}) collective-permute-start(bf16[3]{0:T(256)(128)(2,1)S(1)} %slice.223), channel_id=1, source_target_pairs={{0,4},{4,8},{8,12},{1,5},{5,9},{9,13},{2,6},{6,10},{10,14},{3,7},{... | collective-permute-start | bytes 26 | tf_op jit(solution)/shard_map/ppermute | solution.py:16
  15.9 446.1 %reduce-scatter.27.cloned.1.call-start = ((), (), s32[]{:S(2)}) async-start(), calls=%async_computation.13 | async-start | bytes 2621440 | tf_op jit(solution)/shard_map/reduce_scatter | solution.py:378
  52.4 19.3 collective-permute-start
  58.1 9.4 collective-permute-start.3
  61.4 180.1 %collective-permute-start.2 = (bf16[3,512]{0,1:T(8,128)(2,1)}, bf16[3,512]{0,1:T(8,128)(2,1)}, u32[]{:S(2)}, u32[]{:S(2)}) collective-permute-start(bf16[3,512]{0,1:T(8,128)(2,1)} %get-tuple-element.977), channel_id=1, source_target_pairs={{0,4},{4,8},{8,12},{1,5},{5,9},{9,13},{2,6},{6,10},{10,14},{3,7},{... | collective-permute-start | bytes 9224 | tf_op jit(solution)/shard_map/ppermute | solution.py:16
  67.5 349.2 %copy-start.37 = (f32[512,2,128]{2,0,1:T(8,128)}, f32[512,2,128]{2,0,1:T(8,128)S(1)}, u32[]{:S(2)}) copy-start(f32[512,2,128]{2,0,1:T(8,128)S(1)} %copy.289) | copy-start | bytes 1572868
  419.2 87.5 %all-gather.9.cloned.1.call-start = ((), (), s32[]{:S(2)}) async-start(), calls=%async_computation.14 | async-start | bytes 1310720 | tf_op jit(solution)/shard_map/all_gather | solution.py:405
  479.2 506.6 %reduce-scatter.45.cloned.1.call-start = ((), (), s32[]{:S(2)}) async-start(), calls=%async_computation.23 | async-start | bytes 294912
  881.5 18.5 collective-permute-start.6
  882.8 18.8 collective-permute-start.5
  887.6 10.4 collective-permute-start.4
  915.0 72.3 %reduce-scatter.43.cloned.1.call-start = ((), (), s32[]{:S(2)}) async-start(), calls=%async_computation.22 | async-start | bytes 294912
  916.7 107.9 %reduce-scatter.49.cloned.1.call-start = ((), (), s32[]{:S(2)}) async-start(), calls=%async_computation.25 | async-start | bytes 589824
  918.2 144.2 %reduce-scatter.37.cloned.1.call-start = ((), (), s32[]{:S(2)}) async-start(), calls=%async_computation.19 | async-start | bytes 589824
  920.6 179.4 %reduce-scatter.47.cloned.1.call-start = ((), (), s32[]{:S(2)}) async-start(), calls=%async_computation.24 | async-start | bytes 589824
  921.6 217.6 %reduce-scatter.39.cloned.1.call-start = ((), (), s32[]{:S(2)}) async-start(), calls=%async_computation.20 | async-start | bytes 1179648
  924.8 253.5 %reduce-scatter.41.cloned.1.call-start = ((), (), s32[]{:S(2)}) async-start(), calls=%async_computation.21 | async-start | bytes 1179648
  926.2 281.5 %reduce-scatter.29.cloned.1.call-start = ((), (), s32[]{:S(2)}) async-start(), calls=%async_computation.15 | async-start | bytes 1310720 | tf_op jit(solution)/shard_map/reduce_scatter | solution.py:446
  932.0 529.3 %reduce-scatter.31.cloned.1.call-start = ((), (), s32[]{:S(2)}) async-start(), calls=%async_computation.16 | async-start | bytes 11894784 | tf_op jit(solution)/shard_map/reduce_scatter | solution.py:498
  938.0 774.7 %reduce-scatter.33.cloned.1.call-start = ((), (), s32[]{:S(2)}) async-start(), calls=%async_computation.17 | async-start | bytes 11894784 | tf_op jit(solution)/shard_map/reduce_scatter | solution.py:499
  945.0 1019.0 %reduce-scatter.35.cloned.1.call-start = ((), (), s32[]{:S(2)}) async-start(), calls=%async_computation.18 | async-start | bytes 11894784 | tf_op jit(solution)/shard_map/reduce_scatter | solution.py:500
  956.5 251.2 %copy-start.44 = (bf16[128,1024]{1,0:T(8,128)(2,1)S(1)}, bf16[128,1024]{1,0:T(8,128)(2,1)}, u32[]{:S(2)}) copy-start(bf16[128,1024]{1,0:T(8,128)(2,1)} %param.28) | copy-start | bytes 786436
  956.5 251.2 %copy-start.124 = (f32[1024]{0:T(1024)S(1)}, f32[1024]{0:T(1024)}, u32[]{:S(2)}) copy-start(f32[1024]{0:T(1024)} %param.30) | copy-start | bytes 12292
  956.5 251.2 %copy-start.165 = (f32[128]{0:T(128)S(1)}, f32[128]{0:T(128)}, u32[]{:S(2)}) copy-start(f32[128]{0:T(128)} %copy-done.164) | copy-start | bytes 1540
  956.5 252.5 %copy-start.141 = (f32[1024]{0:T(1024)S(1)}, f32[1024]{0:T(1024)}, u32[]{:S(2)}) copy-start(f32[1024]{0:T(1024)} %get-tuple-element.854) | copy-start | bytes 12292
  956.5 296.3 %copy-start.50 = (f32[128,1024]{1,0:T(8,128)S(1)}, f32[128,1024]{1,0:T(8,128)}, u32[]{:S(2)}) copy-start(f32[128,1024]{1,0:T(8,128)} %copy-done.49) | copy-start | bytes 1572868
  956.5 296.3 %copy-start.120 = (f32[1024]{0:T(1024)S(1)}, f32[1024]{0:T(1024)}, u32[]{:S(2)}) copy-start(f32[1024]{0:T(1024)} %param.43) | copy-start | bytes 12292
  956.5 296.3 %copy-start.163 = (f32[128]{0:T(128)S(1)}, f32[128]{0:T(128)}, u32[]{:S(2)}) copy-start(f32[128]{0:T(128)} %copy-done.162) | copy-start | bytes 1540
  956.5 296.3 %copy-start.178 = (f32[128]{0:T(128)S(1)}, f32[128]{0:T(128)}, u32[]{:S(2)}) copy-start(f32[128]{0:T(128)} %copy-done.177) | copy-start | bytes 1540
  1100.9 863.1 %copy-start.1 = (bf16[256,1024]{1,0:T(8,128)(2,1)S(1)}, bf16[256,1024]{1,0:T(8,128)(2,1)}, u32[]{:S(2)}) copy-start(bf16[256,1024]{1,0:T(8,128)(2,1)} %param.42) | copy-start | bytes 1572868
  (176 other events, 2598.8 us)
Sparse Core Ops, SparseCore 0:
  16.1 28.2 all-gather.6
  419.3 42.7 reduce-scatter.26
  479.4 27.2 all-gather.8
  915.1 34.9 reduce-scatter.44
  953.5 33.6 reduce-scatter.42
  990.4 34.1 reduce-scatter.48
  1028.3 34.0 reduce-scatter.36
  1065.8 34.1 reduce-scatter.46
  1103.1 36.0 reduce-scatter.38
  1142.2 35.9 reduce-scatter.40
  1180.6 27.1 reduce-scatter.28
  1210.6 250.6 reduce-scatter.30
  1464.3 248.4 reduce-scatter.32
  1715.6 248.4 reduce-scatter.34
where the time goes:
time: 1990 us; the launch traced here: 1970 us
  waiting for transfers between devices  990 us (50%)
  matrix products  310 us (16%)
  local copies, waits for them, and re-layouts  280 us (14%)
  other arithmetic  240 us (12%)
  blocking collectives  111 us (6%)
  starting transfers between devices  21.3 us (1%)
    reduce_scatter x1, waiting for transfers between devices, on_device(): lax.psum_scatter(grad_w_up, ('batch', 'seq', 'head'), scatter_dimension=0...  251 us
    reduce_scatter x1, waiting for transfers between devices, on_device(): lax.psum_scatter(grad_w_down, ('batch', 'seq', 'head'), scatter_dimension...  251 us
    reduce_scatter x1, waiting for transfers between devices, on_device(): lax.psum_scatter(grad_w_gate, ('batch', 'seq', 'head'), scatter_dimension...  206 us
    unnamed x21, waiting for transfers between devices  183 us
    another operation x3, other arithmetic, lower_solve(): return jax.scipy.linalg.solve_triangular(system, right_side, lower=True)  160 us
    squeeze x80, local copies, waits for them, and re-layouts, delta_rule_sweep(): lax.scan(jax.checkpoint(advance), initial_state, (mix_keys, mix_values, s...  79.2 us
    dot_general x48, matrix products, advance(): jnp.dot(block_scores, fresh_rows, precision=precise)  70.4 us
    dot_general x48, matrix products, advance(): jnp.dot(block_reach, carry_state, precision=precise)  54.3 us
  transfers between devices with their start and end apart: 21, of which 13 were waited for; matrix products, arithmetic and copies ran while one was open for 14% of the time, Pallas kernels for 0%

commit v1 on v0

v1 whole, which is shorter than its diff:
```python
import functools

import jax
import jax.numpy as jnp
from jax import lax
from jax.experimental import pallas as pl
from jax.experimental.pallas import tpu as pltpu
from jax.sharding import PartitionSpec as P

bf16, f32, i32 = jnp.bfloat16, jnp.float32, jnp.int32
EPS = 1e-06
CT = 64
RIM = 16
NN = ((1,), (0,))
NT = ((1,), (1,))
MIB = 1 << 20


def mm(a, b, dims=NN):
    return lax.dot_general(a, b, (dims, ((), ())), preferred_element_type=f32)


def split(x):
    high = x.astype(bf16)
    return high, (x - high.astype(f32)).astype(bf16)


def mm3(a, b, dims=NN):
    return mm(a[0], b[0], dims) + (mm(a[0], b[1], dims) + mm(a[1], b[0], dims))


def exact(a, b):
    return lax.dot_general(
        a, b, (NN, ((), ())), precision=lax.Precision.HIGHEST, preferred_element_type=f32
    )


def iota2(shape, dim):
    return lax.broadcasted_iota(i32, shape, dim)


def rows_of(c, size=CT, start=0):
    return pl.ds(pl.multiple_of(c * size + start, 16), size)


def near(c, start):
    return pl.ds(pl.multiple_of(c * CT + start, 8), CT + 8)


def step_order():
    size = 2 * CT
    row, col = iota2((size, size), 0), iota2((size, size), 1)
    row_tok, col_tok = row & (CT - 1), col & (CT - 1)
    later = jnp.where(row_tok > col_tok, row_tok ^ col_tok, 0)
    same_token = (row_tok == col_tok) & (row >= CT) & (col < CT)
    return row, col, later, same_token


def twice(x):
    return jnp.concatenate([x, x], 0)


def head_steps(ref, rows, h):
    return jnp.concatenate(
        [ref[rows, (2 * h + j) * 128 : (2 * h + j + 1) * 128] for j in range(2)], 0
    )


def decays(gam_ref, info, rows, h, nh):
    gcol = gam_ref[rows, 2 * nh + h : 2 * nh + h + 1]
    glast = gcol[CT - 1 : CT, :]
    carried = jnp.exp(gcol) * info[:, 4:5]
    tail = jnp.exp(jnp.minimum(glast - gcol, 0.0)) * info[:, 5:6]
    keep = carried[CT - 1 : CT, :]
    return gcol, carried, tail, keep


def forward_kernel(
    nh, count, me_ref, *refs
):
    tok_refs, refs = refs[:count], refs[count:]
    forward_body(nh, me_ref, tok_refs, *refs)


def forward_body(
    nh, me_ref, tok_refs, rim_ref, ng_ref, wq_ref, wk_ref, wv_ref, wg_ref, ws_ref, tq_ref, tk_ref, tv_ref,
    info_ref, drow_ref, rate_ref,
    normed_ref, pre_ref, conv_ref, gate_ref, q_ref, k_ref, v_ref, beta_ref, glog_ref, gam_ref, dec_ref,
    t_ref, w_ref, u_ref, reach_ref, score_ref, at_ref, bt_ref, st_ref,
):
    length = pre_ref.shape[0] - RIM
    nc = length // CT
    gain = ng_ref[...]
    count = len(tok_refs)
    each = tok_refs[0].shape[0]

    def normal(x):
        x = x.astype(f32)
        scale = lax.rsqrt(jnp.mean(x * x, -1, keepdims=True) + EPS)
        return (x * scale * gain).astype(bf16)

    normed_ref[0:RIM, :] = normal(rim_ref[...])

    for shift, tok_ref in enumerate(tok_refs):
        place = lax.rem(me_ref[0] + (count - shift), count) * each

        def norm_rows(c, carry):
            target = pl.ds(pl.multiple_of(place + c * CT + RIM, 16), CT)
            normed_ref[target, :] = normal(tok_ref[rows_of(c), :])
            return carry

        lax.fori_loop(0, each // CT, norm_rows, 0)
    nq = nh * 128
    groups = ((wq_ref, 0, nq), (wk_ref, nq, 2 * nq), (wv_ref, 3 * nq, 2 * nq))

    for weight, first, width in groups:
        pre_ref[0:RIM, first : first + width] = (
            mm(normed_ref[0:RIM, :], weight[...]).astype(bf16).astype(f32)
        )

    def project(i, carry):
        rows = rows_of(i, 256, RIM)
        block = normed_ref[rows, :]
        for weight, first, width in groups:
            pre_ref[rows, first : first + width] = mm(block, weight[...]).astype(bf16).astype(f32)
        plain = rows_of(i, 256)
        gate_ref[plain, :] = mm(block, wg_ref[...])
        glog_ref[plain, :] = mm(block, ws_ref[...])
        return carry

    lax.fori_loop(0, length // 256, project, 0)
    logits = glog_ref[...]
    beta_ref[...] = jax.nn.sigmoid(logits)
    soft = jnp.maximum(logits, 0.0) + jnp.log1p(jnp.exp(-jnp.abs(logits)))
    glog = rate_ref[...] * soft
    glog_ref[...] = glog
    tri = (iota2((CT, CT), 0) >= iota2((CT, CT), 1)).astype(f32)
    for c in range(nc):
        gam_ref[c * CT : (c + 1) * CT, :] = exact(tri, glog[c * CT : (c + 1) * CT, :])

    def conv_rows(c, carry):
        rows = rows_of(c)
        info = info_ref[rows_of(c, CT, RIM), :]
        mask = [info[:, m : m + 1] for m in range(4)]
        for tap_ref, first, count, kind in (
            (tq_ref, 0, nh, "q"), (tk_ref, nq, 2 * nh, "k"), (tv_ref, 3 * nq, 2 * nh, "v")
        ):
            for j in range(count):
                cols = slice(first + j * 128, first + (j + 1) * 128)
                mine = slice(j * 128, (j + 1) * 128)
                taps = tap_ref[:, mine].astype(f32)
                block = pre_ref[near(c, RIM - 8), cols]
                total = block[8:] * taps[0:1]
                for m in range(1, 4):
                    total = total + pltpu.roll(block, m, 0)[8:] * mask[m] * taps[m : m + 1]
                conv_ref[rows, cols] = total
                out = total * jax.nn.sigmoid(total)
                if kind == "k":
                    out = out * lax.rsqrt(jnp.sum(out * out, -1, keepdims=True) + EPS)
                {"q": q_ref, "k": k_ref, "v": v_ref}[kind][rows, mine] = out
        return carry

    lax.fori_loop(0, nc, conv_rows, 0)

    row, col, later, same_token = step_order()
    eye = (row == col).astype(f32)
    small_row, small_col = iota2((CT, CT), 0), iota2((CT, CT), 1)

    def prepare(c, carry):
        rows = rows_of(c)
        heads = range(nh)
        info = info_ref[rows_of(c, CT, RIM), :]
        doc_col = info[:, 6:7]
        doc_row = drow_ref[c]
        same = (doc_col == doc_row) & (small_row >= small_col)
        keys, keys2, systems, rhs, tails, keeps = [], [], [], [], [], []
        for h in heads:
            gcol, carried, tail, keep = decays(gam_ref, info, rows, h, nh)
            grow = jnp.sum(jnp.where(small_row == small_col, gcol, 0.0), 0, keepdims=True)
            decay = jnp.where(same, jnp.exp(jnp.minimum(gcol - grow, 0.0)), 0.0)
            wide = jnp.concatenate([decay, decay], 1)
            dec_ref[c, h] = wide
            key = head_steps(k_ref, rows, h)
            value = head_steps(v_ref, rows, h)
            beta = jnp.concatenate(
                [beta_ref[rows, 2 * h + j : 2 * h + j + 1] for j in range(2)], 0
            )
            key2 = split(key)
            gram = mm3(key2, key2, NT)
            query = q_ref[rows, h * 128 : (h + 1) * 128]
            score_ref[c, h] = mm3(split(query), key2, NT) * wide
            reach_ref[c, h] = query * carried
            systems.append(
                jnp.where((later > 0) | same_token, beta * gram * twice(wide), 0.0)
            )
            rhs.append(jnp.concatenate([beta * twice(carried) * key, beta * value], 1))
            tails.append(key * twice(tail))
            keeps.append(keep)
        inverse = [eye - jnp.where(same_token, n, 0.0) for n in systems]
        for level in range(6):
            part = (later >> level) == 1
            blocks = [split(jnp.where(part, n, 0.0)) for n in systems]
            inverse2 = [split(x) for x in inverse]
            first = [split(mm3(b, x)) for b, x in zip(blocks, inverse2)]
            inverse = [x - mm3(x2, y) for x, x2, y in zip(inverse, inverse2, first)]
        for h in heads:
            t_ref[c, h] = inverse[h]
            mixed = mm3(split(inverse[h]), split(rhs[h]))
            w_ref[c, h] = mixed[:, :128]
            u_ref[c, h] = mixed[:, 128:]
            product = mm3(split(jnp.transpose(mixed)), split(tails[h]))
            at_ref[c, h] = keeps[h] * eye - product[:128]
            bt_ref[c, h] = product[128:]
        return carry

    lax.fori_loop(0, nc, prepare, 0)

    for h in range(nh):
        st_ref[h, :128] = at_ref[0, h]
        st_ref[h, 128:] = bt_ref[0, h]

    def chain(c, carry):
        for h in range(nh):
            after = mm3(split(st_ref[h]), split(at_ref[c, h]))
            st_ref[h, :128] = after[:128]
            st_ref[h, 128:] = after[128:] + bt_ref[c, h]
        return carry

    lax.fori_loop(1, nc, chain, 0)


def output_kernel(nh, count, *refs):
    output_body(nh, refs[:count], *refs[count:])


def output_body(
    nh, map_refs, w_ref, u_ref, reach_ref, score_ref, at_ref, bt_ref, gate_ref, gain_ref, wout_ref,
    sin_ref, fresh_ref, core_ref, gated_ref, branch_ref,
):
    nc = w_ref.shape[0]
    states = []
    for h in range(nh):
        state = map_refs[0][h, 128:].astype(f32)
        for map_ref in map_refs[1:]:
            passed = split(map_ref[h, :128].astype(f32))
            state = mm3(split(state), passed) + map_ref[h, 128:].astype(f32)
        states.append(state)

    def advance(c, states):
        rows = rows_of(c)
        out = []
        for h in range(nh):
            cols = slice(h * 128, (h + 1) * 128)
            state = states[h]
            state2 = split(state)
            sin_ref[c, h] = state
            out.append(mm3(state2, split(at_ref[c, h])) + bt_ref[c, h])
            probe = jnp.concatenate([w_ref[c, h], reach_ref[c, h]], 0)
            seen = mm3(split(probe), state2, NT)
            fresh = u_ref[c, h] - seen[: 2 * CT]
            fresh_ref[c, h] = fresh
            core = seen[2 * CT :] + mm3(split(score_ref[c, h]), split(fresh))
            core_ref[rows, cols] = core
            unit = core * lax.rsqrt(jnp.mean(core * core, -1, keepdims=True) + EPS)
            gate = gate_ref[rows, cols]
            gated_ref[rows, cols] = (
                unit * gain_ref[:, cols] * (gate * jax.nn.sigmoid(gate))
            ).astype(bf16)
        return tuple(out)

    states = lax.fori_loop(0, nc, advance, tuple(states))
    for h in range(nh):
        sin_ref[nc, h] = states[h]
    branch_ref[...] = mm(gated_ref[...], wout_ref[...]).astype(bf16)


def adjoint_kernel(nh, count, me_ref, *refs):
    adjoint_body(nh, me_ref, refs[:count], *refs[count:])


def adjoint_body(
    nh, me_ref, g_refs, wout_ref, core_ref, gate_ref, gain_ref, score_ref, reach_ref, w_ref, at_ref,
    dcore_ref, dft_ref, dt_ref, dgate_ref, dgain_ref, local_ref,
    dgated_ref,
):
    nc = w_ref.shape[0]
    count = len(g_refs)
    each = g_refs[0].shape[0]
    for shift, g_ref in enumerate(g_refs):
        place = lax.rem(me_ref[0] + (count - shift), count) * each
        dgated_ref[pl.ds(pl.multiple_of(place, 16), each), :] = mm(g_ref[...], wout_ref[...], NT)

    def chunk(c, dgain):
        rows = rows_of(c)
        sums = []
        for h in range(nh):
            cols = slice(h * 128, (h + 1) * 128)
            core = core_ref[rows, cols]
            scale = lax.rsqrt(jnp.mean(core * core, -1, keepdims=True) + EPS)
            unit = core * scale
            gate = gate_ref[rows, cols]
            sig = jax.nn.sigmoid(gate)
            silu = gate * sig
            gain = gain_ref[:, cols]
            grad = dgated_ref[rows, cols]
            sums.append(jnp.sum(grad * unit * silu, 0, keepdims=True))
            dgate_ref[rows, cols] = grad * unit * gain * (sig * (1.0 + gate * (1.0 - sig)))
            dunit = grad * gain * silu
            dcore = scale * (dunit - unit * jnp.mean(dunit * unit, -1, keepdims=True))
            dcore_ref[rows, cols] = dcore
            across = jnp.transpose(dcore)
            dft = mm3(split(across), split(score_ref[c, h]))
            dft_ref[c, h] = dft
            left = jnp.concatenate([-dft, across], 1)
            right = jnp.concatenate([w_ref[c, h], reach_ref[c, h]], 0)
            dt_ref[c, h] = mm3(split(left), split(right))
        return dgain + jnp.concatenate(sums, 1)

    dgain_ref[...] = lax.fori_loop(0, nc, chunk, jnp.zeros(dgain_ref.shape, f32))

    def chain(i, carry):
        c = nc - 1 - i
        return tuple(
            mm3(split(carry[h]), split(at_ref[c, h]), NT) + dt_ref[c, h] for h in range(nh)
        )

    start = tuple(dt_ref[nc - 1, h] for h in range(nh))
    total = lax.fori_loop(1, nc, chain, start)
    for h in range(nh):
        local_ref[h] = total[h]


def backward_kernel(nh, count, *refs):
    backward_body(nh, refs[:count], refs[count : 2 * count], *refs[2 * count :])


def backward_body(
    nh, map_refs, local_refs, at_ref, dt_ref, dft_ref, dcore_ref, t_ref, fresh_ref, sin_ref,
    q_ref, k_ref, v_ref, beta_ref, gam_ref, dec_ref, conv_ref, pre_ref, info_ref, tq_ref, tk_ref, tv_ref,
    rate_ref, glog_ref, dgate_ref,
    gp_ref, rim_ref, tail_ref, taps_ref, dlog_ref,
    dconv_ref, small_ref,
):
    length = q_ref.shape[0]
    nc = length // CT
    nq = nh * 128
    width = 5 * nq
    ends = []
    for h in range(nh):
        end = local_refs[0][h].astype(f32)
        for map_ref, local_ref in zip(map_refs[1:], local_refs[1:]):
            passed = split(map_ref[h].astype(f32))
            end = mm3(split(end), passed, NT) + local_ref[h].astype(f32)
        ends.append(end)
    row, col, later, same_token = step_order()
    before = (later > 0) | same_token
    last_row = (iota2((CT, 1), 0) == CT - 1).astype(f32)
    dconv_ref[0:RIM, :] = jnp.zeros((RIM, width), f32)
    dconv_ref[RIM + length :, :] = jnp.zeros((RIM, width), f32)
    lane = iota2((CT, 128), 1)
    upper = (iota2((CT, CT), 0) <= iota2((CT, CT), 1)).astype(f32)

    def chunk(i, ends):
        c = nc - 1 - i
        rows = rows_of(c)
        store = rows_of(c, CT, RIM)
        info = info_ref[store, :]
        out = []
        small = jnp.zeros((CT, 128), f32)
        dgam = jnp.zeros((CT, 128), f32)
        for h in range(nh):
            cols = slice(h * 128, (h + 1) * 128)
            end = ends[h]
            end2 = split(end)
            out.append(mm3(end2, split(at_ref[c, h]), NT) + dt_ref[c, h])
            _, carried, tail, _ = decays(gam_ref, info, rows, h, nh)
            carried2, tail2 = twice(carried), twice(tail)
            key = head_steps(k_ref, rows, h)
            value = head_steps(v_ref, rows, h)
            query = q_ref[rows, cols]
            beta = jnp.concatenate(
                [beta_ref[rows, 2 * h + j : 2 * h + j + 1] for j in range(2)], 0
            )
            wide = dec_ref[c, h]
            full = jnp.where(before, twice(wide), 0.0)
            state = sin_ref[c, h]
            fresh = fresh_ref[c, h]
            fresh2 = split(fresh)
            dcore = dcore_ref[rows, cols]
            dft = dft_ref[c, h] + mm3(end2, split(key * tail2), NT)
            solved = jnp.transpose(mm3(split(dft), split(t_ref[c, h])))
            both = split(jnp.concatenate([solved, dcore], 0))
            through = mm3(both, split(state))
            pairs = mm3(both, fresh2, NT)
            dtail = mm3(fresh2, end2)
            em = -pairs[: 2 * CT] * full
            ps = pairs[2 * CT :] * wide
            mixed = mm3(split(jnp.concatenate([em, ps], 0)), split(key))
            turned = jnp.transpose(jnp.concatenate([beta * em, ps], 0))
            dkb = mm3(split(turned), split(jnp.concatenate([key, query], 0))) + tail2 * dtail
            x1 = mixed[: 2 * CT] - carried2 * through[: 2 * CT]
            dka = beta * x1
            dkey = dka + dkb
            dbeta = jnp.sum(key * x1 + solved * value, -1, keepdims=True)
            dvalue = beta * solved
            dquery = mixed[2 * CT :] + carried * through[2 * CT :]
            turn = jnp.sum(key * (dka - dkb), -1, keepdims=True)
            closing = jnp.sum(
                jnp.sum(end * sin_ref[c + 1, h], -1, keepdims=True), 0, keepdims=True
            )
            dg = (
                jnp.sum(query * dquery, -1, keepdims=True)
                + turn[:CT]
                + turn[CT:]
                + last_row * closing
            )
            dgam = jnp.where(lane == 2 * nh + h, dg, dgam)
            for j in range(2):
                small = jnp.where(lane == 2 * h + j, dbeta[j * CT : (j + 1) * CT], small)
            pre = conv_ref[rows, cols]
            sig = jax.nn.sigmoid(pre)
            dconv_ref[store, cols] = dquery * (sig * (1.0 + pre * (1.0 - sig)))
            for j in range(2):
                kcols = slice(nq + (2 * h + j) * 128, nq + (2 * h + j + 1) * 128)
                pre = conv_ref[rows, kcols]
                sig = jax.nn.sigmoid(pre)
                act = pre * sig
                scale = lax.rsqrt(jnp.sum(act * act, -1, keepdims=True) + EPS)
                unit = key[j * CT : (j + 1) * CT]
                grad = dkey[j * CT : (j + 1) * CT]
                grad = scale * (grad - unit * jnp.sum(unit * grad, -1, keepdims=True))
                dconv_ref[store, kcols] = grad * (sig * (1.0 + pre * (1.0 - sig)))
                vcols = slice(3 * nq + (2 * h + j) * 128, 3 * nq + (2 * h + j + 1) * 128)
                pre = conv_ref[rows, vcols]
                sig = jax.nn.sigmoid(pre)
                dconv_ref[store, vcols] = dvalue[j * CT : (j + 1) * CT] * (
                    sig * (1.0 + pre * (1.0 - sig))
                )
        dglog = exact(upper, dgam)
        small_ref[rows, :] = jnp.where(lane < 2 * nh, small, dglog)
        return tuple(out)

    lax.fori_loop(0, nc, chunk, tuple(ends))

    beta = beta_ref[...]
    small = small_ref[...]
    lanes = iota2(beta.shape, 1)
    grads = small * beta * jnp.where(lanes < 2 * nh, 1.0 - beta, rate_ref[...])
    dlog_ref[...] = jnp.sum(small * glog_ref[...], 0, keepdims=True)
    gp_ref[0:RIM, :] = jnp.zeros((RIM, gp_ref.shape[1]), bf16)
    gp_ref[RIM:, width : width + nq] = dgate_ref[...].astype(bf16)
    gp_ref[RIM:, width + nq :] = grads.astype(bf16)
    groups = ((tq_ref, 0, nh), (tk_ref, nq, 2 * nh), (tv_ref, 3 * nq, 2 * nh))

    def turned_back(grad, masks, taps, count):
        total = grad[:count] * taps[0:1]
        size = grad.shape[0]
        for m in range(1, 4):
            moved = pltpu.roll(grad * masks[:, m : m + 1], size - m, 0)
            total = total + moved[:count] * taps[m : m + 1]
        return total

    def conv_back(c, sums):
        info = info_ref[near(c, RIM), :]
        new = []
        for tap_ref, first, count in groups:
            for j in range(count):
                cols = slice(first + j * 128, first + (j + 1) * 128)
                taps = tap_ref[:, j * 128 : (j + 1) * 128].astype(f32)
                grad = dconv_ref[near(c, RIM), cols]
                gp_ref[rows_of(c, CT, RIM), cols] = turned_back(grad, info, taps, CT).astype(bf16)
                block = pre_ref[near(c, RIM - 8), cols]
                parts = [jnp.sum(grad[:CT] * block[8:], 0, keepdims=True)]
                for m in range(1, 4):
                    moved = pltpu.roll(block, m, 0)[8:]
                    parts.append(
                        jnp.sum(grad[:CT] * info[:CT, m : m + 1] * moved, 0, keepdims=True)
                    )
                new.append(jnp.concatenate(parts, 0))
        return sums + jnp.concatenate(new, 1)

    taps_ref[...] = lax.fori_loop(0, nc, conv_back, jnp.zeros((4, width), f32))
    for tap_ref, first, count in groups:
        cols = slice(first, first + count * 128)
        taps = tap_ref[...].astype(f32)
        early = slice(8, 24)
        rim = turned_back(dconv_ref[early, cols], info_ref[early, :], taps, 8)
        rim_ref[:, cols] = rim
        gp_ref[0:RIM, cols] = jnp.concatenate([jnp.zeros_like(rim), rim], 0).astype(bf16)
        late = slice(length, length + 24)
        tail_ref[:, cols] = turned_back(dconv_ref[late, cols], info_ref[late, :], taps, 16)


VMEM = pl.BlockSpec(memory_space=pltpu.VMEM)
SMEM = pl.BlockSpec(memory_space=pltpu.SMEM)


def kernel_call(body, name, args, outs, scratch=(), flops=0, mib=60):
    moved = sum(a.size * a.dtype.itemsize for a in args) + sum(
        s.size * s.dtype.itemsize for s in outs
    )
    return pl.pallas_call(
        body,
        name=name,
        in_specs=[SMEM if a.dtype == i32 else VMEM for a in args],
        out_specs=[VMEM] * len(outs),
        out_shape=outs,
        scratch_shapes=list(scratch),
        compiler_params=pltpu.CompilerParams(vmem_limit_bytes=mib * MIB),
        cost_estimate=pl.CostEstimate(flops=flops, bytes_accessed=moved, transcendentals=0),
    )(*args)


def sds(*shape, dtype=f32):
    return jax.ShapeDtypeStruct(shape, dtype)


def mixer_forward(me, tokens, rim, norm_gain, weights, taps, info, doc_rows, rate):
    length, width = tokens[0].shape
    length *= len(tokens)
    w_query, w_key, w_value, w_outgate, w_small = weights
    nh = w_query.shape[1] // 128
    nc, nq = length // CT, nh * 128
    per = (nc, nh)
    outs = dict(
        normed=sds(RIM + length, width, dtype=bf16),
        pre=sds(RIM + length, 5 * nq),
        conv=sds(length, 5 * nq),
        gate=sds(length, nq),
        q=sds(length, nq),
        k=sds(length, 2 * nq),
        v=sds(length, 2 * nq),
        beta=sds(length, 128),
        glog=sds(length, 128),
        gam=sds(length, 128),
        dec=sds(*per, CT, 128),
        t=sds(*per, 128, 128),
        w=sds(*per, 128, 128),
        u=sds(*per, 128, 128),
        reach=sds(*per, CT, 128),
        score=sds(*per, CT, 128),
        at=sds(*per, 128, 128),
        bt=sds(*per, 128, 128),
        st=sds(nh, 256, 128),
    )
    args = (me, *tokens, rim, norm_gain, w_query, w_key, w_value, w_outgate, w_small, *taps, info, doc_rows, rate)
    flops = 2 * length * width * 7 * nq + nc * nh * 60 * 2 * 128**3
    res = kernel_call(
        functools.partial(forward_kernel, nh, len(tokens)), "mixer_forward", args, list(outs.values()), flops=flops
    )
    return dict(zip(outs, res))


def mixer_output(maps, fwd, out_gain, w_out):
    nc, nh = fwd["w"].shape[:2]
    length = nc * CT
    outs = dict(
        sin=sds(nc + 1, nh, 128, 128),
        fresh=sds(nc, nh, 128, 128),
        core=sds(length, nh * 128),
        gated=sds(length, nh * 128, dtype=bf16),
        branch=sds(length, w_out.shape[1], dtype=bf16),
    )
    args = (*maps, *(fwd[n] for n in ("w", "u", "reach", "score", "at", "bt", "gate")), out_gain, w_out)
    res = kernel_call(
        functools.partial(output_kernel, nh, len(maps)), "mixer_output", args, list(outs.values()),
        flops=nc * nh * 12 * 2 * 128**3,
    )
    return dict(zip(outs, res))


def mixer_adjoint(me, grad, w_out, fwd, out, out_gain):
    nc, nh = fwd["w"].shape[:2]
    length = nc * CT
    outs = dict(
        dcore=sds(length, nh * 128),
        dft=sds(nc, nh, 128, 128),
        dt=sds(nc, nh, 128, 128),
        dgate=sds(length, nh * 128),
        dgain=sds(1, nh * 128),
        local=sds(nh, 128, 128),
    )
    args = (me, *grad, w_out, out["core"], fwd["gate"], out_gain, fwd["score"], fwd["reach"], fwd["w"], fwd["at"])
    res = kernel_call(
        functools.partial(adjoint_kernel, nh, len(grad)), "mixer_adjoint", args, list(outs.values()),
        scratch=[pltpu.VMEM((length, nh * 128), f32)],
        flops=nc * nh * 8 * 2 * 128**3,
    )
    return dict(zip(outs, res))


def mixer_backward(maps, local_sums, fwd, out, adj, info, taps, rate):
    nc, nh = fwd["w"].shape[:2]
    length, nq = nc * CT, nh * 128
    width = 5 * nq
    outs = dict(
        gp=sds(RIM + length, width + nq + 128, dtype=bf16),
        rim=sds(8, width),
        tail=sds(16, width),
        taps=sds(4, width),
        dlog=sds(1, 128),
    )
    args = (
        *maps, *local_sums, fwd["at"], adj["dt"], adj["dft"], adj["dcore"], fwd["t"], out["fresh"], out["sin"],
        *(fwd[n] for n in ("q", "k", "v", "beta", "gam", "dec", "conv", "pre")), info, *taps, rate,
        fwd["glog"], adj["dgate"],
    )
    res = kernel_call(
        functools.partial(backward_kernel, nh, len(maps)), "mixer_backward", args, list(outs.values()),
        scratch=[pltpu.VMEM((length + 2 * RIM, width), f32), pltpu.VMEM((length, 128), f32)],
        flops=nc * nh * 36 * 2 * 128**3,
    )
    return dict(zip(outs, res))


def token_info(doc_ids, rim_ids):
    ids = doc_ids.astype(f32)
    length = ids.shape[0]
    extended = jnp.concatenate([rim_ids.astype(f32), ids])
    masks = [(extended[3 - m : 3 - m + length] == ids).astype(f32) for m in range(4)]
    blocks = ids.reshape(-1, CT)
    last = blocks[:, -1:]
    previous = jnp.concatenate([rim_ids[-1:].astype(f32)[None], last[:-1]], 0)
    columns = masks + [
        (blocks == previous).astype(f32).reshape(-1),
        (blocks == last).astype(f32).reshape(-1),
        ids,
        jnp.zeros_like(ids),
    ]
    info = jnp.pad(jnp.stack(columns, 1), ((RIM, RIM), (0, 0)))
    return info, blocks[:, None, :]


def middle_kernel(count, tok_ref, *refs):
    parts, (gain_ref, middle_ref, normed_ref) = refs[:count], refs[count:]
    middle = tok_ref[...].astype(f32)
    total = parts[0][...].astype(f32)
    for part in parts[1:]:
        total = total + part[...].astype(f32)
    middle = middle + total
    middle_ref[...] = middle
    scale = lax.rsqrt(jnp.mean(middle * middle, -1, keepdims=True) + EPS)
    normed_ref[...] = (middle * scale * gain_ref[...]).astype(bf16)


def feed_kernel(
    own_ref, near_ref, far_ref, cot_ref, gate_w, up_w, down_w,
    x_ref, act_ref, ggate_ref, gup_ref, gnorm_ref, block_ref,
):
    each = own_ref.shape[0]
    x_ref[0:each, :] = own_ref[...]
    x_ref[each : 2 * each, :] = near_ref[...]
    x_ref[2 * each :, :] = far_ref[...]

    def rows(i, carry):
        at = rows_of(i, 2 * each)
        x = x_ref[at, :]
        gate = mm(x, gate_w[...])
        up = mm(x, up_w[...])
        sig = jax.nn.sigmoid(gate)
        silu = gate * sig
        act = (silu * up).astype(bf16)
        act_ref[at, :] = act
        grad = mm(cot_ref[at, :], down_w[...], NT)
        ggate = (grad * up * sig * (1.0 + gate * (1.0 - sig))).astype(bf16)
        gup = (grad * silu).astype(bf16)
        ggate_ref[at, :] = ggate
        gup_ref[at, :] = gup
        gnorm_ref[at, :] = (mm(ggate, gate_w[...], NT) + mm(gup, up_w[...], NT)).astype(bf16)
        block_ref[at, :] = mm(act, down_w[...]).astype(bf16)
        return carry

    lax.fori_loop(0, 2, rows, 0)


def norm_back(grad_normed, rows, gain):
    scale = lax.rsqrt(jnp.mean(rows * rows, -1, keepdims=True) + EPS)
    unit = rows * scale
    scaled = grad_normed * gain
    grad_rows = scale * (scaled - unit * jnp.mean(scaled * unit, -1, keepdims=True))
    return grad_rows, jnp.sum(grad_normed * unit, 0, keepdims=True)


def middle_back_kernel(a_ref, b_ref, c_ref, middle_ref, cot_ref, gain_ref, grad_ref, low_ref, sum_ref):
    total = a_ref[...].astype(f32) + b_ref[...].astype(f32) + c_ref[...].astype(f32)
    rows, sum_ref[...] = norm_back(total, middle_ref[...], gain_ref[...])
    grad = cot_ref[...].astype(f32) + rows
    grad_ref[...] = grad
    low_ref[...] = grad.astype(bf16)


def tokens_back_kernel(count, *refs):
    parts, (tok_ref, gain_ref, middle_ref, grad_ref) = refs[:count], refs[count:]
    total = parts[0][...].astype(f32)
    for part in parts[1:]:
        total = total + part[...].astype(f32)
    rows, _ = norm_back(total, tok_ref[...].astype(f32), gain_ref[...])
    grad_ref[...] = middle_ref[...] + rows


def normed_back_kernel(gp_ref, tail_ref, late_ref, w_ref, normed_ref, gain_ref, out_ref, sum_ref, full_ref):
    length = out_ref.shape[0]
    width = tail_ref.shape[1]
    last = slice(length, length + RIM)
    full_ref[...] = gp_ref[...]
    late = jnp.concatenate([jnp.zeros_like(late_ref), late_ref[...]], 0)
    full_ref[last, 0:width] = (tail_ref[...] + late).astype(bf16)

    def rows(i, total):
        grad = mm(full_ref[rows_of(i, 256, RIM), :], w_ref[...], NT)
        out_ref[rows_of(i, 256), :] = grad.astype(bf16)
        unit = normed_ref[rows_of(i, 256, RIM), :].astype(f32)
        return total + jnp.sum(grad * unit, 0, keepdims=True)

    total = lax.fori_loop(0, length // 256, rows, jnp.zeros(sum_ref.shape, f32))
    sum_ref[...] = total / gain_ref[...]


def ring(value, axis):
    count = lax.axis_size(axis)
    return [value] + [
        lax.ppermute(value, axis, [(i, (i + shift) % count) for i in range(count)])
        for shift in range(1, count)
    ]


def along(value, axis, shift):
    count = lax.axis_size(axis)
    pairs = [(i, i + shift) for i in range(count) if 0 <= i + shift < count]
    return lax.ppermute(value, axis, pairs)


def crossed(value, axis, bit=0):
    return lax.ppermute(value, axis, [(i, i ^ (1 << bit)) for i in range(lax.axis_size(axis))])


def ring_scatter(value, axis):
    count, me = lax.axis_size(axis), lax.axis_index(axis)
    blocks = value.reshape((count, -1) + value.shape[1:])

    def block(place):
        return lax.dynamic_index_in_dim(blocks, lax.rem(place, count), 0, False)

    return [block(me)] + [
        lax.ppermute(block(me + shift), axis, [(i, (i + shift) % count) for i in range(count)])
        for shift in range(1, count)
    ]


def add_up(parts):
    total = parts[0].astype(f32)
    for part in parts[1:]:
        total = total + part.astype(f32)
    return total


def sum_over(value, axis):
    return add_up(ring(value, axis))


def halved(value, dim, axis, bit):
    mine = (lax.axis_index(axis) >> bit) & 1
    given = lax.dynamic_slice_in_dim(value, 1 - mine, 1, dim)
    kept = lax.dynamic_slice_in_dim(value, mine, 1, dim)
    got = crossed(given, axis, bit)
    return (kept.astype(f32) + got.astype(f32)).astype(bf16)


def in_order(own, other, axis):
    first = (lax.axis_index(axis) & 1) == 0
    return [jnp.where(first, own, other), jnp.where(first, other, own)]


def bits_of(count):
    return count.bit_length() - 1


def rows_dot(left, right):
    return lax.dot_general(
        left, right, (((0,), (0,)), ((), ())), preferred_element_type=f32
    )


def on_device(
    tokens, doc_ids, norm_gain, w_query, w_key, w_value, w_beta, w_decay, w_outgate, conv_query,
    conv_key, conv_value, decay_log, out_gain, w_out, mlp_gain, w_gate, w_up, w_down, cotangent,
):
    head_n, seq_n, batch_n = (lax.axis_size(a) for a in ("head", "seq", "batch"))
    me = lax.axis_index("head")
    nh = w_decay.shape[1]
    nq = nh * 128
    each, model = tokens.shape
    length = each * head_n
    me_array = me.astype(i32).reshape(1)

    blocks = ring(tokens, "head")
    rim = jnp.zeros((RIM, model), bf16)
    for target in range(head_n):
        rim = rim + lax.ppermute(
            tokens[-RIM:],
            ("seq", "head"),
            [
                (s * head_n + head_n - 1, (s + 1) * head_n + target)
                for s in range(seq_n - 1)
            ],
        )
    rim_ids = along(doc_ids[-3:], "seq", 1)
    info, doc_rows = token_info(doc_ids, rim_ids)
    w_small = jnp.pad(
        jnp.concatenate([w_beta, w_decay], 1), ((0, 0), (0, 128 - 3 * nh))
    )
    rate = jnp.pad(-jnp.exp(decay_log), (2 * nh, 128 - 3 * nh))[None]
    weights = (w_query, w_key, w_value, w_outgate, w_small)
    taps = (conv_query, conv_key, conv_value)
    gain = norm_gain[None]
    fwd = mixer_forward(me_array, blocks, rim, gain, weights, taps, info, doc_rows, rate)

    state = fwd["st"]
    earlier = [along(state, "seq", s) for s in range(seq_n - 1, 0, -1)]
    out = mixer_output(earlier, fwd, out_gain[None], w_out)

    parts = ring_scatter(out["branch"], "head")
    middle, normed_mid = kernel_call(
        functools.partial(middle_kernel, len(parts)), "middle",
        (tokens, *parts, mlp_gain[None]),
        [sds(each, model), sds(each, model, dtype=bf16)],
    )
    near = crossed(normed_mid, "head")
    far = crossed(jnp.concatenate([normed_mid, near], 0), "batch")
    cot_pair = jnp.concatenate([cotangent, crossed(cotangent, "head")], 0)
    cot_all = jnp.concatenate([cot_pair, crossed(cot_pair, "batch")], 0)
    ways = 2 * batch_n
    hidden = w_gate.shape[1] // ways
    mine = ((me & 1) * batch_n + lax.axis_index("batch")) * hidden
    gate_w = lax.dynamic_slice_in_dim(w_gate, mine, hidden, 1)
    up_w = lax.dynamic_slice_in_dim(w_up, mine, hidden, 1)
    down_w = lax.dynamic_slice_in_dim(w_down, mine, hidden, 0)
    rows = 4 * each
    x_all, act, ggate, gup, gnorm, block_part = kernel_call(
        feed_kernel, "feed",
        (normed_mid, near, far, cot_all, gate_w, up_w, down_w),
        [
            sds(rows, model, dtype=bf16),
            *[sds(rows, hidden, dtype=bf16)] * 3,
            *[sds(rows, model, dtype=bf16)] * 2,
        ],
        flops=12 * rows * model * hidden,
    )

    def own_parts(value):
        pair = value[: 2 * each]
        other = crossed(value[2 * each :], "batch")
        given = (pair[each:].astype(f32) + other[each:].astype(f32)).astype(bf16)
        return pair[:each], other[:each], crossed(given, "head")

    grad_middle, grad_branch, grad_mlp_gain = kernel_call(
        middle_back_kernel, "middle_back",
        (*own_parts(gnorm), middle, cotangent, mlp_gain[None]),
        [sds(each, model), sds(each, model, dtype=bf16), sds(1, model)],
    )
    block_out = (middle + add_up(own_parts(block_part))).astype(bf16)

    grad_blocks = ring(grad_branch, "head")
    adj = mixer_adjoint(me_array, grad_blocks, w_out, fwd, out, out_gain[None])
    later_maps = [along(state[:, :128], "seq", -s) for s in range(seq_n - 1, 0, -1)]
    later = [along(adj["local"], "seq", -s) for s in range(seq_n - 1, 0, -1)]
    back = mixer_backward(later_maps, later, fwd, out, adj, info, taps, rate)
    late_rim = along(back["rim"], "seq", -1)
    w_all = jnp.concatenate(weights, 1)
    partial_normed, gain_part = kernel_call(
        normed_back_kernel, "normed_back",
        (back["gp"], back["tail"], late_rim, w_all, fwd["normed"], gain),
        [sds(length, model, dtype=bf16), sds(1, model)],
        scratch=[pltpu.VMEM(back["gp"].shape, bf16)],
        flops=2 * length * model * w_all.shape[1],
    )
    normed_parts = ring_scatter(partial_normed, "head")
    (grad_tokens,) = kernel_call(
        functools.partial(tokens_back_kernel, len(normed_parts)), "tokens_back",
        (*normed_parts, tokens, gain, grad_middle),
        [sds(each, model)],
    )

    def mixer_rows(partial):
        spread = partial.reshape((2, -1) + partial.shape[1:])
        half = halved(spread, 0, "batch", 0)[0]
        return add_up(ring_scatter(half, "seq"))

    grad_weights = mixer_rows(rows_dot(fwd["normed"], back["gp"]).astype(bf16))
    g_all = jnp.concatenate(grad_blocks[:1] + grad_blocks[:0:-1], 0)
    g_all = lax.dynamic_slice_in_dim(
        jnp.concatenate([g_all, g_all], 0), (head_n - me) * each, length, 0
    )
    grad_w_out = mixer_rows(rows_dot(g_all, out["gated"]).astype(bf16)).T

    seq_bits, pair_bits = bits_of(seq_n), bits_of(head_n) - 1
    own_rows = model // (batch_n * seq_n * head_n)
    dims = (batch_n,) + (2,) * (seq_bits + pair_bits + 1)

    def feed_rows(partial, order):
        value = partial.reshape(dims + (own_rows, partial.shape[1]))
        for bit in order:
            value = halved(value, seq_bits - bit, "seq", bit)
        for bit in range(pair_bits, 0, -1):
            value = halved(value, 1 + seq_bits + pair_bits - bit, "head", bit)
        value = value.reshape((batch_n, 2) + value.shape[-2:])
        mine = me & 1
        given = lax.dynamic_index_in_dim(value, 1 - mine, 1, False)
        kept = lax.dynamic_index_in_dim(value, mine, 1, False)
        pair = jnp.stack(in_order(kept, crossed(given, "head"), "head"), 1)
        core = lax.axis_index("batch")
        given = lax.dynamic_index_in_dim(pair, 1 - core, 0, False)
        kept = lax.dynamic_index_in_dim(pair, core, 0, False)
        quad = jnp.stack(in_order(kept, crossed(given, "batch"), "batch"), 1)
        return quad.reshape((ways,) + quad.shape[2:])

    up_order = list(range(seq_bits))
    in_parts = rows_dot(x_all, jnp.concatenate([ggate, gup], 1)).astype(bf16)
    down_part = rows_dot(cot_all, act).astype(bf16)
    in_rows = feed_rows(in_parts, up_order)
    down_rows = feed_rows(down_part, up_order[::-1])

    def joined(value):
        return jnp.swapaxes(value, 0, 1).reshape(own_rows, -1).astype(f32)

    grad_w_gate = joined(in_rows[..., :hidden])
    grad_w_up = joined(in_rows[..., hidden:])
    grad_w_down = joined(down_rows).T

    width = 5 * nq
    wide = max(width, model)

    def padded(value):
        return jnp.pad(value, ((0, 0), (0, wide - value.shape[1])))

    small = jnp.concatenate(
        [padded(v) for v in (back["taps"], back["dlog"], adj["dgain"], grad_mlp_gain, gain_part)], 0
    )
    small = sum_over(sum_over(small, "batch"), "seq")
    gains = sum_over(small[6:8, :model], "head")
    index = (lax.axis_index("batch") * seq_n + lax.axis_index("seq")) * head_n + me
    gains = lax.dynamic_slice_in_dim(gains, index * own_rows, own_rows, 1)

    cols = [0, nq, 3 * nq, 5 * nq, 6 * nq, 6 * nq + 2 * nh, 6 * nq + 3 * nh]
    grad_q, grad_k, grad_v, grad_g, grad_b, grad_d = (
        grad_weights[:, a:b] for a, b in zip(cols[:-1], cols[1:])
    )
    return (
        block_out, grad_tokens, gains[1], grad_q, grad_k, grad_v, grad_b, grad_d, grad_g,
        small[0:4, :nq], small[0:4, nq : 3 * nq], small[0:4, 3 * nq : width],
        small[4, 2 * nh : 3 * nh], small[5, :nq], grad_w_out, gains[0], grad_w_gate, grad_w_up,
        grad_w_down,
    )


def solution(mesh):
    return jax.shard_map(
        on_device,
        mesh=mesh,
        in_specs=(
            P(("batch", "seq", "head"), None),
            P(("batch", "seq")),
            P(),
            P(None, "head"),
            P(None, "head"),
            P(None, "head"),
            P(None, "head"),
            P(None, "head"),
            P(None, "head"),
            P(None, "head"),
            P(None, "head"),
            P(None, "head"),
            P("head"),
            P("head"),
            P("head", None),
            P(),
            P(),
            P(),
            P(),
            P(("batch", "seq", "head"), None),
        ),
        out_specs=(
            P(("batch", "seq", "head"), None),
            P(("batch", "seq", "head"), None),
            P(("batch", "seq", "head")),
            P(("batch", "seq"), "head"),
            P(("batch", "seq"), "head"),
            P(("batch", "seq"), "head"),
            P(("batch", "seq"), "head"),
            P(("batch", "seq"), "head"),
            P(("batch", "seq"), "head"),
            P(None, "head"),
            P(None, "head"),
            P(None, "head"),
            P("head"),
            P("head"),
            P("head", ("batch", "seq")),
            P(("batch", "seq", "head")),
            P(("batch", "seq", "head"), None),
            P(("batch", "seq", "head"), None),
            P(None, ("batch", "seq", "head")),
        ),
        check_vma=False,
    )
```

time: 1990 us -> 411 us (0.21)
  waiting for transfers between devices: 990 us -> 102 us
  matrix products: 310 us -> 10.9 us
  other arithmetic: 240 us -> 16.2 us
  local copies, waits for them, and re-layouts: 280 us -> 67.4 us
  Pallas kernels: 0 us -> 117 us
  blocking collectives: 111 us -> 0 us
  starting transfers between devices: 21.3 us -> 93.1 us
    reduce_scatter x5 -> x0, waiting for transfers between devices: 779 us -> none  [the longest x1 251 us: on_device(): lax.psum_scatter(grad_w_up, ('batch', 'seq', 'head'), scatter_dimension=0...]
    dot_general x235 -> x0, matrix products: 278 us -> none  [the longest x48 70.4 us: advance(): jnp.dot(block_scores, fresh_rows, precision=precise)]
    unnamed x21 -> x0, waiting for transfers between devices: 183 us -> none
    another operation x10 -> x5, other arithmetic: 167 us -> 0.17 us  [the longest x3 0.11 us: feed_rows(): quad = jnp.stack(in_order(kept, crossed(given, 'batch'), 'batch'), 1)]
    pallas_call x0 -> x9, Pallas kernels: none -> 117 us  [kernel_call(): pl.pallas_call(body, name=name, in_specs=[SMEM if a.dtype == i32 else VME...]
    ppermute x7 -> x60, waiting for transfers between devices: 2.76 us -> 102 us  [the longest x20 44.5 us: crossed(): lax.ppermute(value, axis, [(i, i ^ 1 << bit) for i in range(lax.axis_size...]
    ppermute x7 -> x60, starting transfers between devices: 20.1 us -> 93.1 us  [the longest x20 27.8 us: crossed(): lax.ppermute(value, axis, [(i, i ^ 1 << bit) for i in range(lax.axis_size...]
    squeeze x80 -> x8, local copies, waits for them, and re-layouts: 79.2 us -> 6.4 us  [the longest x4 5.25 us: block(): return lax.dynamic_index_in_dim(blocks, lax.rem(place, count), 0, False)]
  transfers between devices with their start and end apart: 21 -> 60, of which waited for: 13 -> 20; matrix products, arithmetic and copies ran while one was open for 14% -> 20% of each run, Pallas kernels for 0% -> 16%
where the time goes in v1:
time: 411 us; the launch traced here: 409 us
  Pallas kernels  117 us (28%)
  waiting for transfers between devices  102 us (25%)
  starting transfers between devices  93.1 us (23%)
  local copies, waits for them, and re-layouts  67.4 us (16%)
  other arithmetic  16.2 us (4%)
  matrix products  10.9 us (3%)
    pallas_call x9, Pallas kernels, kernel_call(): pl.pallas_call(body, name=name, in_specs=[SMEM if a.dtype == i32 else VME...  117 us
    ppermute x20, waiting for transfers between devices, crossed(): lax.ppermute(value, axis, [(i, i ^ 1 << bit) for i in range(lax.axis_size...  44.5 us
    ppermute x12, waiting for transfers between devices, ring_scatter(): lax.ppermute(block(me + shift), axis, [(i, (i + shift) % count) for i in...  34.9 us
    ppermute x20, starting transfers between devices, crossed(): lax.ppermute(value, axis, [(i, i ^ 1 << bit) for i in range(lax.axis_size...  27.8 us
    ppermute x11, starting transfers between devices, along(): return lax.ppermute(value, axis, pairs)  25.4 us
    unnamed x104, local copies, waits for them, and re-layouts  24.5 us
    ppermute x13, starting transfers between devices, ring(): lax.ppermute(value, axis, [(i, (i + shift) % count) for i in range(count)])  23.1 us
    ppermute x13, waiting for transfers between devices, ring(): lax.ppermute(value, axis, [(i, (i + shift) % count) for i in range(count)])  14.2 us
  transfers between devices with their start and end apart: 60, of which 20 were waited for; matrix products, arithmetic and copies ran while one was open for 20% of the time, Pallas kernels for 16%

profile of v1, /device:TPU:0, one launch (start us, length us, event | category | flops | bytes accessed | tf_op | source)
XLA Modules:
  0.0 408.7 jit_solution(7608729633312682974)
XLA Ops:
  0.7 3.1 collective-permute-start
  9.9 3.4 collective-permute-start.7
  29.3 40.4 %mixer_forward.1 = (bf16[528,1024]{1,0:T(8,128)(2,1)}, f32[528,1280]{1,0:T(8,128)}, f32[512,1280]{1,0:T(8,128)}, f32[512,256]{1,0:T(8,128)}, f32[512,256]{1,0:T(...) custom-call(s32[1]{0:T(128)} %bitcast.me_ref, ...), custom_call_target="tpu_custom_call" | custom-call | flops 5905580032 | bytes 21939716 | tf_op jit(solution)/shard_map/mixer_forward/pallas_call | solution.py:502
  69.7 8.4 %collective-permute-start.8 = (f32[2,256,128]{2,1,0:T(8,128)}, f32[2,256,128]{2,1,0:T(8,128)S(1)}, u32[]{:S(2)}, u32[]{:S(2)}) collective-permute-start(f32[2,256,128]{2,1,0:T(8,128)} %get-tuple-element.67), channel_id=1, source_target_pairs={{0,12},{1,13},{2,14},{3,15},{16,28},{17,29},{18,30},{19,31}} | collective-permute-start | bytes 786440 | tf_op jit(solution)/shard_map/ppermute | solution.py:730
  78.1 2.8 collective-permute-start.9
  84.5 5.6 %collective-permute-done.9.refs_1_ = f32[2,256,128]{2,1,0:T(8,128)S(1)} collective-permute-done((f32[2,256,128]{2,1,0:T(8,128)}, f32[2,256,128]{2,1,0:T(8,128)S(1)}, u32[]{:S(2)}, u32[]{:S(2)}) %collective-permute-start.9) | collective-permute-done | bytes 262176 | tf_op jit(solution)/shard_map/ppermute | solution.py:730
  90.9 10.7 %mixer_output.1 = (f32[9,2,128,128]{3,2,1,0:T(8,128)}, f32[8,2,128,128]{3,2,1,0:T(8,128)}, f32[512,256]{1,0:T(8,128)}, bf16[512,256]{1,0:T(8,128)(2,1)}, bf16[512,1024]{1,0:T(8,128)(2,1)}) custom-call(f32[2,256,128]{2,1,0:T(8,128)} %copy-done.23, f32[2,256,128]{2,1,0:T(8,128)} %copy-done.24, f32[2,256,128]{2,1,0:T(8,128)} %copy-done.25, ...), custom_call_target="tpu_custom_call" | custom-call | flops 805306368 | bytes 11142144 | tf_op jit(solution)/shard_map/mixer_output/pallas_call | solution.py:502
  108.0 6.7 %collective-permute-done.11.refs_1_ = bf16[128,1024]{1,0:T(8,128)(2,1)S(1)} collective-permute-done((bf16[128,1024]{1,0:T(8,128)(2,1)S(1)}, bf16[128,1024]{1,0:T(8,128)(2,1)S(1)}, u32[]{:S(2)}, u32[]{:S(2)}) %collective-permute-start.11) | collective-permute-done | bytes 262176 | tf_op jit(solution)/shard_map/ppermute | solution.py:745
  114.8 7.9 %collective-permute-done.12.refs_2_ = bf16[128,1024]{1,0:T(8,128)(2,1)S(1)} collective-permute-done((bf16[128,1024]{1,0:T(8,128)(2,1)S(1)}, bf16[128,1024]{1,0:T(8,128)(2,1)S(1)}, u32[]{:S(2)}, u32[]{:S(2)}) %collective-permute-start.12) | collective-permute-done | bytes 262176 | tf_op jit(solution)/shard_map/ppermute | solution.py:745
  126.4 5.4 %collective-permute-start.14 = (bf16[128,1024]{1,0:T(8,128)(2,1)}, bf16[128,1024]{1,0:T(8,128)(2,1)S(1)}, u32[]{:S(2)}, u32[]{:S(2)}) collective-permute-start(bf16[128,1024]{1,0:T(8,128)(2,1)} %get-tuple-element.77.own_ref), channel_id=1, source_target_pairs={{0,1},{1,0},{2,3},{3,2},{4,5},{5,4},{6,7},{7,6},{8,9},{9,8},{10,11... | collective-permute-start | bytes 786440 | tf_op jit(solution)/shard_map/ppermute | solution.py:734
  134.6 4.1 collective-permute-done.14.near_ref
  138.8 5.4 %constant_dynamic-slice_fusion.13 = (bf16[1024,704]{1,0:T(8,128)(2,1)}, bf16[1024,704]{1,0:T(8,128)(2,1)}) fusion(bf16[1024,2816]{1,0:T(8,128)(2,1)} %param.37, s32[]{:T(128)S(6)} %select_n.146, bf16[1024,2816]{1,0:T(8,128)(2,1)} %param.36), kind=kLoop, calls=%fused_computation.109 | loop fusion | bytes 5767172 | tf_op jit(solution)/shard_map/dynamic_slice | solution.py:836
  149.5 10.2 %feed.1 = (bf16[512,1024]{1,0:T(8,128)(2,1)}, bf16[512,704]{1,0:T(8,128)(2,1)}, bf16[512,704]{1,0:T(8,128)(2,1)}, bf16[512,704]{1,0:T(8,128)(2,1)}, bf16[512,102...) custom-call(bf16[128,1024]{1,0:T(8,128)(2,1)} %get-tuple-element.77.own_ref, bf16[128,1024]{1,0:T(8,128)(2,1)} %copy-done.21, ...), custom_call_target="tpu_custom_call" | custom-call | flops 4429185024 | bytes 11730944 | tf_op jit(solution)/shard_map/feed/pallas_call | solution.py:502
  167.5 3.2 collective-permute-start.55
  170.7 3.5 convolution_convert_fusion
  180.7 8.0 %collective-permute-done.55 = bf16[2,1,2,2,2,32,704]{6,5,4,3,2,1,0:T(8,128)(2,1)S(1)} collective-permute-done((bf16[2,1,2,2,2,32,704]{6,5,4,3,2,1,0:T(8,128)(2,1)S(1)}, bf16[2,1,2,2,2,32,704]{6,5,4,3,2,1,0:T(8,128)(2,1)S(1)}, u32[]{:S(2)}, u32[]{:S(2)}) %collective-permute-start.55) | collective-permute-done | bytes 720928 | tf_op jit(solution)/shard_map/ppermute | solution.py:734
  202.2 3.2 collective-permute-done.25.refs_1_
  206.6 8.1 %collective-permute-done.26.refs_2_ = bf16[128,1024]{1,0:T(8,128)(2,1)S(1)} collective-permute-done((bf16[128,1024]{1,0:T(8,128)(2,1)}, bf16[128,1024]{1,0:T(8,128)(2,1)S(1)}, u32[]{:S(2)}, u32[]{:S(2)}) %collective-permute-start.26) | collective-permute-done | bytes 262176 | tf_op jit(solution)/shard_map/ppermute | solution.py:722
  217.3 12.4 %mixer_adjoint.1 = (f32[512,256]{1,0:T(8,128)}, f32[8,2,128,128]{3,2,1,0:T(8,128)}, f32[8,2,128,128]{3,2,1,0:T(8,128)}, f32[512,256]{1,0:T(8,128)}, f32[1,256]{1,0:T(1,128)}, /*index=5*/f32[2,128,128]{2,1,0:T(8,128)}) custom-call(s32[1]{0:T(128)} %bitcast.me_ref, bf16[128,1024]{1,0:T(8,128)(2,1)} %get-tuple-element.80.refs_0_, bf16[128,1024]{1,0:T(8,128)(2,1)} %copy-done.4, ...), custom_call_target="tpu_custom_call" | custom-call | flops 536870912 | bytes 9046020 | tf_op jit(solution)/shard_map/mixer_adjoint/pallas_call | solution.py:502
  244.6 2.7 collective-permute-start.50
  247.4 3.4 collective-permute-start.57
  251.9 29.4 %mixer_backward.1 = (bf16[528,1664]{1,0:T(8,128)(2,1)}, f32[8,1280]{1,0:T(8,128)}, f32[16,1280]{1,0:T(8,128)}, f32[4,1280]{1,0:T(4,128)}, f32[1,128]{1,0:T(1,128)}) custom-call(f32[2,128,128]{2,1,0:T(8,128)} %collective-permute-done.20.refs_0_, f32[2,128,128]{2,1,0:T(8,128)} %collective-permute-done.21.refs_1_, f32[2,128,128]{2,1,0:T(8,128)} %copy-done.26, ...), custom_call_target="tpu_custom_call" | custom-call | flops 2415919104 | bytes 19443712 | tf_op jit(solution)/shard_map/mixer_backward/pallas_call | solution.py:502
  282.7 4.7 %convolution_convert_fusion.1 = bf16[1024,1664]{1,0:T(8,128)(2,1)S(1)} fusion(bf16[528,1024]{1,0:T(8,128)(2,1)S(1)} %copy-done.42, bf16[528,1664]{1,0:T(8,128)(2,1)} %get-tuple-element.99.gp_ref), kind=kOutput, calls=%fused_computation.1 | convolution fusion | flops 1801060352 | bytes 6246400 | tf_op jit(solution)/shard_map/dot_general | solution.py:779
  291.2 6.3 %normed_back.1 = (bf16[512,1024]{1,0:T(8,128)(2,1)}, f32[1,1024]{1,0:T(1,128)}) custom-call(bf16[528,1664]{1,0:T(8,128)(2,1)} %get-tuple-element.99.gp_ref, f32[16,1280]{1,0:T(8,128)} %get-tuple-element.100.tail_ref, f32[8,1280]{1,0:T(8,128)} %copy-done.41, bf16[1024,1664]{1,0:T(8,128)(2,1)} %get-tuple-element.238.w_ref, ...), custom_call_target="tpu_custom_call" | custom-call | flops 1744830464 | bytes 7426048 | tf_op jit(solution)/shard_map/normed_back/pallas_call | solution.py:502
  301.4 4.8 %collective-permute-start.38 = (f32[8,1280]{1,0:T(8,128)S(1)}, f32[8,1280]{1,0:T(8,128)S(1)}, u32[]{:S(2)}, u32[]{:S(2)}) collective-permute-start(f32[8,1280]{1,0:T(8,128)S(1)} %add.255), channel_id=1, source_target_pairs={{0,12},{4,0},{8,4},{12,8},{1,13},{5,1},{9,5},{13,9},{2,14},{6,2},{... | collective-permute-start | bytes 122888 | tf_op jit(solution)/shard_map/ppermute | solution.py:722
  311.1 5.7 %collective-permute-start.41 = (f32[2,1024]{1,0:T(2,128)S(1)}, f32[2,1024]{1,0:T(2,128)S(1)}, u32[]{:S(2)}, u32[]{:S(2)}) collective-permute-start(f32[2,1024]{1,0:T(2,128)S(1)} %slice.156), channel_id=1, source_target_pairs={{0,3},{1,0},{2,1},{3,2},{4,7},{5,4},{6,5},{7,6},{8,11},{9,8},{10,9... | collective-permute-start | bytes 24584 | tf_op jit(solution)/shard_map/ppermute | solution.py:722
  323.8 3.8 collective-permute-start.58
  329.9 7.5 %collective-permute-done.51 = bf16[2,1,1,2,2,32,1408]{6,5,4,3,2,1,0:T(8,128)(2,1)S(1)} collective-permute-done((bf16[2,1,1,2,2,32,1408]{6,5,4,3,2,1,0:T(8,128)(2,1)S(1)}, bf16[2,1,1,2,2,32,1408]{6,5,4,3,2,1,0:T(8,128)(2,1)S(1)}, u32[]{:S(2)}, u32[]{:S(2)}) %collective-permute-start.51) | collective-permute-done | bytes 720928 | tf_op jit(solution)/shard_map/ppermute | solution.py:734
  347.3 22.4 %collective-permute-done.52 = bf16[2,1,1,1,2,32,1408]{6,5,4,3,2,1,0:T(8,128)(2,1)} collective-permute-done((bf16[2,1,1,1,2,32,1408]{6,5,4,3,2,1,0:T(8,128)(2,1)}, bf16[2,1,1,1,2,32,1408]{6,5,4,3,2,1,0:T(8,128)(2,1)}, u32[]{:S(2)}, u32[]{:S(2)}) %collective-permute-start.52) | collective-permute-done | bytes 360480 | tf_op jit(solution)/shard_map/ppermute | solution.py:734
  372.3 2.9 collective-permute-done.33.refs_2_
  387.9 6.5 %collective-permute-done.45 = bf16[128,1664]{1,0:T(8,128)(2,1)S(1)} collective-permute-done((bf16[128,1664]{1,0:T(8,128)(2,1)}, bf16[128,1664]{1,0:T(8,128)(2,1)S(1)}, u32[]{:S(2)}, u32[]{:S(2)}) %collective-permute-start.45) | collective-permute-done | bytes 426016 | tf_op jit(solution)/shard_map/ppermute | solution.py:745
  394.3 10.1 %collective-permute-done.44 = bf16[128,1664]{1,0:T(8,128)(2,1)} collective-permute-done((bf16[128,1664]{1,0:T(8,128)(2,1)}, bf16[128,1664]{1,0:T(8,128)(2,1)}, u32[]{:S(2)}, u32[]{:S(2)}) %collective-permute-start.44) | collective-permute-done | bytes 426016 | tf_op jit(solution)/shard_map/ppermute | solution.py:745
  (306 shorter events, 143.8 us)
Async XLA Ops:
  0.7 27.9 %collective-permute-start = (bf16[128,1024]{1,0:T(8,128)(2,1)}, bf16[128,1024]{1,0:T(8,128)(2,1)S(1)}, u32[]{:S(2)}, u32[]{:S(2)}) collective-permute-start(bf16[128,1024]{1,0:T(8,128)(2,1)} %refs_4_.3), channel_id=1, source_target_pairs={{0,1},{1,2},{2,3},{3,0},{4,5},{5,6},{6,7},{7,4},{8,9},{9,10},{10,1... | collective-permute-start | bytes 786440 | tf_op jit(solution)/shard_map/ppermute | solution.py:722
  3.8 24.8 %collective-permute-start.1 = (bf16[128,1024]{1,0:T(8,128)(2,1)}, bf16[128,1024]{1,0:T(8,128)(2,1)S(1)}, u32[]{:S(2)}, u32[]{:S(2)}) collective-permute-start(bf16[128,1024]{1,0:T(8,128)(2,1)} %refs_4_.3), channel_id=1, source_target_pairs={{0,2},{1,3},{2,0},{3,1},{4,6},{5,7},{6,4},{7,5},{8,10},{9,11},{10,... | collective-permute-start | bytes 786440 | tf_op jit(solution)/shard_map/ppermute | solution.py:722
  6.3 22.2 %collective-permute-start.2 = (bf16[128,1024]{1,0:T(8,128)(2,1)}, bf16[128,1024]{1,0:T(8,128)(2,1)}, u32[]{:S(2)}, u32[]{:S(2)}) collective-permute-start(bf16[128,1024]{1,0:T(8,128)(2,1)} %refs_4_.3), channel_id=1, source_target_pairs={{0,3},{1,0},{2,1},{3,2},{4,7},{5,4},{6,5},{7,6},{8,11},{9,8},{10,9... | collective-permute-start | bytes 786440 | tf_op jit(solution)/shard_map/ppermute | solution.py:722
  8.5 17.1 %collective-permute-start.6 = (bf16[16,1024]{1,0:T(8,128)(2,1)S(1)}, bf16[16,1024]{1,0:T(8,128)(2,1)S(1)}, u32[]{:S(2)}, u32[]{:S(2)}) collective-permute-start(bf16[16,1024]{1,0:T(8,128)(2,1)S(1)} %slice.117), channel_id=1, source_target_pairs={{3,7},{7,11},{11,15},{19,23},{23,27},{27,31}} | collective-permute-start | bytes 98312 | tf_op jit(solution)/shard_map/ppermute | solution.py:799
  9.9 13.5 %collective-permute-start.7 = (s32[3]{0:T(128)S(1)}, s32[3]{0:T(128)S(1)}, u32[]{:S(2)}, u32[]{:S(2)}) collective-permute-start(s32[3]{0:T(128)S(1)} %slice.118), channel_id=1, source_target_pairs={{0,4},{4,8},{8,12},{1,5},{5,9},{9,13},{2,6},{6,10},{10,14},{3,7},{... | collective-permute-start | bytes 44 | tf_op jit(solution)/shard_map/ppermute | solution.py:730
  69.7 14.8 %collective-permute-start.8 = (f32[2,256,128]{2,1,0:T(8,128)}, f32[2,256,128]{2,1,0:T(8,128)S(1)}, u32[]{:S(2)}, u32[]{:S(2)}) collective-permute-start(f32[2,256,128]{2,1,0:T(8,128)} %get-tuple-element.67), channel_id=1, source_target_pairs={{0,12},{1,13},{2,14},{3,15},{16,28},{17,29},{18,30},{19,31}} | collective-permute-start | bytes 786440 | tf_op jit(solution)/shard_map/ppermute | solution.py:730
  105.5 17.2 %collective-permute-start.12 = (bf16[128,1024]{1,0:T(8,128)(2,1)S(1)}, bf16[128,1024]{1,0:T(8,128)(2,1)S(1)}, u32[]{:S(2)}, u32[]{:S(2)}) collective-permute-start(bf16[128,1024]{1,0:T(8,128)(2,1)S(1)} %get-tuple-element.218), channel_id=1, source_target_pairs={{0,2},{1,3},{2,0},{3,1},{4,6},{5,7},{6,4},{7,5},{8,10},{9,11},{10,... | collective-permute-start | bytes 786440 | tf_op jit(solution)/shard_map/ppermute | solution.py:745
  105.5 17.8 %collective-permute-start.13 = (bf16[128,1024]{1,0:T(8,128)(2,1)S(1)}, bf16[128,1024]{1,0:T(8,128)(2,1)S(1)}, u32[]{:S(2)}, u32[]{:S(2)}) collective-permute-start(bf16[128,1024]{1,0:T(8,128)(2,1)S(1)} %get-tuple-element.217), channel_id=1, source_target_pairs={{0,3},{1,0},{2,1},{3,2},{4,7},{5,4},{6,5},{7,6},{8,11},{9,8},{10,9... | collective-permute-start | bytes 786440 | tf_op jit(solution)/shard_map/ppermute | solution.py:745
  107.9 26.6 %collective-permute-start.16 = (bf16[128,1024]{1,0:T(8,128)(2,1)S(1)}, bf16[128,1024]{1,0:T(8,128)(2,1)S(1)}, u32[]{:S(2)}, u32[]{:S(2)}) collective-permute-start(bf16[128,1024]{1,0:T(8,128)(2,1)S(1)} %copy-done.10), channel_id=1, source_target_pairs={{0,1},{1,0},{2,3},{3,2},{4,5},{5,4},{6,7},{7,6},{8,9},{9,8},{10,11... | collective-permute-start | bytes 786440 | tf_op jit(solution)/shard_map/ppermute | solution.py:734
  134.5 13.1 %collective-permute-start.17 = (bf16[256,1024]{1,0:T(8,128)(2,1)S(1)}, bf16[256,1024]{1,0:T(8,128)(2,1)S(1)}, u32[]{:S(2)}, u32[]{:S(2)}) collective-permute-start(bf16[256,1024]{1,0:T(8,128)(2,1)S(1)} %pad_maximum_fusion.1), channel_id=1, source_target_pairs={{0,16},{16,0},{1,17},{17,1},{2,18},{18,2},{3,19},{19,3},{4,20},{20... | collective-permute-start | bytes 1572872 | tf_op jit(solution)/shard_map/ppermute | solution.py:734
  144.8 96.9 %collective-permute-start.20 = (f32[2,128,128]{2,1,0:T(8,128)}, f32[2,128,128]{2,1,0:T(8,128)}, u32[]{:S(2)}, u32[]{:S(2)}) collective-permute-start(f32[2,128,128]{2,1,0:T(8,128)} %slice.130), channel_id=1, source_target_pairs={{12,0},{13,1},{14,2},{15,3},{28,16},{29,17},{30,18},{31,19}} | collective-permute-start | bytes 393224 | tf_op jit(solution)/shard_map/ppermute | solution.py:730
  146.1 98.6 %collective-permute-start.21 = (f32[2,128,128]{2,1,0:T(8,128)}, f32[2,128,128]{2,1,0:T(8,128)}, u32[]{:S(2)}, u32[]{:S(2)}) collective-permute-start(f32[2,128,128]{2,1,0:T(8,128)} %slice.130), channel_id=1, source_target_pairs={{8,0},{12,4},{9,1},{13,5},{10,2},{14,6},{11,3},{15,7},{24,16},{28,... | collective-permute-start | bytes 393224 | tf_op jit(solution)/shard_map/ppermute | solution.py:730
  167.5 21.2 %collective-permute-start.55 = (bf16[2,1,2,2,2,32,704]{6,5,4,3,2,1,0:T(8,128)(2,1)S(1)}, bf16[2,1,2,2,2,32,704]{6,5,4,3,2,1,0:T(8,128)(2,1)S(1)}, u32[]{:S(2)}, u32[]{:S(2)}) collective-permute-start(bf16[2,1,2,2,2,32,704]{6,5,4,3,2,1,0:T(8,128)(2,1)S(1)} %constant_dynamic-slice_fusion.5), channel_id=1, source_target_pairs={{0,8},{4,12},{8,0},{12,4},{1,9},{5,13},{9,1},{13,5},{2,10},{6,14},... | collective-permute-start | bytes 2162696 | tf_op jit(solution)/shard_map/ppermute | solution.py:734
  176.8 21.1 %collective-permute-start.19 = (bf16[128,1024]{1,0:T(8,128)(2,1)S(1)}, bf16[128,1024]{1,0:T(8,128)(2,1)}, u32[]{:S(2)}, u32[]{:S(2)}) collective-permute-start(bf16[128,1024]{1,0:T(8,128)(2,1)S(1)} %add_convert_fusion.9), channel_id=1, source_target_pairs={{0,1},{1,0},{2,3},{3,2},{4,5},{5,4},{6,7},{7,6},{8,9},{9,8},{10,11... | collective-permute-start | bytes 786440 | tf_op jit(solution)/shard_map/ppermute | solution.py:734
  195.5 19.3 %collective-permute-start.26 = (bf16[128,1024]{1,0:T(8,128)(2,1)}, bf16[128,1024]{1,0:T(8,128)(2,1)S(1)}, u32[]{:S(2)}, u32[]{:S(2)}) collective-permute-start(bf16[128,1024]{1,0:T(8,128)(2,1)} %get-tuple-element.80.refs_0_), channel_id=1, source_target_pairs={{0,2},{1,3},{2,0},{3,1},{4,6},{5,7},{6,4},{7,5},{8,10},{9,11},{10,... | collective-permute-start | bytes 786440 | tf_op jit(solution)/shard_map/ppermute | solution.py:722
  197.9 18.7 %collective-permute-start.27 = (bf16[128,1024]{1,0:T(8,128)(2,1)}, bf16[128,1024]{1,0:T(8,128)(2,1)S(1)}, u32[]{:S(2)}, u32[]{:S(2)}) collective-permute-start(bf16[128,1024]{1,0:T(8,128)(2,1)} %get-tuple-element.80.refs_0_), channel_id=1, source_target_pairs={{0,3},{1,0},{2,1},{3,2},{4,7},{5,4},{6,5},{7,6},{8,11},{9,8},{10,9... | collective-permute-start | bytes 786440 | tf_op jit(solution)/shard_map/ppermute | solution.py:722
  205.3 42.0 %collective-permute-start.22 = (f32[2,128,128]{2,1,0:T(8,128)}, f32[2,128,128]{2,1,0:T(8,128)S(1)}, u32[]{:S(2)}, u32[]{:S(2)}) collective-permute-start(f32[2,128,128]{2,1,0:T(8,128)} %slice.130), channel_id=1, source_target_pairs={{4,0},{8,4},{12,8},{5,1},{9,5},{13,9},{6,2},{10,6},{14,10},{7,3},{... | collective-permute-start | bytes 393224 | tf_op jit(solution)/shard_map/ppermute | solution.py:730
  214.8 28.2 %collective-permute-start.56 = (bf16[2,1,1,2,2,32,704]{6,5,4,3,2,1,0:T(8,128)(2,1)S(1)}, bf16[2,1,1,2,2,32,704]{6,5,4,3,2,1,0:T(8,128)(2,1)S(1)}, u32[]{:S(2)}, u32[]{:S(2)}) collective-permute-start(bf16[2,1,1,2,2,32,704]{6,5,4,3,2,1,0:T(8,128)(2,1)S(1)} %constant_dynamic-slice_fusion.4), channel_id=1, source_target_pairs={{0,4},{4,0},{8,12},{12,8},{1,5},{5,1},{9,13},{13,9},{2,6},{6,2},{1... | collective-permute-start | bytes 1081352 | tf_op jit(solution)/shard_map/ppermute | solution.py:734
  229.7 17.6 %collective-permute-start.28 = (f32[2,128,128]{2,1,0:T(8,128)}, f32[2,128,128]{2,1,0:T(8,128)S(1)}, u32[]{:S(2)}, u32[]{:S(2)}) collective-permute-start(f32[2,128,128]{2,1,0:T(8,128)} %get-tuple-element.82), channel_id=1, source_target_pairs={{12,0},{13,1},{14,2},{15,3},{28,16},{29,17},{30,18},{31,19}} | collective-permute-start | bytes 393224 | tf_op jit(solution)/shard_map/ppermute | solution.py:730
  244.6 73.4 %collective-permute-start.50 = (bf16[2,2,1,2,2,32,1408]{6,5,4,3,2,1,0:T(8,128)(2,1)}, bf16[2,2,1,2,2,32,1408]{6,5,4,3,2,1,0:T(8,128)(2,1)}, u32[]{:S(2)}, u32[]{:S(2)}) collective-permute-start(bf16[2,2,1,2,2,32,1408]{6,5,4,3,2,1,0:T(8,128)(2,1)} %constant_dynamic-slice_fusion.8), channel_id=1, source_target_pairs={{0,4},{4,0},{8,12},{12,8},{1,5},{5,1},{9,13},{13,9},{2,6},{6,2},{1... | collective-permute-start | bytes 4325384 | tf_op jit(solution)/shard_map/ppermute | solution.py:734
  247.4 80.9 %collective-permute-start.46 = (bf16[1,512,256]{2,1,0:T(8,128)(2,1)}, bf16[1,512,256]{2,1,0:T(8,128)(2,1)}, u32[]{:S(2)}, u32[]{:S(2)}) collective-permute-start(bf16[1,512,256]{2,1,0:T(8,128)(2,1)} %constant_dynamic-slice_fusion.9), channel_id=1, source_target_pairs={{0,16},{16,0},{1,17},{17,1},{2,18},{18,2},{3,19},{19,3},{4,20},{20... | collective-permute-start | bytes 786440 | tf_op jit(solution)/shard_map/ppermute | solution.py:734
  247.4 58.8 %collective-permute-start.57 = (bf16[2,1,1,1,2,32,704]{6,5,4,3,2,1,0:T(8,128)(2,1)S(1)}, bf16[2,1,1,1,2,32,704]{6,5,4,3,2,1,0:T(8,128)(2,1)}, u32[]{:S(2)}, u32[]{:S(2)}) collective-permute-start(bf16[2,1,1,1,2,32,704]{6,5,4,3,2,1,0:T(8,128)(2,1)S(1)} %constant_dynamic-slice_fusion.3), channel_id=1, source_target_pairs={{0,2},{1,3},{2,0},{3,1},{4,6},{5,7},{6,4},{7,5},{8,10},{9,11},{10,... | collective-permute-start | bytes 540680 | tf_op jit(solution)/shard_map/ppermute | solution.py:734
  319.9 17.4 %collective-permute-start.51 = (bf16[2,1,1,2,2,32,1408]{6,5,4,3,2,1,0:T(8,128)(2,1)S(1)}, bf16[2,1,1,2,2,32,1408]{6,5,4,3,2,1,0:T(8,128)(2,1)S(1)}, u32[]{:S(2)}, u32[]{:S(2)}) collective-permute-start(bf16[2,1,1,2,2,32,1408]{6,5,4,3,2,1,0:T(8,128)(2,1)S(1)} %constant_dynamic-slice_fusion.7), channel_id=1, source_target_pairs={{0,8},{4,12},{8,0},{12,4},{1,9},{5,13},{9,1},{13,5},{2,10},{6,14},... | collective-permute-start | bytes 2162696 | tf_op jit(solution)/shard_map/ppermute | solution.py:734
  323.8 54.8 %collective-permute-start.42 = (bf16[1,512,1664]{2,1,0:T(8,128)(2,1)}, bf16[1,512,1664]{2,1,0:T(8,128)(2,1)S(1)}, u32[]{:S(2)}, u32[]{:S(2)}) collective-permute-start(bf16[1,512,1664]{2,1,0:T(8,128)(2,1)} %constant_dynamic-slice_fusion.10), channel_id=1, source_target_pairs={{0,16},{16,0},{1,17},{17,1},{2,18},{18,2},{3,19},{19,3},{4,20},{20... | collective-permute-start | bytes 5111816 | tf_op jit(solution)/shard_map/ppermute | solution.py:734
  323.8 16.2 %collective-permute-start.58 = (bf16[2,32,704]{2,1,0:T(8,128)(2,1)S(1)}, bf16[2,32,704]{2,1,0:T(8,128)(2,1)S(1)}, u32[]{:S(2)}, u32[]{:S(2)}) collective-permute-start(bf16[2,32,704]{2,1,0:T(8,128)(2,1)S(1)} %dynamic-slice_bitcast_fusion.12), channel_id=1, source_target_pairs={{0,1},{1,0},{2,3},{3,2},{4,5},{5,4},{6,7},{7,6},{8,9},{9,8},{10,11... | collective-permute-start | bytes 270344 | tf_op jit(solution)/shard_map/ppermute | solution.py:734
  329.3 14.5 %collective-permute-start.48 = (bf16[128,256]{1,0:T(8,128)(2,1)S(1)}, bf16[128,256]{1,0:T(8,128)(2,1)S(1)}, u32[]{:S(2)}, u32[]{:S(2)}) collective-permute-start(bf16[128,256]{1,0:T(8,128)(2,1)S(1)} %get-tuple-element.237), channel_id=1, source_target_pairs={{0,8},{4,12},{8,0},{12,4},{1,9},{5,13},{9,1},{13,5},{2,10},{6,14},... | collective-permute-start | bytes 196616 | tf_op jit(solution)/shard_map/ppermute | solution.py:745
  339.9 29.7 %collective-permute-start.52 = (bf16[2,1,1,1,2,32,1408]{6,5,4,3,2,1,0:T(8,128)(2,1)}, bf16[2,1,1,1,2,32,1408]{6,5,4,3,2,1,0:T(8,128)(2,1)}, u32[]{:S(2)}, u32[]{:S(2)}) collective-permute-start(bf16[2,1,1,1,2,32,1408]{6,5,4,3,2,1,0:T(8,128)(2,1)} %constant_dynamic-slice_fusion.6), channel_id=1, source_target_pairs={{0,2},{1,3},{2,0},{3,1},{4,6},{5,7},{6,4},{7,5},{8,10},{9,11},{10,... | collective-permute-start | bytes 1081352 | tf_op jit(solution)/shard_map/ppermute | solution.py:734
  342.3 30.0 %collective-permute-start.32 = (bf16[128,1024]{1,0:T(8,128)(2,1)}, bf16[128,1024]{1,0:T(8,128)(2,1)}, u32[]{:S(2)}, u32[]{:S(2)}) collective-permute-start(bf16[128,1024]{1,0:T(8,128)(2,1)} %get-tuple-element.215), channel_id=1, source_target_pairs={{0,1},{1,2},{2,3},{3,0},{4,5},{5,6},{6,7},{7,4},{8,9},{9,10},{10,1... | collective-permute-start | bytes 786440 | tf_op jit(solution)/shard_map/ppermute | solution.py:745
  343.8 31.5 %collective-permute-start.33 = (bf16[128,1024]{1,0:T(8,128)(2,1)}, bf16[128,1024]{1,0:T(8,128)(2,1)}, u32[]{:S(2)}, u32[]{:S(2)}) collective-permute-start(bf16[128,1024]{1,0:T(8,128)(2,1)} %get-tuple-element.214), channel_id=1, source_target_pairs={{0,2},{1,3},{2,0},{3,1},{4,6},{5,7},{6,4},{7,5},{8,10},{9,11},{10,... | collective-permute-start | bytes 786440 | tf_op jit(solution)/shard_map/ppermute | solution.py:745
  346.5 28.8 %collective-permute-start.34 = (bf16[128,1024]{1,0:T(8,128)(2,1)}, bf16[128,1024]{1,0:T(8,128)(2,1)}, u32[]{:S(2)}, u32[]{:S(2)}) collective-permute-start(bf16[128,1024]{1,0:T(8,128)(2,1)} %get-tuple-element.213), channel_id=1, source_target_pairs={{0,3},{1,0},{2,1},{3,2},{4,7},{5,4},{6,5},{7,6},{8,11},{9,8},{10,9... | collective-permute-start | bytes 786440 | tf_op jit(solution)/shard_map/ppermute | solution.py:745
  383.1 21.4 %collective-permute-start.44 = (bf16[128,1664]{1,0:T(8,128)(2,1)}, bf16[128,1664]{1,0:T(8,128)(2,1)}, u32[]{:S(2)}, u32[]{:S(2)}) collective-permute-start(bf16[128,1664]{1,0:T(8,128)(2,1)} %get-tuple-element.212), channel_id=1, source_target_pairs={{0,8},{4,12},{8,0},{12,4},{1,9},{5,13},{9,1},{13,5},{2,10},{6,14},... | collective-permute-start | bytes 1277960 | tf_op jit(solution)/shard_map/ppermute | solution.py:745
  384.4 20.1 %collective-permute-start.43 = (bf16[128,1664]{1,0:T(8,128)(2,1)S(1)}, bf16[128,1664]{1,0:T(8,128)(2,1)}, u32[]{:S(2)}, u32[]{:S(2)}) collective-permute-start(bf16[128,1664]{1,0:T(8,128)(2,1)S(1)} %get-tuple-element.210), channel_id=1, source_target_pairs={{0,4},{4,8},{8,12},{12,0},{1,5},{5,9},{9,13},{13,1},{2,6},{6,10},{... | collective-permute-start | bytes 1277960 | tf_op jit(solution)/shard_map/ppermute | solution.py:745
  (72 other events, 521.4 us)

commit v2 on v1

v2 whole, which is shorter than its diff:
```python
import functools

import jax
import jax.numpy as jnp
from jax import lax
from jax.experimental import pallas as pl
from jax.experimental.pallas import tpu as pltpu
from jax.sharding import Mesh
from jax.sharding import PartitionSpec as P

bf16, f32, i32 = jnp.bfloat16, jnp.float32, jnp.int32
EPS = 1e-06
CT = 64
RIM = 16
NN = ((1,), (0,))
NT = ((1,), (1,))
MIB = 1 << 20
FORWARD, OUTPUT, ADJOINT, BACKWARD = 4, 4, 4, 4


def mm(a, b, dims=NN):
    return lax.dot_general(a, b, (dims, ((), ())), preferred_element_type=f32)


def split(x):
    high = x.astype(bf16)
    return high, (x - high.astype(f32)).astype(bf16)


def mm3(a, b, dims=NN):
    return mm(a[0], b[0], dims) + (mm(a[0], b[1], dims) + mm(a[1], b[0], dims))


def exact(a, b):
    return lax.dot_general(
        a, b, (NN, ((), ())), precision=lax.Precision.HIGHEST, preferred_element_type=f32
    )


def iota2(shape, dim):
    return lax.broadcasted_iota(i32, shape, dim)


def rows_of(c, size=CT, start=0):
    return pl.ds(pl.multiple_of(c * size + start, 16), size)


def near(c, start):
    return pl.ds(pl.multiple_of(c * CT + start, 8), CT + 8)


def step_order():
    size = 2 * CT
    row, col = iota2((size, size), 0), iota2((size, size), 1)
    row_tok, col_tok = row & (CT - 1), col & (CT - 1)
    later = jnp.where(row_tok > col_tok, row_tok ^ col_tok, 0)
    same_token = (row_tok == col_tok) & (row >= CT) & (col < CT)
    return row, col, later, same_token


def twice(x):
    return jnp.concatenate([x, x], 0)


def head_steps(ref, rows, h):
    return jnp.concatenate(
        [ref[rows, (2 * h + j) * 128 : (2 * h + j + 1) * 128] for j in range(2)], 0
    )


def decays(gam_ref, info, rows, h, nh):
    gcol = gam_ref[rows, 2 * nh + h : 2 * nh + h + 1]
    glast = gcol[CT - 1 : CT, :]
    carried = jnp.exp(gcol) * info[:, 4:5]
    tail = jnp.exp(jnp.minimum(glast - gcol, 0.0)) * info[:, 5:6]
    keep = carried[CT - 1 : CT, :]
    return gcol, carried, tail, keep


def forward_kernel(
    nh, count, me_ref, *refs
):
    tok_refs, refs = refs[:count], refs[count:]
    forward_body(nh, me_ref, tok_refs, *refs)


def forward_body(
    nh, me_ref, tok_refs, rim_ref, ng_ref, wq_ref, wk_ref, wv_ref, wg_ref, ws_ref, tq_ref, tk_ref, tv_ref,
    flags_ref, drow_ref, rate_ref,
    normed_ref, pre_ref, conv_ref, gate_ref, q_ref, k_ref, v_ref, beta_ref, glog_ref, gam_ref, dec_ref,
    t_ref, w_ref, u_ref, reach_ref, score_ref, at_ref, bt_ref, info_ref, low_ref, st_ref,
):
    length = pre_ref.shape[0] - RIM
    nc = length // CT
    gain = ng_ref[...]
    count = len(tok_refs)
    each = tok_refs[0].shape[0]

    def normal(x):
        x = x.astype(f32)
        scale = lax.rsqrt(jnp.mean(x * x, -1, keepdims=True) + EPS)
        return (x * scale * gain).astype(bf16)

    model = ng_ref.shape[1]
    normed_ref[0:RIM, :] = normal(rim_ref[:, :model])
    info_ref[...] = flags_ref[...]
    first = flags_ref[RIM : RIM + 8, :]
    ids = jnp.concatenate([rim_ref[8:, model : model + 8].astype(f32), first[:, 6:7] + jnp.zeros((8, 8), f32)], 0)
    row, col = iota2((8, 8), 0), iota2((8, 8), 1)
    for m in range(1, 4):
        same = (pltpu.roll(ids, m, 0)[8:] == ids[8:]).astype(f32)
        first = jnp.where((col == m) & (row < m), same, first)
    info_ref[RIM : RIM + 8, :] = first

    for shift, tok_ref in enumerate(tok_refs):
        place = lax.rem(me_ref[0] + (count - shift), count) * each

        def norm_rows(c, carry):
            target = pl.ds(pl.multiple_of(place + c * CT + RIM, 16), CT)
            normed_ref[target, :] = normal(tok_ref[rows_of(c), :])
            return carry

        lax.fori_loop(0, each // CT, norm_rows, 0)
    nq = nh * 128
    groups = ((wq_ref, 0, nq), (wk_ref, nq, 2 * nq), (wv_ref, 3 * nq, 2 * nq))

    for weight, first, width in groups:
        pre_ref[0:RIM, first : first + width] = (
            mm(normed_ref[0:RIM, :], weight[...]).astype(bf16).astype(f32)
        )

    def project(i, carry):
        rows = rows_of(i, 256, RIM)
        block = normed_ref[rows, :]
        for weight, first, width in groups:
            pre_ref[rows, first : first + width] = mm(block, weight[...]).astype(bf16).astype(f32)
        plain = rows_of(i, 256)
        gate_ref[plain, :] = mm(block, wg_ref[...])
        glog_ref[plain, :] = mm(block, ws_ref[...])
        return carry

    lax.fori_loop(0, length // 256, project, 0)
    logits = glog_ref[...]
    beta_ref[...] = jax.nn.sigmoid(logits)
    soft = jnp.maximum(logits, 0.0) + jnp.log1p(jnp.exp(-jnp.abs(logits)))
    glog = rate_ref[...] * soft
    glog_ref[...] = glog
    tri = (iota2((CT, CT), 0) >= iota2((CT, CT), 1)).astype(f32)
    for c in range(nc):
        gam_ref[c * CT : (c + 1) * CT, :] = exact(tri, glog[c * CT : (c + 1) * CT, :])

    def conv_rows(c, carry):
        rows = rows_of(c)
        info = info_ref[rows_of(c, CT, RIM), :]
        mask = [info[:, m : m + 1] for m in range(4)]
        for tap_ref, first, count, kind in (
            (tq_ref, 0, nh, "q"), (tk_ref, nq, 2 * nh, "k"), (tv_ref, 3 * nq, 2 * nh, "v")
        ):
            for j in range(count):
                cols = slice(first + j * 128, first + (j + 1) * 128)
                mine = slice(j * 128, (j + 1) * 128)
                taps = tap_ref[:, mine].astype(f32)
                block = pre_ref[near(c, RIM - 8), cols]
                total = block[8:] * taps[0:1]
                for m in range(1, 4):
                    total = total + pltpu.roll(block, m, 0)[8:] * mask[m] * taps[m : m + 1]
                conv_ref[rows, cols] = total
                out = total * jax.nn.sigmoid(total)
                if kind == "k":
                    out = out * lax.rsqrt(jnp.sum(out * out, -1, keepdims=True) + EPS)
                {"q": q_ref, "k": k_ref, "v": v_ref}[kind][rows, mine] = out
        return carry

    lax.fori_loop(0, nc, conv_rows, 0)

    row, col, later, same_token = step_order()
    eye = (row == col).astype(f32)
    small_row, small_col = iota2((CT, CT), 0), iota2((CT, CT), 1)

    def prepare(group, carry):
        items = [(group * FORWARD + i, h) for i in range(FORWARD) for h in range(nh)]
        systems, rhs, tails, keeps = [], [], [], []
        for c, h in items:
            rows = rows_of(c)
            info = info_ref[rows_of(c, CT, RIM), :]
            same = (info[:, 6:7] == drow_ref[c]) & (small_row >= small_col)
            gcol, carried, tail, keep = decays(gam_ref, info, rows, h, nh)
            grow = jnp.sum(jnp.where(small_row == small_col, gcol, 0.0), 0, keepdims=True)
            decay = jnp.where(same, jnp.exp(jnp.minimum(gcol - grow, 0.0)), 0.0)
            wide = jnp.concatenate([decay, decay], 1)
            dec_ref[c, h] = wide
            key = head_steps(k_ref, rows, h)
            value = head_steps(v_ref, rows, h)
            beta = jnp.concatenate(
                [beta_ref[rows, 2 * h + j : 2 * h + j + 1] for j in range(2)], 0
            )
            key2 = split(key)
            query = q_ref[rows, h * 128 : (h + 1) * 128]
            query2 = split(query)
            pairs = mm3([jnp.concatenate(x, 0) for x in zip(key2, query2)], key2, NT)
            score_ref[c, h] = pairs[2 * CT :] * wide
            reach_ref[c, h] = query * carried
            systems.append(
                jnp.where((later > 0) | same_token, beta * pairs[: 2 * CT] * twice(wide), 0.0)
            )
            rhs.append(jnp.concatenate([beta * twice(carried) * key, beta * value], 1))
            tails.append(key * twice(tail))
            keeps.append(keep)
        inverse = [eye - jnp.where(same_token, n, 0.0) for n in systems]
        for level in range(6):
            part = (later >> level) == 1
            blocks = [split(jnp.where(part, n, 0.0)) for n in systems]
            inverse2 = [split(x) for x in inverse]
            first = [split(mm3(b, x)) for b, x in zip(blocks, inverse2)]
            inverse = [x - mm3(x2, y) for x, x2, y in zip(inverse, inverse2, first)]
        mixed = [mm3(split(x), split(r)) for x, r in zip(inverse, rhs)]
        products = [mm3(split(jnp.transpose(m)), split(t)) for m, t in zip(mixed, tails)]
        for n, (c, h) in enumerate(items):
            t_ref[c, h] = inverse[n]
            w_ref[c, h] = mixed[n][:, :128]
            u_ref[c, h] = mixed[n][:, 128:]
            at_ref[c, h] = keeps[n] * eye - products[n][:128]
            bt_ref[c, h] = products[n][128:]
        return carry

    lax.fori_loop(0, nc // FORWARD, prepare, 0)

    for h in range(nh):
        st_ref[h, :128] = at_ref[0, h]
        st_ref[h, 128:] = bt_ref[0, h]

    def chain(c, carry):
        for h in range(nh):
            after = mm3(split(st_ref[h]), split(at_ref[c, h]))
            st_ref[h, :128] = after[:128]
            st_ref[h, 128:] = after[128:] + bt_ref[c, h]
        return carry

    lax.fori_loop(1, nc, chain, 0)
    low_ref[...] = st_ref[...].astype(bf16)


def output_kernel(nh, count, blocks, me_ref, *refs):
    output_body(nh, me_ref, refs[:count], *refs[count : -blocks - 1], refs[-blocks - 1 : -1], refs[-1])


def output_body(
    nh, me_ref, map_refs, w_ref, u_ref, reach_ref, score_ref, at_ref, bt_ref, gate_ref, gain_ref, wout_ref,
    sin_ref, fresh_ref, core_ref, gated_ref, branch_refs, all_ref,
):
    nc = w_ref.shape[0]
    states = []
    for h in range(nh):
        state = jnp.zeros((128, 128), f32)
        for distance in range(len(map_refs), 0, -1):
            map_ref = map_refs[distance - 1]
            passed = split(map_ref[h, :128].astype(f32))
            state = mm3(split(state), passed) + map_ref[h, 128:].astype(f32)
            state = jnp.where(me_ref[2] >= distance, state, 0.0)
        states.append(state)

    def chain(c, states):
        out = []
        for h in range(nh):
            sin_ref[c, h] = states[h]
            out.append(mm3(split(states[h]), split(at_ref[c, h])) + bt_ref[c, h])
        return tuple(out)

    states = lax.fori_loop(0, nc, chain, tuple(states))
    for h in range(nh):
        sin_ref[nc, h] = states[h]

    def outputs(group, carry):
        for c, h in [(group * OUTPUT + i, h) for i in range(OUTPUT) for h in range(nh)]:
            rows = rows_of(c)
            cols = slice(h * 128, (h + 1) * 128)
            state2 = split(sin_ref[c, h])
            probe = jnp.concatenate([w_ref[c, h], reach_ref[c, h]], 0)
            seen = mm3(split(probe), state2, NT)
            fresh = u_ref[c, h] - seen[: 2 * CT]
            fresh_ref[c, h] = fresh
            core = seen[2 * CT :] + mm3(split(score_ref[c, h]), split(fresh))
            core_ref[rows, cols] = core
            unit = core * lax.rsqrt(jnp.mean(core * core, -1, keepdims=True) + EPS)
            gate = gate_ref[rows, cols]
            gated_ref[rows, cols] = (
                unit * gain_ref[:, cols] * (gate * jax.nn.sigmoid(gate))
            ).astype(bf16)
        return carry

    lax.fori_loop(0, nc // OUTPUT, outputs, 0)
    all_ref[...] = mm(gated_ref[...], wout_ref[...]).astype(bf16)
    count = len(branch_refs)
    each = branch_refs[0].shape[0]
    for shift, branch_ref in enumerate(branch_refs):
        place = lax.rem(me_ref[0] + shift, count) * each
        branch_ref[...] = all_ref[pl.ds(pl.multiple_of(place, 16), each), :]


def adjoint_kernel(nh, count, me_ref, *refs):
    adjoint_body(nh, me_ref, refs[:count], *refs[count:])


def adjoint_body(
    nh, me_ref, g_refs, wout_ref, core_ref, gate_ref, gain_ref, score_ref, reach_ref, w_ref, at_ref,
    dcore_ref, dft_ref, dt_ref, dgate_ref, dgain_ref, local_ref, all_ref,
    dgated_ref,
):
    nc = w_ref.shape[0]
    count = len(g_refs)
    each = g_refs[0].shape[0]
    for shift, g_ref in enumerate(g_refs):
        place = lax.rem(me_ref[0] + (count - shift), count) * each
        all_ref[pl.ds(pl.multiple_of(place, 16), each), :] = g_ref[...]
    dgated_ref[...] = mm(all_ref[...], wout_ref[...], NT)

    def chunks(group, dgain):
        for i in range(ADJOINT):
            dgain = dgain + chunk(group * ADJOINT + i)
        return dgain

    def chunk(c):
        rows = rows_of(c)
        sums = []
        for h in range(nh):
            cols = slice(h * 128, (h + 1) * 128)
            core = core_ref[rows, cols]
            scale = lax.rsqrt(jnp.mean(core * core, -1, keepdims=True) + EPS)
            unit = core * scale
            gate = gate_ref[rows, cols]
            sig = jax.nn.sigmoid(gate)
            silu = gate * sig
            gain = gain_ref[:, cols]
            grad = dgated_ref[rows, cols]
            sums.append(jnp.sum(grad * unit * silu, 0, keepdims=True))
            dgate_ref[rows, cols] = (
                grad * unit * gain * (sig * (1.0 + gate * (1.0 - sig)))
            ).astype(bf16)
            dunit = grad * gain * silu
            dcore = scale * (dunit - unit * jnp.mean(dunit * unit, -1, keepdims=True))
            dcore_ref[rows, cols] = dcore
            across = jnp.transpose(dcore)
            dft = mm3(split(across), split(score_ref[c, h]))
            dft_ref[c, h] = dft
            left = jnp.concatenate([-dft, across], 1)
            right = jnp.concatenate([w_ref[c, h], reach_ref[c, h]], 0)
            dt_ref[c, h] = mm3(split(left), split(right))
        return jnp.concatenate(sums, 1)

    dgain_ref[...] = lax.fori_loop(0, nc // ADJOINT, chunks, jnp.zeros(dgain_ref.shape, f32))

    def chain(i, carry):
        c = nc - 1 - i
        return tuple(
            mm3(split(carry[h]), split(at_ref[c, h]), NT) + dt_ref[c, h] for h in range(nh)
        )

    start = tuple(dt_ref[nc - 1, h] for h in range(nh))
    total = lax.fori_loop(1, nc, chain, start)
    for h in range(nh):
        local_ref[h] = total[h].astype(bf16)


def normed_back(count, place_ref, gp_ref, weights, normed_ref, gain_ref, mlp_ref, out_refs, all_ref):
    each = out_refs[0].shape[0] - RIM
    length = all_ref.shape[0] - RIM
    total = jnp.zeros(gain_ref.shape, f32)
    for start in range(0, length, 256):
        rows = slice(start + (RIM if start else 0), start + 256 + RIM)
        first = 0
        grad = None
        for weight in weights:
            width = weight.shape[1]
            term = mm(gp_ref[rows, first : first + width], weight[...], NT)
            grad = term if grad is None else grad + term
            first += width
        all_ref[rows, :] = grad.astype(bf16)
        total = total + jnp.sum(grad * normed_ref[rows, :].astype(f32), 0, keepdims=True)
    rim = all_ref[0:RIM, :].astype(f32)
    row = iota2((RIM, 1), 0)
    gains = [*split(total / gain_ref[...]), *split(mlp_ref[...])]
    for n, gain in enumerate(gains):
        rim = jnp.where(row == n, gain.astype(f32), rim)
    rim = rim.astype(bf16)
    for shift, out_ref in enumerate(out_refs):
        place = lax.rem(place_ref[0] + shift, count) * each + RIM
        out_ref[0:each, :] = all_ref[pl.ds(pl.multiple_of(place, 16), each), :]
        out_ref[each:, :] = rim


def turn(left_ref, turned_ref):
    tokens, width = left_ref.shape
    for n in range(width // 128):
        turned_ref[n * 128 : (n + 1) * 128, :tokens] = jnp.transpose(
            left_ref[:, n * 128 : (n + 1) * 128]
        )


def two_halves(place_ref, turned, right, own_ref, given_ref, cols):
    half = turned.shape[0] // 2
    for core, out_ref in ((place_ref[1], own_ref), (1 - place_ref[1], given_ref)):
        rows = pl.ds(pl.multiple_of(core * half, 16), half)
        out_ref[0:half, cols] = mm(turned[rows, : right.shape[0]], right[...]).astype(out_ref.dtype)


def two_parts(value):
    high, low = split(value)
    return jnp.concatenate([high, low], 0)


def backward_kernel(nh, count, blocks, *refs):
    at = 2 * count + 1
    maps, local_sums, place, refs = refs[:count], refs[count : at - 1], refs[at - 1], refs[at:]
    inputs, refs = refs[:21], refs[21:]
    dgate, weights, (normed, gain, mlp, dgain), refs = refs[0], refs[1:6], refs[6:10], refs[10:]
    (grad, gated), refs = refs[:2], refs[2:]
    out_refs, (own, given), refs = refs[:blocks], refs[blocks : blocks + 2], refs[blocks + 2 :]
    gp, taps, dlog, dconv, small, ends, everything, turned = refs
    half, width = own.shape[0] - 8, gp.shape[1]
    wide, nq = own.shape[1], gated.shape[1]
    gp[0:RIM, width - nq :] = jnp.zeros((RIM, nq), bf16)
    gp[RIM:, width - nq :] = dgate[...]
    backward_body(nh, maps, local_sums, *inputs, gp, taps, dlog, dconv, small, ends)
    normed_back(blocks, place, gp, weights, normed, gain, mlp, out_refs, everything)
    turn(normed, turned)
    two_halves(place, turned, gp, own, given, slice(0, width))
    turn(grad, turned)
    two_halves(place, turned, gated, own, given, slice(width, wide))
    own[half:, :] = jnp.zeros((8, wide), f32)
    own[half : half + 4, : taps.shape[1]] = taps[...]
    own[half + 4 : half + 5, :128] = dlog[...]
    own[half + 4 : half + 5, 128 : 128 + dgain.shape[1]] = dgain[...]
    given[half:, :] = two_parts(own[half:, :])


def backward_body(
    nh, map_refs, local_refs, at_ref, dt_ref, dft_ref, dcore_ref, t_ref, fresh_ref, sin_ref,
    q_ref, k_ref, v_ref, beta_ref, gam_ref, dec_ref, conv_ref, pre_ref, info_ref, tq_ref, tk_ref, tv_ref,
    rate_ref, glog_ref,
    gp_ref, taps_ref, dlog_ref,
    dconv_ref, small_ref, ends_ref,
):
    length = q_ref.shape[0]
    nc = length // CT
    nq = nh * 128
    width = 5 * nq
    ends = []
    for h in range(nh):
        end = local_refs[0][h].astype(f32)
        for map_ref, local_ref in zip(map_refs[1:], local_refs[1:]):
            passed = split(map_ref[h, :128].astype(f32))
            end = mm3(split(end), passed, NT) + local_ref[h].astype(f32)
        ends.append(end)
    row, col, later, same_token = step_order()
    before = (later > 0) | same_token
    last_row = (iota2((CT, 1), 0) == CT - 1).astype(f32)
    dconv_ref[0:RIM, :] = jnp.zeros((RIM, width), f32)
    dconv_ref[RIM + length :, :] = jnp.zeros((RIM, width), f32)
    lane = iota2((CT, 128), 1)
    upper = (iota2((CT, CT), 0) <= iota2((CT, CT), 1)).astype(f32)

    def chain(i, ends):
        c = nc - 1 - i
        out = []
        for h in range(nh):
            ends_ref[c, h] = ends[h]
            out.append(mm3(split(ends[h]), split(at_ref[c, h]), NT) + dt_ref[c, h])
        return tuple(out)

    lax.fori_loop(0, nc, chain, tuple(ends))

    def chunks(group, carry):
        for i in range(BACKWARD):
            chunk(group * BACKWARD + i)
        return carry

    def chunk(c):
        rows = rows_of(c)
        store = rows_of(c, CT, RIM)
        info = info_ref[store, :]
        small = jnp.zeros((CT, 128), f32)
        dgam = jnp.zeros((CT, 128), f32)
        for h in range(nh):
            cols = slice(h * 128, (h + 1) * 128)
            end = ends_ref[c, h]
            end2 = split(end)
            _, carried, tail, _ = decays(gam_ref, info, rows, h, nh)
            carried2, tail2 = twice(carried), twice(tail)
            key = head_steps(k_ref, rows, h)
            value = head_steps(v_ref, rows, h)
            query = q_ref[rows, cols]
            beta = jnp.concatenate(
                [beta_ref[rows, 2 * h + j : 2 * h + j + 1] for j in range(2)], 0
            )
            wide = dec_ref[c, h]
            full = jnp.where(before, twice(wide), 0.0)
            state = sin_ref[c, h]
            fresh = fresh_ref[c, h]
            fresh2 = split(fresh)
            dcore = dcore_ref[rows, cols]
            dft = dft_ref[c, h] + mm3(end2, split(key * tail2), NT)
            solved = jnp.transpose(mm3(split(dft), split(t_ref[c, h])))
            both = split(jnp.concatenate([solved, dcore], 0))
            through = mm3(both, split(state))
            pairs = mm3(both, fresh2, NT)
            dtail = mm3(fresh2, end2)
            em = -pairs[: 2 * CT] * full
            ps = pairs[2 * CT :] * wide
            mixed = mm3(split(jnp.concatenate([em, ps], 0)), split(key))
            turned = jnp.transpose(jnp.concatenate([beta * em, ps], 0))
            dkb = mm3(split(turned), split(jnp.concatenate([key, query], 0))) + tail2 * dtail
            x1 = mixed[: 2 * CT] - carried2 * through[: 2 * CT]
            dka = beta * x1
            dkey = dka + dkb
            dbeta = jnp.sum(key * x1 + solved * value, -1, keepdims=True)
            dvalue = beta * solved
            dquery = mixed[2 * CT :] + carried * through[2 * CT :]
            turn = jnp.sum(key * (dka - dkb), -1, keepdims=True)
            closing = jnp.sum(
                jnp.sum(end * sin_ref[c + 1, h], -1, keepdims=True), 0, keepdims=True
            )
            dg = (
                jnp.sum(query * dquery, -1, keepdims=True)
                + turn[:CT]
                + turn[CT:]
                + last_row * closing
            )
            dgam = jnp.where(lane == 2 * nh + h, dg, dgam)
            for j in range(2):
                small = jnp.where(lane == 2 * h + j, dbeta[j * CT : (j + 1) * CT], small)
            pre = conv_ref[rows, cols]
            sig = jax.nn.sigmoid(pre)
            dconv_ref[store, cols] = dquery * (sig * (1.0 + pre * (1.0 - sig)))
            for j in range(2):
                kcols = slice(nq + (2 * h + j) * 128, nq + (2 * h + j + 1) * 128)
                pre = conv_ref[rows, kcols]
                sig = jax.nn.sigmoid(pre)
                act = pre * sig
                scale = lax.rsqrt(jnp.sum(act * act, -1, keepdims=True) + EPS)
                unit = key[j * CT : (j + 1) * CT]
                grad = dkey[j * CT : (j + 1) * CT]
                grad = scale * (grad - unit * jnp.sum(unit * grad, -1, keepdims=True))
                dconv_ref[store, kcols] = grad * (sig * (1.0 + pre * (1.0 - sig)))
                vcols = slice(3 * nq + (2 * h + j) * 128, 3 * nq + (2 * h + j + 1) * 128)
                pre = conv_ref[rows, vcols]
                sig = jax.nn.sigmoid(pre)
                dconv_ref[store, vcols] = dvalue[j * CT : (j + 1) * CT] * (
                    sig * (1.0 + pre * (1.0 - sig))
                )
        dglog = exact(upper, dgam)
        small_ref[rows, :] = jnp.where(lane < 2 * nh, small, dglog)

    lax.fori_loop(0, nc // BACKWARD, chunks, 0)

    beta = beta_ref[...]
    small = small_ref[...]
    lanes = iota2(beta.shape, 1)
    grads = small * beta * jnp.where(lanes < 2 * nh, 1.0 - beta, rate_ref[...])
    dlog_ref[...] = jnp.sum(small * glog_ref[...], 0, keepdims=True)
    gp_ref[0:RIM, 0 : width + 128] = jnp.zeros((RIM, width + 128), bf16)
    gp_ref[RIM:, width : width + 128] = grads.astype(bf16)
    groups = ((tq_ref, 0, nh), (tk_ref, nq, 2 * nh), (tv_ref, 3 * nq, 2 * nh))

    def turned_back(grad, masks, taps, count):
        total = grad[:count] * taps[0:1]
        size = grad.shape[0]
        for m in range(1, 4):
            moved = pltpu.roll(grad * masks[:, m : m + 1], size - m, 0)
            total = total + moved[:count] * taps[m : m + 1]
        return total

    def conv_back(c, sums):
        info = info_ref[near(c, RIM), :]
        new = []
        for tap_ref, first, count in groups:
            for j in range(count):
                cols = slice(first + j * 128, first + (j + 1) * 128)
                taps = tap_ref[:, j * 128 : (j + 1) * 128].astype(f32)
                grad = dconv_ref[near(c, RIM), cols]
                gp_ref[rows_of(c, CT, RIM), cols] = turned_back(grad, info, taps, CT).astype(bf16)
                block = pre_ref[near(c, RIM - 8), cols]
                parts = [jnp.sum(grad[:CT] * block[8:], 0, keepdims=True)]
                for m in range(1, 4):
                    moved = pltpu.roll(block, m, 0)[8:]
                    parts.append(
                        jnp.sum(grad[:CT] * info[:CT, m : m + 1] * moved, 0, keepdims=True)
                    )
                new.append(jnp.concatenate(parts, 0))
        return sums + jnp.concatenate(new, 1)

    taps_ref[...] = lax.fori_loop(0, nc, conv_back, jnp.zeros((4, width), f32))
    for tap_ref, first, count in groups:
        cols = slice(first, first + count * 128)
        taps = tap_ref[...].astype(f32)
        early = slice(8, 24)
        rim = turned_back(dconv_ref[early, cols], info_ref[early, :], taps, 8)
        gp_ref[0:RIM, cols] = jnp.concatenate([jnp.zeros_like(rim), rim], 0).astype(bf16)


VMEM = pl.BlockSpec(memory_space=pltpu.VMEM)
SMEM = pl.BlockSpec(memory_space=pltpu.SMEM)
ANY = pl.BlockSpec(memory_space=pl.ANY)


def kernel_call(body, name, args, outs, scratch=(), after=(), mib=60, cost=2):
    extra = len(after)

    def run(*refs):
        body(*refs[: len(args)], *refs[len(args) + extra :])

    return pl.pallas_call(
        run,
        name=name,
        in_specs=[SMEM if a.dtype == i32 else VMEM for a in args] + [ANY] * extra,
        out_specs=[VMEM] * len(outs),
        out_shape=outs,
        scratch_shapes=list(scratch),
        compiler_params=pltpu.CompilerParams(vmem_limit_bytes=mib * MIB),
        cost_estimate=pl.CostEstimate(flops=cost * 10**9, bytes_accessed=0, transcendentals=0),
    )(*args, *after)


def sds(*shape, dtype=f32):
    return jax.ShapeDtypeStruct(shape, dtype)


def mixer_forward(me, tokens, rim, norm_gain, weights, taps, info, doc_rows, rate):
    length, width = tokens[0].shape
    length *= len(tokens)
    w_query, w_key, w_value, w_outgate, w_small = weights
    nh = w_query.shape[1] // 128
    nc, nq = length // CT, nh * 128
    per = (nc, nh)
    outs = dict(
        normed=sds(RIM + length, width, dtype=bf16),
        pre=sds(RIM + length, 5 * nq),
        conv=sds(length, 5 * nq),
        gate=sds(length, nq),
        q=sds(length, nq),
        k=sds(length, 2 * nq),
        v=sds(length, 2 * nq),
        beta=sds(length, 128),
        glog=sds(length, 128),
        gam=sds(length, 128),
        dec=sds(*per, CT, 128),
        t=sds(*per, 128, 128),
        w=sds(*per, 128, 128),
        u=sds(*per, 128, 128),
        reach=sds(*per, CT, 128),
        score=sds(*per, CT, 128),
        at=sds(*per, 128, 128),
        bt=sds(*per, 128, 128),
        info=sds(length + 2 * RIM, 8),
        low=sds(nh, 256, 128, dtype=bf16),
    )
    args = (me, *tokens, rim, norm_gain, w_query, w_key, w_value, w_outgate, w_small, *taps, info, doc_rows, rate)
    res = kernel_call(
        functools.partial(forward_kernel, nh, len(tokens)), "mixer_forward", args, list(outs.values()),
        cost=25,
        scratch=[pltpu.VMEM((nh, 256, 128), f32)],
    )
    return dict(zip(outs, res))


def mixer_output(me, maps, fwd, out_gain, w_out, blocks, after=()):
    nc, nh = fwd["w"].shape[:2]
    length = nc * CT
    outs = dict(
        sin=sds(nc + 1, nh, 128, 128),
        fresh=sds(nc, nh, 128, 128),
        core=sds(length, nh * 128),
        gated=sds(length, nh * 128, dtype=bf16),
    )
    parts = [sds(length // blocks, w_out.shape[1], dtype=bf16)] * blocks
    args = (me, *maps, *(fwd[n] for n in ("w", "u", "reach", "score", "at", "bt", "gate")), out_gain, w_out)
    res = kernel_call(
        functools.partial(output_kernel, nh, len(maps), blocks), "mixer_output", args,
        [*outs.values(), *parts], cost=10,
        scratch=[pltpu.VMEM((length, w_out.shape[1]), bf16)],
        after=after,
    )
    return dict(zip(outs, res), branch=res[len(outs) :])


def mixer_adjoint(me, grad, w_out, fwd, out, out_gain, after=()):
    nc, nh = fwd["w"].shape[:2]
    length = nc * CT
    outs = dict(
        dcore=sds(length, nh * 128),
        dft=sds(nc, nh, 128, 128),
        dt=sds(nc, nh, 128, 128),
        dgate=sds(length, nh * 128, dtype=bf16),
        dgain=sds(1, nh * 128),
        local=sds(nh, 128, 128, dtype=bf16),
        g=sds(length, w_out.shape[1], dtype=bf16),
    )
    args = (me, *grad, w_out, out["core"], fwd["gate"], out_gain, fwd["score"], fwd["reach"], fwd["w"], fwd["at"])
    res = kernel_call(
        functools.partial(adjoint_kernel, nh, len(grad)), "mixer_adjoint", args, list(outs.values()),
        cost=10,
        scratch=[pltpu.VMEM((length, nh * 128), f32)],
        after=after,
    )
    return dict(zip(outs, res))


def mixer_backward(
    place, maps, local_sums, fwd, out, adj, taps, rate, weights, gain, mlp, blocks, after=()
):
    nc, nh = fwd["w"].shape[:2]
    length, nq = nc * CT, nh * 128
    width = 5 * nq
    model = gain.shape[1]
    parts = [sds(RIM + length // blocks, model, dtype=bf16)] * blocks
    columns = width + 128 + 2 * nq
    halves = [sds(model // 2 + 8, columns), sds(model // 2 + 16, columns, dtype=bf16)]
    args = (
        *maps, *local_sums, place, fwd["at"], adj["dt"], adj["dft"], adj["dcore"], fwd["t"], out["fresh"],
        out["sin"], *(fwd[n] for n in ("q", "k", "v", "beta", "gam", "dec", "conv", "pre", "info")), *taps,
        rate, fwd["glog"], adj["dgate"], *weights, fwd["normed"], gain, mlp, adj["dgain"],
        adj["g"], out["gated"],
    )
    *res, own, given = kernel_call(
        functools.partial(backward_kernel, nh, len(maps), blocks), "mixer_backward", args,
        [*parts, *halves], cost=300,
        scratch=[
            pltpu.VMEM((RIM + length, width + 128 + nq), bf16), pltpu.VMEM((4, width), f32),
            pltpu.VMEM((1, 128), f32),
            pltpu.VMEM((length + 2 * RIM, width), f32), pltpu.VMEM((length, 128), f32),
            pltpu.VMEM((nc, nh, 128, 128), f32), pltpu.VMEM((RIM + length, model), bf16),
            pltpu.VMEM((model, RIM + length), bf16),
        ],
        after=after,
    )
    return res, (own, given)


def token_info(doc_ids):
    ids = doc_ids.astype(f32)
    length = ids.shape[0]
    extended = jnp.concatenate([ids[:3], ids])
    masks = [(extended[3 - m : 3 - m + length] == ids).astype(f32) for m in range(4)]
    blocks = ids.reshape(-1, CT)
    last = blocks[:, -1:]
    previous = jnp.concatenate([blocks[:1, :1], last[:-1]], 0)
    columns = masks + [
        (blocks == previous).astype(f32).reshape(-1),
        (blocks == last).astype(f32).reshape(-1),
        ids,
        jnp.zeros_like(ids),
    ]
    info = jnp.pad(jnp.stack(columns, 1), ((RIM, RIM), (0, 0)))
    return info, blocks[:, None, :]


def middle_kernel(count, tok_ref, *refs):
    parts, (gain_ref, middle_ref, normed_ref) = refs[:count], refs[count:]
    middle = tok_ref[...].astype(f32)
    total = parts[0][...].astype(f32)
    for part in parts[1:]:
        total = total + part[...].astype(f32)
    middle = middle + total
    middle_ref[...] = middle
    scale = lax.rsqrt(jnp.mean(middle * middle, -1, keepdims=True) + EPS)
    normed_ref[...] = (middle * scale * gain_ref[...]).astype(bf16)


def feed_kernel(hidden, place_ref, *refs):
    x_refs, cot_refs, weights, refs = refs[:4], refs[4:8], refs[8:11], refs[11:]
    norm_refs, block_refs, cols_ref, refs = refs[:4], refs[4:8], refs[8], refs[9:]
    gate_w, up_w, down_w, sems = refs
    width = gate_w.shape[1]
    each = x_refs[0].shape[0]
    start = pl.multiple_of(place_ref[3], 128)
    window = pl.ds(start, width)
    copies = [
        pltpu.make_async_copy(weights[0].at[:, window], gate_w, sems.at[0]),
        pltpu.make_async_copy(weights[1].at[:, window], up_w, sems.at[1]),
        pltpu.make_async_copy(weights[2].at[window, :], down_w, sems.at[2]),
    ]
    for copy in copies:
        copy.start()
    lane = iota2((1, width), 1) - place_ref[4]
    mask = ((lane >= 0) & (lane < hidden)).astype(f32)
    for n, pair in enumerate(((1, 3), (0, 2))):
        x = jnp.concatenate([x_refs[p][...] for p in pair], 0)
        cot = jnp.concatenate([cot_refs[p][...] for p in pair], 0)
        if n == 0:
            copies[0].wait()
        gate = mm(x, gate_w[...])
        if n == 0:
            copies[1].wait()
        up = mm(x, up_w[...]) * mask
        sig = jax.nn.sigmoid(gate)
        silu = gate * sig * mask
        act = (silu * up).astype(bf16)
        if n == 0:
            copies[2].wait()
        grad = mm(cot, down_w[...], NT)
        ggate = (grad * up * sig * (1.0 + gate * (1.0 - sig))).astype(bf16)
        gup = (grad * silu).astype(bf16)
        gnorm = (mm(ggate, gate_w[...], NT) + mm(gup, up_w[...], NT)).astype(bf16)
        block = mm(act, down_w[...]).astype(bf16)
        for n, p in enumerate(pair):
            half, at = slice(n * each, (n + 1) * each), slice(p * each, (p + 1) * each)
            norm_refs[p][...] = gnorm[half]
            block_refs[p][...] = block[half]
            for k, value in enumerate((ggate, gup, act)):
                cols_ref[k, at, :] = value[half]


def feed_grads_kernel(seq_n, head_n, place_ref, *refs):
    x_refs, cot_refs, cols_ref, refs = refs[:4], refs[4:8], refs[8], refs[9:]
    out_ref, turned_ref, full_ref = refs
    each = x_refs[0].shape[0]
    half = full_ref.shape[0]
    rows = half // (seq_n * head_n)
    for n, blocks in enumerate((x_refs, cot_refs)):
        for p, ref in enumerate(blocks):
            turned_ref[n, :, p * each : (p + 1) * each] = jnp.transpose(ref[...])
    for k in range(3):
        for b in range(2):
            left = turned_ref[k // 2, b * half : (b + 1) * half, :]
            full_ref[...] = mm(left, cols_ref[k]).astype(bf16)
            for n in range(seq_n * head_n):
                first = ((n // 2 * 2 + b) * 2 + n % 2) * 3 + k
                out_ref[first * rows : (first + 1) * rows, :] = full_ref[n * rows : (n + 1) * rows, :]


def feed_group_kernel(place_ref, *refs):
    sum_ref, out_refs = refs[0], refs[1:]
    rows = out_refs[0].shape[0] // 2
    blocks = [sum_ref[n * rows : (n + 1) * rows, :] for n in range(4)]
    halves = [blocks[:2], blocks[2:]]
    for other, out_ref in enumerate(out_refs):
        odd = lax.rem(place_ref[0] + other, 2) == 1
        values = [jnp.where(odd, high, low) for low, high in halves]
        for n in range(2):
            core = lax.rem(place_ref[1] + n, 2) == 1
            out_ref[n * rows : (n + 1) * rows, :] = jnp.where(core, values[1], values[0])


def feed_out_kernel(hidden, place_ref, *refs):
    parts, (gate_ref, up_ref, down_ref) = refs[:4], refs[4:]
    rows = parts[0].shape[0] // 6
    own = lax.rem(place_ref[0], 2) * 2 + place_ref[1]
    for k, out_ref in enumerate((gate_ref, up_ref, down_ref)):
        values = [
            part[(n % 2 * 3 + k) * rows : (n % 2 * 3 + k + 1) * rows, :].astype(f32)
            for n, part in enumerate(parts)
        ]
        for g in range(4):
            value = values[0]
            for n in range(1, 4):
                value = jnp.where(own == (g ^ n), values[n], value)
            start = g * hidden % 128
            value = value[:, start : start + hidden]
            out_ref[:, g * hidden : (g + 1) * hidden] = value


def mixer_blocks_kernel(place_ref, own_ref, got_ref, *out_refs):
    extra = 8
    count = len(out_refs)
    half = own_ref.shape[0] - extra
    rows = half // count
    for shift, out_ref in enumerate(out_refs):
        at = pl.ds(pl.multiple_of(lax.rem(place_ref[2] + shift, count) * rows, 16), rows)
        out_ref[0:rows, :] = (own_ref[at, :] + got_ref[at, :].astype(f32)).astype(out_ref.dtype)
        small = own_ref[half:, :] + joined_parts(got_ref, half, extra)
        out_ref[rows:, :] = two_parts(small) if shift else small


def joined_parts(ref, start, extra):
    both = ref[start : start + 2 * extra, :].astype(f32)
    return both[:extra] + both[extra:]


def mixer_sum_kernel(count, nh, *refs):
    parts, out_refs = refs[:count], refs[count:]
    weight_refs, conv_refs, (decay_ref, gain_ref) = out_refs[:7], out_refs[7:10], out_refs[10:]
    rows = weight_refs[0].shape[0]
    nq = nh * 128
    starts = (0, nq, 3 * nq, 5 * nq, 5 * nq + 2 * nh, 5 * nq + 128, 6 * nq + 128)
    for n, (start, out_ref) in enumerate(zip(starts, weight_refs)):
        turned = n in (3, 4, 6)
        width = out_ref.shape[0] if turned else out_ref.shape[1]
        total = add_up([part[0:rows, start : start + width] for part in parts])
        out_ref[...] = jnp.transpose(total) if turned else total
    small = parts[0][rows:, :]
    for part in parts[1:]:
        small = small + joined_parts(part, rows, 8)
    for start, out_ref in zip(starts, conv_refs):
        out_ref[...] = small[0:4, start : start + out_ref.shape[1]]
    decay_ref[...] = small[4:5, 2 * nh : 3 * nh]
    gain_ref[...] = small[4:5, 128 : 128 + nq]


def norm_back(grad_normed, rows, gain):
    scale = lax.rsqrt(jnp.mean(rows * rows, -1, keepdims=True) + EPS)
    unit = rows * scale
    scaled = grad_normed * gain
    grad_rows = scale * (scaled - unit * jnp.mean(scaled * unit, -1, keepdims=True))
    return grad_rows, jnp.sum(grad_normed * unit, 0, keepdims=True)


def middle_back_kernel(a_ref, b_ref, c_ref, middle_ref, cot_ref, gain_ref, grad_ref, low_ref, sum_ref):
    total = a_ref[...].astype(f32) + b_ref[...].astype(f32) + c_ref[...].astype(f32)
    rows, sum_ref[...] = norm_back(total, middle_ref[...], gain_ref[...])
    grad = cot_ref[...].astype(f32) + rows
    grad_ref[...] = grad
    low_ref[...] = grad.astype(bf16)


def extra_rows_kernel(count, *refs):
    parts, (rim_ref, gains_ref) = refs[:count], refs[count:]
    each = parts[0].shape[0] - RIM
    total = add_up([part[each:, :] for part in parts])
    row = iota2((RIM, 1), 0)
    rim_ref[...] = jnp.where(row >= RIM - 3, total, 0.0).astype(bf16)
    gains_ref[...] = jnp.zeros(gains_ref.shape, f32)
    for n in range(2):
        gains_ref[n : n + 1, :] = total[2 * n : 2 * n + 1] + total[2 * n + 1 : 2 * n + 2]


def tokens_back_kernel(count, *refs):
    parts, (rim_ref, tok_ref, gain_ref, middle_ref, grad_ref) = refs[:count], refs[count:]
    each = tok_ref.shape[0]
    total = add_up([part[0:each, :] for part in parts])
    rim = rim_ref[...].astype(f32)
    total = total + jnp.concatenate([jnp.zeros((each - RIM, rim.shape[1]), f32), rim], 0)
    rows, _ = norm_back(total, tok_ref[...].astype(f32), gain_ref[...])
    grad_ref[...] = middle_ref[...] + rows


HEAD = ("pair", "half")


def axis_size(axis):
    return lax.axis_size(axis) if isinstance(axis, str) else lax.psum(1, axis)


def ring(value, axis):
    count = axis_size(axis)
    return [value] + [
        lax.ppermute(value, axis, [(i, (i + shift) % count) for i in range(count)])
        for shift in range(1, count)
    ]


def along(value, axis, shift):
    count = axis_size(axis)
    pairs = [(i, i + shift) for i in range(count) if 0 <= i + shift < count]
    return lax.ppermute(value, axis, pairs)


def crossed(value, axis, bit=0):
    return lax.ppermute(value, axis, [(i, i ^ (1 << bit)) for i in range(axis_size(axis))])


def spread(blocks, axis):
    count = axis_size(axis)
    return [blocks[0]] + [
        lax.ppermute(blocks[shift], axis, [(i, (i + shift) % count) for i in range(count)])
        for shift in range(1, count)
    ]


def add_up(parts):
    total = parts[0].astype(f32)
    for part in parts[1:]:
        total = total + part.astype(f32)
    return total


def sum_over(value, axis):
    return add_up(ring(value, axis))


def tied(*values):
    return lax.optimization_barrier(values)


def on_device(
    tokens, doc_ids, norm_gain, w_query, w_key, w_value, w_beta, w_decay, w_outgate, conv_query,
    conv_key, conv_value, decay_log, out_gain, w_out, mlp_gain, w_gate, w_up, w_down, cotangent,
):
    head_n, seq_n, batch_n = (axis_size(a) for a in (HEAD, "seq", "batch"))
    me = lax.axis_index(HEAD)
    nh = w_decay.shape[1]
    nq = nh * 128
    each, model = tokens.shape
    length = each * head_n
    me_array = me.astype(i32).reshape(1)

    head_last = head_n - 1
    blocks = ring(tokens, HEAD)
    seq_place = lax.axis_index("seq")
    core = lax.axis_index("batch")
    ways = 2 * batch_n
    hidden = w_gate.shape[1] // ways
    mine = ((me & 1) * batch_n + core) * hidden
    place = jnp.stack([me, core, seq_place, mine // 128 * 128, mine % 128]).astype(i32)
    window = -(-(hidden + 64) // 128) * 128
    ids = jnp.broadcast_to(doc_ids[-RIM:, None], (RIM, 128)).astype(bf16)
    tail = tied(jnp.concatenate([tokens[-RIM:], ids], 1), blocks[1])[0]
    rim = add_up(
        [
            lax.ppermute(
                tail,
                ("seq", *HEAD),
                [(s * head_n + head_last, (s + 1) * head_n + h) for s in range(seq_n - 1)],
            )
            for h in range(head_n)
        ]
    ).astype(bf16)
    info, doc_rows = token_info(doc_ids)
    w_small = jnp.pad(jnp.concatenate([w_beta, w_decay], 1), ((0, 0), (0, 128 - 3 * nh)))
    rate = jnp.pad(-jnp.exp(decay_log), (2 * nh, 128 - 3 * nh))[None]
    weights = (w_query, w_key, w_value, w_outgate, w_small)
    taps = (conv_query, conv_key, conv_value)
    gain = norm_gain[None]
    fwd = mixer_forward(me_array, blocks, rim, gain, weights, taps, info, doc_rows, rate)

    states = ring(fwd["low"], "seq")
    cot_near = crossed(tied(cotangent, *blocks[1:])[0], HEAD)
    cot_sent = tied(cotangent, cot_near, fwd["low"])
    cots = [cotangent, cot_near, *[crossed(value, "batch") for value in cot_sent[:2]]]
    out = mixer_output(place, states[1:], fwd, out_gain[None], w_out, head_n, after=cots[1:])

    low = lambda *shape: sds(*shape, dtype=bf16)
    parts = spread(out["branch"], HEAD)
    middle, normed_mid = kernel_call(
        functools.partial(middle_kernel, len(parts)), "middle",
        (tokens, *parts, mlp_gain[None]), [sds(each, model), low(each, model)],
    )
    near = crossed(normed_mid, HEAD)
    rows = [normed_mid, near, crossed(normed_mid, "batch"), crossed(near, "batch")]
    fed = pl.pallas_call(
        functools.partial(feed_kernel, hidden),
        name="feed",
        in_specs=[SMEM] + [VMEM] * 8 + [ANY] * 3,
        out_specs=[VMEM] * 9,
        out_shape=[low(each, model)] * 8 + [low(3, 4 * each, window)],
        scratch_shapes=[
            pltpu.VMEM((model, window), bf16), pltpu.VMEM((model, window), bf16),
            pltpu.VMEM((window, model), bf16), pltpu.SemaphoreType.DMA((3,)),
        ],
        compiler_params=pltpu.CompilerParams(vmem_limit_bytes=60 * MIB),
        cost_estimate=pl.CostEstimate(flops=10**10, bytes_accessed=0, transcendentals=0),
    )(place, *rows, *cots, w_gate, w_up, w_down)

    def own_parts(blocks):
        given = (blocks[1].astype(f32) + crossed(blocks[3], "batch").astype(f32)).astype(bf16)
        return given, (blocks[0], crossed(blocks[2], "batch"), crossed(given, HEAD))

    given, norm_parts = own_parts(fed[:4])
    block_own = crossed(fed[6], "batch")
    block_given = (fed[5].astype(f32) + crossed(fed[7], "batch").astype(f32)).astype(bf16)

    (feed_grads,) = kernel_call(
        functools.partial(feed_grads_kernel, seq_n, head_n), "feed_grads",
        (place, *rows, *cots, fed[8]), [low(3 * model, window)],
        scratch=[
            pltpu.VMEM((2, model, 4 * each), bf16), pltpu.VMEM((model // 2, window), bf16),
        ],
        after=[given], cost=8,
    )
    grad_middle, grad_branch, grad_mlp_gain = kernel_call(
        middle_back_kernel, "middle_back",
        (*norm_parts, middle, cotangent, mlp_gain[None]),
        [sds(each, model), low(each, model), sds(1, model)],
        after=[feed_grads],
    )
    grad_blocks = ring(grad_branch, HEAD)

    feed_sums = lax.psum_scatter(feed_grads, "seq", scatter_dimension=0, tiled=True)

    adj = mixer_adjoint(
        me_array, grad_blocks, w_out, fwd, out, out_gain[None], after=[block_given, block_own]
    )
    block_given = crossed(tied(adj["local"], block_given)[1], HEAD)
    block_out = (middle + add_up([fed[4], block_own, block_given])).astype(bf16)
    later = [along(adj["local"], "seq", -s) for s in range(seq_n - 1, 0, -1)]

    own_rows = model // (batch_n * seq_n * head_n)
    seq_rows = own_rows * head_n
    normed_parts, wide = mixer_backward(
        place, states[1:], later, fwd, out, adj, taps, rate,
        (w_query, w_key, w_value, w_small, w_outgate), gain, grad_mlp_gain, head_n,
        after=[block_given, feed_sums],
    )
    feed_sums = lax.psum_scatter(feed_sums, "pair", scatter_dimension=0, tiled=True)
    normed_parts = spread(normed_parts, HEAD)

    columns = wide[0].shape[1]
    wide_blocks = kernel_call(
        mixer_blocks_kernel, "mixer_blocks",
        (place, wide[0], crossed(wide[1], "batch")),
        [sds(seq_rows + 8, columns)] + [low(seq_rows + 16, columns)] * (seq_n - 1),
        after=[feed_sums],
    )
    wide_parts = spread(wide_blocks, "seq")
    extra, gains = kernel_call(
        functools.partial(extra_rows_kernel, head_n), "extra_rows", normed_parts,
        [low(RIM, model), sds(8, model)],
        after=wide_parts[1:2],
    )
    gains = add_up([gains, crossed(gains, "batch")])
    gain_parts = ring(gains, "seq")
    rim_part = lax.ppermute(
        extra,
        ("seq", *HEAD),
        [(s * head_n + head_last, (s - 1) * head_n + head_last) for s in range(1, seq_n)],
    )
    group_own, group_sent = kernel_call(
        feed_group_kernel, "feed_group", (place, feed_sums),
        [low(6 * own_rows, window)] * 2,
        after=[extra],
    )
    group_got = crossed(group_sent, HEAD)
    group = [group_own, crossed(group_own, "batch"), group_got, crossed(group_got, "batch")]
    grad_gate, grad_up, grad_down = kernel_call(
        functools.partial(feed_out_kernel, hidden), "feed_out", (place, *group),
        [sds(own_rows, ways * hidden)] * 3,
    )
    (grad_tokens,) = kernel_call(
        functools.partial(tokens_back_kernel, head_n), "tokens_back",
        (*normed_parts, rim_part, tokens, gain, grad_middle),
        [sds(each, model)],
    )
    *sums, grad_decay, grad_out_gain = kernel_call(
        functools.partial(mixer_sum_kernel, seq_n, nh), "mixer_sum", wide_parts,
        [sds(seq_rows, w) for w in (nq, 2 * nq, 2 * nq)] + [sds(w, seq_rows) for w in (2 * nh, nh)]
        + [sds(seq_rows, nq), sds(nq, seq_rows)]
        + [sds(4, w) for w in (nq, 2 * nq, 2 * nq)] + [sds(1, nh), sds(1, nq)],
    )
    grad_q, grad_k, grad_v, grad_b, grad_d, grad_g, grad_out, *grad_convs = sums
    gains = add_up(gain_parts)
    index = (core * seq_n + seq_place) * head_n + me
    gains = lax.dynamic_slice_in_dim(gains, index * own_rows, own_rows, 1)
    return (
        block_out, grad_tokens, gains[0], grad_q, grad_k, grad_v, grad_b.T, grad_d.T, grad_g,
        *grad_convs, grad_decay[0], grad_out_gain[0], grad_out, gains[1], grad_gate, grad_up,
        grad_down.T,
    )


def solution(mesh):
    batch, seq, head = mesh.devices.shape
    split_mesh = Mesh(mesh.devices.reshape(batch, seq, head // 2, 2), ("batch", "seq", *HEAD))
    return jax.shard_map(
        on_device,
        mesh=split_mesh,
        in_specs=(
            P(("batch", "seq", *HEAD), None),
            P(("batch", "seq")),
            P(),
            P(None, HEAD),
            P(None, HEAD),
            P(None, HEAD),
            P(None, HEAD),
            P(None, HEAD),
            P(None, HEAD),
            P(None, HEAD),
            P(None, HEAD),
            P(None, HEAD),
            P(HEAD),
            P(HEAD),
            P(HEAD, None),
            P(),
            P(),
            P(),
            P(),
            P(("batch", "seq", *HEAD), None),
        ),
        out_specs=(
            P(("batch", "seq", *HEAD), None),
            P(("batch", "seq", *HEAD), None),
            P(("batch", "seq", *HEAD)),
            P(("batch", "seq"), HEAD),
            P(("batch", "seq"), HEAD),
            P(("batch", "seq"), HEAD),
            P(("batch", "seq"), HEAD),
            P(("batch", "seq"), HEAD),
            P(("batch", "seq"), HEAD),
            P(None, HEAD),
            P(None, HEAD),
            P(None, HEAD),
            P(HEAD),
            P(HEAD),
            P(HEAD, ("batch", "seq")),
            P(("batch", "seq", *HEAD)),
            P(("batch", "seq", *HEAD), None),
            P(("batch", "seq", *HEAD), None),
            P(None, ("batch", "seq", *HEAD)),
        ),
        check_vma=False,
    )
```

time: 411 us -> 315 us (0.77)
  local copies, waits for them, and re-layouts: 67.4 us -> 15.5 us
  waiting for transfers between devices: 102 us -> 79 us
  starting transfers between devices: 93.1 us -> 71.9 us
  between operations: 2.17 us -> 14.5 us
  matrix products: 10.9 us -> 0 us
  other arithmetic: 16.2 us -> 7.76 us
  Pallas kernels: 117 us -> 124 us
    ppermute x36 -> x31, waiting for transfers between devices: 79.3 us -> 45.7 us  [the longest x9 24.4 us: spread(): lax.ppermute(blocks[shift], axis, [(i, (i + shift) % count) for i in rang...]
    ppermute x11 -> x3, starting transfers between devices: 25.4 us -> 4.08 us  [along(): return lax.ppermute(value, axis, pairs)]
    unnamed x104 -> x92, local copies, waits for them, and re-layouts: 24.5 us -> 9.08 us
    ppermute x13 -> x12, waiting for transfers between devices: 14.2 us -> 28.5 us  [ring(): lax.ppermute(value, axis, [(i, (i + shift) % count) for i in range(count)])]
    dynamic_slice x10 -> x0, local copies, waits for them, and re-layouts: 12.4 us -> none  [the longest x1 5.36 us: on_device(): up_w = lax.dynamic_slice_in_dim(w_up, mine, hidden, 1)]
    slice x18 -> x6, local copies, waits for them, and re-layouts: 12.7 us -> 1.52 us  [the longest x1 0.76 us: on_device(): tail = tied(jnp.concatenate([tokens[-RIM:], ids], 1), blocks[1])[0]]
    dot_general x4 -> x0, matrix products: 10.9 us -> none  [rows_dot(): lax.dot_general(left, right, (((0,), (0,)), ((), ())), preferred_element_...]
    convert_element_type x13 -> x4, other arithmetic: 11.5 us -> 3.96 us  [the longest x1 1.71 us: own_parts(): (blocks[1].astype(f32) + crossed(blocks[3], 'batch').astype(f32)).astype(...]
  transfers between devices with their start and end apart: 60 -> 48, of which waited for: 20 -> 20; matrix products, arithmetic and copies ran while one was open for 20% -> 4% of each run, Pallas kernels for 16% -> 29%
where the time goes in v2:
time: 315 us; the launch traced here: 312 us
  Pallas kernels  124 us (39%)
  waiting for transfers between devices  79 us (25%)
  starting transfers between devices  71.9 us (23%)
  local copies, waits for them, and re-layouts  15.5 us (5%)
  between operations  14.5 us (5%)
  other arithmetic  7.76 us (2%)
    pallas_call x13, Pallas kernels, kernel_call(): pl.pallas_call(run, name=name, in_specs=[SMEM if a.dtype == i32 else VMEM...  113 us
    ppermute x12, waiting for transfers between devices, ring(): lax.ppermute(value, axis, [(i, (i + shift) % count) for i in range(count)])  28.5 us
    ppermute x17, starting transfers between devices, crossed(): lax.ppermute(value, axis, [(i, i ^ 1 << bit) for i in range(axis_size(axi...  26.5 us
    ppermute x9, waiting for transfers between devices, spread(): lax.ppermute(blocks[shift], axis, [(i, (i + shift) % count) for i in rang...  24.4 us
    ppermute x17, waiting for transfers between devices, crossed(): lax.ppermute(value, axis, [(i, i ^ 1 << bit) for i in range(axis_size(axi...  21.3 us
    ppermute x12, starting transfers between devices, ring(): lax.ppermute(value, axis, [(i, (i + shift) % count) for i in range(count)])  20.5 us
    ppermute x9, starting transfers between devices, spread(): lax.ppermute(blocks[shift], axis, [(i, (i + shift) % count) for i in rang...  17.2 us
    pallas_call x1, Pallas kernels, on_device(): pl.pallas_call(functools.partial(feed_kernel, hidden), name='feed', in_sp...  10.6 us
  transfers between devices with their start and end apart: 48, of which 20 were waited for; matrix products, arithmetic and copies ran while one was open for 4% of the time, Pallas kernels for 29%

profile of v2, /device:TPU:0, one launch (start us, length us, event | category | flops | bytes accessed | tf_op | source)
XLA Modules:
  0.0 312.4 jit_solution(8032097547145945184)
XLA Ops:
  7.2 3.1 collective-permute-start
  10.3 2.6 collective-permute-start.1
  22.2 8.9 %collective-permute-done.1.refs_3_ = bf16[128,1024]{1,0:T(8,128)(2,1)S(1)} collective-permute-done((bf16[128,1024]{1,0:T(8,128)(2,1)}, bf16[128,1024]{1,0:T(8,128)(2,1)S(1)}, u32[]{:S(2)}, u32[]{:S(2)}) %collective-permute-start.1) | collective-permute-done | bytes 262176 | tf_op jit(solution)/shard_map/ppermute | solution.py:945
  34.8 3.6 %collective-permute-start.10 = (bf16[128,1024]{1,0:T(8,128)(2,1)}, bf16[128,1024]{1,0:T(8,128)(2,1)S(1)}, u32[]{:S(2)}, u32[]{:S(2)}) collective-permute-start(bf16[128,1024]{1,0:T(8,128)(2,1)} %refs_4_.3), channel_id=1, source_target_pairs={{0,1},{1,0},{2,3},{3,2},{4,5},{5,4},{6,7},{7,6},{8,9},{9,8},{10,11... | collective-permute-start | bytes 786440 | tf_op jit(solution)/shard_map/ppermute | solution.py:957
  39.1 26.0 %mixer_forward.1 = (bf16[528,1024]{1,0:T(8,128)(2,1)}, f32[528,1280]{1,0:T(8,128)}, f32[512,1280]{1,0:T(8,128)}, f32[512,256]{1,0:T(8,128)}, f32[512,256]{1,0:T(...) custom-call(s32[1]{0:T(128)} %bitcast.refs_0_, ...), custom_call_target="tpu_custom_call" | custom-call | flops 24999999488 | tf_op jit(solution)/shard_map/mixer_forward/pallas_call | solution.py:611
  70.8 2.4 collective-permute-done.7.refs_1_.refs_0_
  76.0 10.2 %mixer_output.1 = (f32[9,2,128,128]{3,2,1,0:T(8,128)}, f32[8,2,128,128]{3,2,1,0:T(8,128)}, f32[512,256]{1,0:T(8,128)}, bf16[512,256]{1,0:T(8,128)(2,1)}, bf16[12...) custom-call(s32[5]{0:T(128)} %stack.51.refs_0_.place_ref.refs_6_, ...), custom_call_target="tpu_custom_call" | custom-call | flops 10000000000 | tf_op jit(solution)/shard_map/mixer_output/pallas_call | solution.py:611
  87.1 5.6 %collective-permute-start.14 = (bf16[128,1024]{1,0:T(8,128)(2,1)}, bf16[128,1024]{1,0:T(8,128)(2,1)S(1)}, u32[]{:S(2)}, u32[]{:S(2)}) collective-permute-start(bf16[128,1024]{1,0:T(8,128)(2,1)} %get-tuple-element.116), channel_id=1, source_target_pairs={{0,2},{1,3},{2,0},{3,1},{4,6},{5,7},{6,4},{7,5},{8,10},{9,11},{10,... | collective-permute-start | bytes 786440 | tf_op jit(solution)/shard_map/ppermute | solution.py:963
  92.7 2.7 collective-permute-start.15
  95.4 4.2 %collective-permute-done.13.refs_2_ = bf16[128,1024]{1,0:T(8,128)(2,1)S(1)} collective-permute-done((bf16[128,1024]{1,0:T(8,128)(2,1)}, bf16[128,1024]{1,0:T(8,128)(2,1)S(1)}, u32[]{:S(2)}, u32[]{:S(2)}) %collective-permute-start.13) | collective-permute-done | bytes 262176 | tf_op jit(solution)/shard_map/ppermute | solution.py:963
  99.6 10.4 %collective-permute-done.14.refs_3_ = bf16[128,1024]{1,0:T(8,128)(2,1)S(1)} collective-permute-done((bf16[128,1024]{1,0:T(8,128)(2,1)}, bf16[128,1024]{1,0:T(8,128)(2,1)S(1)}, u32[]{:S(2)}, u32[]{:S(2)}) %collective-permute-start.14) | collective-permute-done | bytes 262176 | tf_op jit(solution)/shard_map/ppermute | solution.py:963
  110.8 2.4 middle.1
  113.2 6.0 %collective-permute-start.16 = (bf16[128,1024]{1,0:T(8,128)(2,1)}, bf16[128,1024]{1,0:T(8,128)(2,1)S(1)}, u32[]{:S(2)}, u32[]{:S(2)}) collective-permute-start(bf16[128,1024]{1,0:T(8,128)(2,1)} %get-tuple-element.119.refs_0_.refs_1_), channel_id=1, source_target_pairs={{0,1},{1,0},{2,3},{3,2},{4,5},{5,4},{6,7},{7,6},{8,9},{9,8},{10,11... | collective-permute-start | bytes 786440 | tf_op jit(solution)/shard_map/ppermute | solution.py:957
  119.2 6.7 %collective-permute-done.16.refs_1_.refs_2_ = bf16[128,1024]{1,0:T(8,128)(2,1)S(1)} collective-permute-done((bf16[128,1024]{1,0:T(8,128)(2,1)}, bf16[128,1024]{1,0:T(8,128)(2,1)S(1)}, u32[]{:S(2)}, u32[]{:S(2)}) %collective-permute-start.16) | collective-permute-done | bytes 262176 | tf_op jit(solution)/shard_map/ppermute | solution.py:957
  128.1 10.6 %feed.1 = (bf16[128,1024]{1,0:T(8,128)(2,1)}, bf16[128,1024]{1,0:T(8,128)(2,1)}, bf16[128,1024]{1,0:T(8,128)(2,1)}, bf16[128,1024]{1,0:T(8,128)(2,1)}, bf16[128,...) custom-call(s32[5]{0:T(128)} %stack.51.refs_0_.place_ref.refs_6_, ...), custom_call_target="tpu_custom_call" | custom-call | flops 10000000000 | tf_op jit(solution)/shard_map/feed/pallas_call | solution.py:1038
  142.3 7.2 %feed_grads.1.refs_6_ = bf16[3072,768]{1,0:T(8,128)(2,1)} custom-call(s32[5]{0:T(128)} %stack.51.refs_0_.place_ref.refs_6_, bf16[128,1024]{1,0:T(8,128)(2,1)} %get-tuple-element.119.refs_0_.refs_1_, bf16[128,1024]{1,0:T(8,128)(2,1)} %copy-done.28, bf16[128,1024]{1,0:T(8,128)(2,1)} %copy-done.30, bf16[128,1024]{1,0:T(8,128)(2,1)} %copy-done.33, ...), custom_call_target="tpu_custom_call" | custom-call | flops 8000000000 | tf_op jit(solution)/shard_map/feed_grads/pallas_call | solution.py:611
  152.9 6.3 %collective-permute-done.22.refs_2_ = bf16[128,1024]{1,0:T(8,128)(2,1)S(1)} collective-permute-done((bf16[128,1024]{1,0:T(8,128)(2,1)S(1)}, bf16[128,1024]{1,0:T(8,128)(2,1)S(1)}, u32[]{:S(2)}, u32[]{:S(2)}) %collective-permute-start.22) | collective-permute-done | bytes 262176 | tf_op jit(solution)/shard_map/ppermute | solution.py:957
  159.9 2.6 middle_back.1
  164.2 2.4 collective-permute-start.24
  168.6 5.3 %collective-permute-done.23.refs_2_ = bf16[128,1024]{1,0:T(8,128)(2,1)S(1)} collective-permute-done((bf16[128,1024]{1,0:T(8,128)(2,1)}, bf16[128,1024]{1,0:T(8,128)(2,1)S(1)}, u32[]{:S(2)}, u32[]{:S(2)}) %collective-permute-start.23) | collective-permute-done | bytes 262176 | tf_op jit(solution)/shard_map/ppermute | solution.py:945
  173.9 9.9 %collective-permute-done.24.refs_3_ = bf16[128,1024]{1,0:T(8,128)(2,1)S(1)} collective-permute-done((bf16[128,1024]{1,0:T(8,128)(2,1)}, bf16[128,1024]{1,0:T(8,128)(2,1)S(1)}, u32[]{:S(2)}, u32[]{:S(2)}) %collective-permute-start.24) | collective-permute-done | bytes 262176 | tf_op jit(solution)/shard_map/ppermute | solution.py:945
  184.5 9.8 %mixer_adjoint.1 = (f32[512,256]{1,0:T(8,128)}, f32[8,2,128,128]{3,2,1,0:T(8,128)}, f32[8,2,128,128]{3,2,1,0:T(8,128)}, bf16[512,256]{1,0:T(8,128)(2,1)}, f32[1,...) custom-call(s32[1]{0:T(128)} %bitcast.refs_0_, bf16[128,1024]{1,0:T(8,128)(2,1)} %get-tuple-element.127.refs_1_, ...), custom_call_target="tpu_custom_call" | custom-call | flops 10000000000 | tf_op jit(solution)/shard_map/mixer_adjoint/pallas_call | solution.py:611
  194.3 6.8 %collective-permute-start.27 = (bf16[128,1024]{1,0:T(8,128)(2,1)S(1)}, bf16[128,1024]{1,0:T(8,128)(2,1)S(1)}, u32[]{:S(2)}, u32[]{:S(2)}) collective-permute-start(bf16[128,1024]{1,0:T(8,128)(2,1)S(1)} %copy-done.2), channel_id=1, source_target_pairs={{0,1},{1,0},{2,3},{3,2},{4,5},{5,4},{6,7},{7,6},{8,9},{9,8},{10,11... | collective-permute-start | bytes 786440 | tf_op jit(solution)/shard_map/ppermute | solution.py:957
  206.2 2.3 collective-permute-done.28.refs_3_
  210.8 38.7 %mixer_backward.1 = (bf16[144,1024]{1,0:T(8,128)(2,1)}, bf16[144,1024]{1,0:T(8,128)(2,1)}, bf16[144,1024]{1,0:T(8,128)(2,1)}, bf16[144,1024]{1,0:T(8,128)(2,1)},...) custom-call(bf16[2,256,128]{2,1,0:T(8,128)(2,1)} %copy-done.39, bf16[2,256,128]{2,1,0:T(8,128)(2,1)} %copy-done.40, ...), custom_call_target="tpu_custom_call" | custom-call | flops 299999985664 | tf_op jit(solution)/shard_map/mixer_backward/pallas_call | solution.py:611
  249.7 4.2 %collective-permute-done.34.refs_2_ = bf16[528,1920]{1,0:T(8,128)(2,1)S(1)} collective-permute-done((bf16[528,1920]{1,0:T(8,128)(2,1)}, bf16[528,1920]{1,0:T(8,128)(2,1)S(1)}, u32[]{:S(2)}, u32[]{:S(2)}) %collective-permute-start.34) | collective-permute-done | bytes 2027552 | tf_op jit(solution)/shard_map/ppermute | solution.py:957
  255.2 4.7 %mixer_blocks.1 = (f32[136,1920]{1,0:T(8,128)}, bf16[144,1920]{1,0:T(8,128)(2,1)}, bf16[144,1920]{1,0:T(8,128)(2,1)}, bf16[144,1920]{1,0:T(8,128)(2,1)}) custom-call(s32[5]{0:T(128)} %stack.51.refs_0_.place_ref.refs_6_, f32[520,1920]{1,0:T(8,128)} %get-tuple-element.159.refs_1_, bf16[528,1920]{1,0:T(8,128)(2,1)} %copy-done.10, ...), custom_call_target="tpu_custom_call" | custom-call | flops 2000000000 | tf_op jit(solution)/shard_map/mixer_blocks/pallas_call | solution.py:611
  264.9 2.9 collective-permute-start.42
  268.7 9.1 %collective-permute-done.32.refs_2_ = bf16[144,1024]{1,0:T(8,128)(2,1)S(1)} collective-permute-done((bf16[144,1024]{1,0:T(8,128)(2,1)}, bf16[144,1024]{1,0:T(8,128)(2,1)S(1)}, u32[]{:S(2)}, u32[]{:S(2)}) %collective-permute-start.32) | collective-permute-done | bytes 294944 | tf_op jit(solution)/shard_map/ppermute | solution.py:963
  283.9 6.2 %collective-permute-start.44 = (bf16[192,768]{1,0:T(8,128)(2,1)}, bf16[192,768]{1,0:T(8,128)(2,1)S(1)}, u32[]{:S(2)}, u32[]{:S(2)}) collective-permute-start(bf16[192,768]{1,0:T(8,128)(2,1)} %get-tuple-element.181), channel_id=1, source_target_pairs={{0,1},{1,0},{2,3},{3,2},{4,5},{5,4},{6,7},{7,6},{8,9},{9,8},{10,11... | collective-permute-start | bytes 884744 | tf_op jit(solution)/shard_map/ppermute | solution.py:957
  291.5 2.8 mixer_sum.1
  298.2 2.6 tokens_back.1
  (208 shorter events, 68.7 us)
Async XLA Ops:
  7.2 199.0 %reduce-scatter.3.cloned.1.call-start = ((), (), s32[]{:S(2)}) async-start(), calls=%async_computation.2 | async-start | bytes 5898240 | tf_op jit(solution)/shard_map/reduce_scatter | solution.py:1076
  7.2 12.9 %collective-permute-start = (bf16[128,1024]{1,0:T(8,128)(2,1)}, bf16[128,1024]{1,0:T(8,128)(2,1)S(1)}, u32[]{:S(2)}, u32[]{:S(2)}) collective-permute-start(bf16[128,1024]{1,0:T(8,128)(2,1)} %refs_5_.5), channel_id=1, source_target_pairs={{0,1},{1,2},{2,3},{3,0},{4,5},{5,6},{6,7},{7,4},{8,9},{9,10},{10,1... | collective-permute-start | bytes 786440 | tf_op jit(solution)/shard_map/ppermute | solution.py:945
  10.3 20.7 %collective-permute-start.1 = (bf16[128,1024]{1,0:T(8,128)(2,1)}, bf16[128,1024]{1,0:T(8,128)(2,1)S(1)}, u32[]{:S(2)}, u32[]{:S(2)}) collective-permute-start(bf16[128,1024]{1,0:T(8,128)(2,1)} %refs_5_.5), channel_id=1, source_target_pairs={{0,2},{1,3},{2,0},{3,1},{4,6},{5,7},{6,4},{7,5},{8,10},{9,11},{10,... | collective-permute-start | bytes 786440 | tf_op jit(solution)/shard_map/ppermute | solution.py:945
  12.9 21.9 %collective-permute-start.2 = (bf16[128,1024]{1,0:T(8,128)(2,1)}, bf16[128,1024]{1,0:T(8,128)(2,1)S(1)}, u32[]{:S(2)}, u32[]{:S(2)}) collective-permute-start(bf16[128,1024]{1,0:T(8,128)(2,1)} %refs_5_.5), channel_id=1, source_target_pairs={{0,3},{1,0},{2,1},{3,2},{4,7},{5,4},{6,5},{7,6},{8,11},{9,8},{10,9... | collective-permute-start | bytes 786440 | tf_op jit(solution)/shard_map/ppermute | solution.py:945
  20.1 18.3 %collective-permute-start.3 = (bf16[16,1152]{1,0:T(8,128)(2,1)S(1)}, bf16[16,1152]{1,0:T(8,128)(2,1)S(1)}, u32[]{:S(2)}, u32[]{:S(2)}) collective-permute-start(bf16[16,1152]{1,0:T(8,128)(2,1)S(1)} %pad_maximum_fusion), channel_id=1, source_target_pairs={{3,4},{7,8},{11,12},{19,20},{23,24},{27,28}} | collective-permute-start | bytes 110600 | tf_op jit(solution)/shard_map/ppermute | solution.py:1008
  20.8 17.6 %collective-permute-start.4 = (bf16[16,1152]{1,0:T(8,128)(2,1)S(1)}, bf16[16,1152]{1,0:T(8,128)(2,1)S(1)}, u32[]{:S(2)}, u32[]{:S(2)}) collective-permute-start(bf16[16,1152]{1,0:T(8,128)(2,1)S(1)} %pad_maximum_fusion), channel_id=1, source_target_pairs={{3,5},{7,9},{11,13},{19,21},{23,25},{27,29}} | collective-permute-start | bytes 110600 | tf_op jit(solution)/shard_map/ppermute | solution.py:1008
  21.5 17.0 %collective-permute-start.5 = (bf16[16,1152]{1,0:T(8,128)(2,1)S(1)}, bf16[16,1152]{1,0:T(8,128)(2,1)S(1)}, u32[]{:S(2)}, u32[]{:S(2)}) collective-permute-start(bf16[16,1152]{1,0:T(8,128)(2,1)S(1)} %pad_maximum_fusion), channel_id=1, source_target_pairs={{3,6},{7,10},{11,14},{19,22},{23,26},{27,30}} | collective-permute-start | bytes 110600 | tf_op jit(solution)/shard_map/ppermute | solution.py:1008
  34.8 30.3 %collective-permute-start.10 = (bf16[128,1024]{1,0:T(8,128)(2,1)}, bf16[128,1024]{1,0:T(8,128)(2,1)S(1)}, u32[]{:S(2)}, u32[]{:S(2)}) collective-permute-start(bf16[128,1024]{1,0:T(8,128)(2,1)} %refs_4_.3), channel_id=1, source_target_pairs={{0,1},{1,0},{2,3},{3,2},{4,5},{5,4},{6,7},{7,6},{8,9},{9,8},{10,11... | collective-permute-start | bytes 786440 | tf_op jit(solution)/shard_map/ppermute | solution.py:957
  65.1 10.1 %collective-permute-start.11 = (bf16[128,1024]{1,0:T(8,128)(2,1)S(1)}, bf16[128,1024]{1,0:T(8,128)(2,1)S(1)}, u32[]{:S(2)}, u32[]{:S(2)}) collective-permute-start(bf16[128,1024]{1,0:T(8,128)(2,1)S(1)} %copy-done.18), channel_id=1, source_target_pairs={{0,16},{16,0},{1,17},{17,1},{2,18},{18,2},{3,19},{19,3},{4,20},{20... | collective-permute-start | bytes 786440 | tf_op jit(solution)/shard_map/ppermute | solution.py:957
  65.2 10.0 %collective-permute-start.12 = (bf16[128,1024]{1,0:T(8,128)(2,1)S(1)}, bf16[128,1024]{1,0:T(8,128)(2,1)S(1)}, u32[]{:S(2)}, u32[]{:S(2)}) collective-permute-start(bf16[128,1024]{1,0:T(8,128)(2,1)S(1)} %collective-permute-done.10.refs_13_.refs_5_.refs_6_), channel_id=1, source_target_pairs={{0,16},{16,0},{1,17},{17,1},{2,18},{18,2},{3,19},{19,3},{4,20},{20... | collective-permute-start | bytes 786440 | tf_op jit(solution)/shard_map/ppermute | solution.py:957
  67.2 7.9 %collective-permute-start.8 = (bf16[2,256,128]{2,1,0:T(8,128)(2,1)}, bf16[2,256,128]{2,1,0:T(8,128)(2,1)S(1)}, u32[]{:S(2)}, u32[]{:S(2)}) collective-permute-start(bf16[2,256,128]{2,1,0:T(8,128)(2,1)} %get-tuple-element.103), channel_id=1, source_target_pairs={{0,8},{4,12},{8,0},{12,4},{1,9},{5,13},{9,1},{13,5},{2,10},{6,14},... | collective-permute-start | bytes 393224 | tf_op jit(solution)/shard_map/ppermute | solution.py:945
  86.2 13.4 %collective-permute-start.13 = (bf16[128,1024]{1,0:T(8,128)(2,1)}, bf16[128,1024]{1,0:T(8,128)(2,1)S(1)}, u32[]{:S(2)}, u32[]{:S(2)}) collective-permute-start(bf16[128,1024]{1,0:T(8,128)(2,1)} %get-tuple-element.115), channel_id=1, source_target_pairs={{0,1},{1,2},{2,3},{3,0},{4,5},{5,6},{6,7},{7,4},{8,9},{9,10},{10,1... | collective-permute-start | bytes 786440 | tf_op jit(solution)/shard_map/ppermute | solution.py:963
  87.1 22.9 %collective-permute-start.14 = (bf16[128,1024]{1,0:T(8,128)(2,1)}, bf16[128,1024]{1,0:T(8,128)(2,1)S(1)}, u32[]{:S(2)}, u32[]{:S(2)}) collective-permute-start(bf16[128,1024]{1,0:T(8,128)(2,1)} %get-tuple-element.116), channel_id=1, source_target_pairs={{0,2},{1,3},{2,0},{3,1},{4,6},{5,7},{6,4},{7,5},{8,10},{9,11},{10,... | collective-permute-start | bytes 786440 | tf_op jit(solution)/shard_map/ppermute | solution.py:963
  92.7 17.3 %collective-permute-start.15 = (bf16[128,1024]{1,0:T(8,128)(2,1)}, bf16[128,1024]{1,0:T(8,128)(2,1)S(1)}, u32[]{:S(2)}, u32[]{:S(2)}) collective-permute-start(bf16[128,1024]{1,0:T(8,128)(2,1)} %get-tuple-element.117), channel_id=1, source_target_pairs={{0,3},{1,0},{2,1},{3,2},{4,7},{5,4},{6,5},{7,6},{8,11},{9,8},{10,9... | collective-permute-start | bytes 786440 | tf_op jit(solution)/shard_map/ppermute | solution.py:963
  113.2 12.7 %collective-permute-start.16 = (bf16[128,1024]{1,0:T(8,128)(2,1)}, bf16[128,1024]{1,0:T(8,128)(2,1)S(1)}, u32[]{:S(2)}, u32[]{:S(2)}) collective-permute-start(bf16[128,1024]{1,0:T(8,128)(2,1)} %get-tuple-element.119.refs_0_.refs_1_), channel_id=1, source_target_pairs={{0,1},{1,0},{2,3},{3,2},{4,5},{5,4},{6,7},{7,6},{8,9},{9,8},{10,11... | collective-permute-start | bytes 786440 | tf_op jit(solution)/shard_map/ppermute | solution.py:957
  149.6 104.3 %reduce-scatter.5.cloned.1.call-start = ((), (), s32[]{:S(2)}) async-start(), calls=%async_computation.3 | async-start | bytes 1769472 | tf_op jit(solution)/shard_map/reduce_scatter | solution.py:1092
  150.6 8.6 %collective-permute-start.22 = (bf16[128,1024]{1,0:T(8,128)(2,1)S(1)}, bf16[128,1024]{1,0:T(8,128)(2,1)S(1)}, u32[]{:S(2)}, u32[]{:S(2)}) collective-permute-start(bf16[128,1024]{1,0:T(8,128)(2,1)S(1)} %copy-done.3), channel_id=1, source_target_pairs={{0,1},{1,0},{2,3},{3,2},{4,5},{5,4},{6,7},{7,6},{8,9},{9,8},{10,11... | collective-permute-start | bytes 786440 | tf_op jit(solution)/shard_map/ppermute | solution.py:957
  152.4 15.4 %collective-permute-start.26 = (bf16[128,1024]{1,0:T(8,128)(2,1)S(1)}, bf16[128,1024]{1,0:T(8,128)(2,1)S(1)}, u32[]{:S(2)}, u32[]{:S(2)}) collective-permute-start(bf16[128,1024]{1,0:T(8,128)(2,1)S(1)} %copy-done.26), channel_id=1, source_target_pairs={{0,16},{16,0},{1,17},{17,1},{2,18},{18,2},{3,19},{19,3},{4,20},{20... | collective-permute-start | bytes 786440 | tf_op jit(solution)/shard_map/ppermute | solution.py:957
  152.4 16.1 %collective-permute-start.19 = (bf16[128,1024]{1,0:T(8,128)(2,1)S(1)}, bf16[128,1024]{1,0:T(8,128)(2,1)S(1)}, u32[]{:S(2)}, u32[]{:S(2)}) collective-permute-start(bf16[128,1024]{1,0:T(8,128)(2,1)S(1)} %copy-done.25), channel_id=1, source_target_pairs={{0,16},{16,0},{1,17},{17,1},{2,18},{18,2},{3,19},{19,3},{4,20},{20... | collective-permute-start | bytes 786440 | tf_op jit(solution)/shard_map/ppermute | solution.py:957
  162.5 11.4 %collective-permute-start.23 = (bf16[128,1024]{1,0:T(8,128)(2,1)}, bf16[128,1024]{1,0:T(8,128)(2,1)S(1)}, u32[]{:S(2)}, u32[]{:S(2)}) collective-permute-start(bf16[128,1024]{1,0:T(8,128)(2,1)} %get-tuple-element.127.refs_1_), channel_id=1, source_target_pairs={{0,1},{1,2},{2,3},{3,0},{4,5},{5,6},{6,7},{7,4},{8,9},{9,10},{10,1... | collective-permute-start | bytes 786440 | tf_op jit(solution)/shard_map/ppermute | solution.py:945
  164.2 19.5 %collective-permute-start.24 = (bf16[128,1024]{1,0:T(8,128)(2,1)}, bf16[128,1024]{1,0:T(8,128)(2,1)S(1)}, u32[]{:S(2)}, u32[]{:S(2)}) collective-permute-start(bf16[128,1024]{1,0:T(8,128)(2,1)} %get-tuple-element.127.refs_1_), channel_id=1, source_target_pairs={{0,2},{1,3},{2,0},{3,1},{4,6},{5,7},{6,4},{7,5},{8,10},{9,11},{10,... | collective-permute-start | bytes 786440 | tf_op jit(solution)/shard_map/ppermute | solution.py:945
  166.6 17.2 %collective-permute-start.25 = (bf16[128,1024]{1,0:T(8,128)(2,1)}, bf16[128,1024]{1,0:T(8,128)(2,1)S(1)}, u32[]{:S(2)}, u32[]{:S(2)}) collective-permute-start(bf16[128,1024]{1,0:T(8,128)(2,1)} %get-tuple-element.127.refs_1_), channel_id=1, source_target_pairs={{0,3},{1,0},{2,1},{3,2},{4,7},{5,4},{6,5},{7,6},{8,11},{9,8},{10,9... | collective-permute-start | bytes 786440 | tf_op jit(solution)/shard_map/ppermute | solution.py:945
  194.3 15.8 %collective-permute-start.27 = (bf16[128,1024]{1,0:T(8,128)(2,1)S(1)}, bf16[128,1024]{1,0:T(8,128)(2,1)S(1)}, u32[]{:S(2)}, u32[]{:S(2)}) collective-permute-start(bf16[128,1024]{1,0:T(8,128)(2,1)S(1)} %copy-done.2), channel_id=1, source_target_pairs={{0,1},{1,0},{2,3},{3,2},{4,5},{5,4},{6,7},{7,6},{8,9},{9,8},{10,11... | collective-permute-start | bytes 786440 | tf_op jit(solution)/shard_map/ppermute | solution.py:957
  249.6 15.3 %collective-permute-start.31 = (bf16[144,1024]{1,0:T(8,128)(2,1)}, bf16[144,1024]{1,0:T(8,128)(2,1)}, u32[]{:S(2)}, u32[]{:S(2)}) collective-permute-start(bf16[144,1024]{1,0:T(8,128)(2,1)} %get-tuple-element.156), channel_id=1, source_target_pairs={{0,1},{1,2},{2,3},{3,0},{4,5},{5,6},{6,7},{7,4},{8,9},{9,10},{10,1... | collective-permute-start | bytes 884744 | tf_op jit(solution)/shard_map/ppermute | solution.py:963
  259.9 18.6 %collective-permute-start.35 = (bf16[144,1920]{1,0:T(8,128)(2,1)}, bf16[144,1920]{1,0:T(8,128)(2,1)S(1)}, u32[]{:S(2)}, u32[]{:S(2)}) collective-permute-start(bf16[144,1920]{1,0:T(8,128)(2,1)} %get-tuple-element.161), channel_id=1, source_target_pairs={{0,4},{4,8},{8,12},{12,0},{1,5},{5,9},{9,13},{13,1},{2,6},{6,10},{... | collective-permute-start | bytes 1658888 | tf_op jit(solution)/shard_map/ppermute | solution.py:963
  262.0 15.8 %collective-permute-start.32 = (bf16[144,1024]{1,0:T(8,128)(2,1)}, bf16[144,1024]{1,0:T(8,128)(2,1)S(1)}, u32[]{:S(2)}, u32[]{:S(2)}) collective-permute-start(bf16[144,1024]{1,0:T(8,128)(2,1)} %get-tuple-element.157), channel_id=1, source_target_pairs={{0,2},{1,3},{2,0},{3,1},{4,6},{5,7},{6,4},{7,5},{8,10},{9,11},{10,... | collective-permute-start | bytes 884744 | tf_op jit(solution)/shard_map/ppermute | solution.py:963
  263.4 15.1 %collective-permute-start.33 = (bf16[144,1024]{1,0:T(8,128)(2,1)}, bf16[144,1024]{1,0:T(8,128)(2,1)}, u32[]{:S(2)}, u32[]{:S(2)}) collective-permute-start(bf16[144,1024]{1,0:T(8,128)(2,1)} %get-tuple-element.158), channel_id=1, source_target_pairs={{0,3},{1,0},{2,1},{3,2},{4,7},{5,4},{6,5},{7,6},{8,11},{9,8},{10,9... | collective-permute-start | bytes 884744 | tf_op jit(solution)/shard_map/ppermute | solution.py:963
  264.4 25.7 %collective-permute-start.41 = (bf16[144,1920]{1,0:T(8,128)(2,1)}, bf16[144,1920]{1,0:T(8,128)(2,1)S(1)}, u32[]{:S(2)}, u32[]{:S(2)}) collective-permute-start(bf16[144,1920]{1,0:T(8,128)(2,1)} %get-tuple-element.166), channel_id=1, source_target_pairs={{0,8},{4,12},{8,0},{12,4},{1,9},{5,13},{9,1},{13,5},{2,10},{6,14},... | collective-permute-start | bytes 1658888 | tf_op jit(solution)/shard_map/ppermute | solution.py:963
  264.9 25.8 %collective-permute-start.42 = (bf16[144,1920]{1,0:T(8,128)(2,1)}, bf16[144,1920]{1,0:T(8,128)(2,1)S(1)}, u32[]{:S(2)}, u32[]{:S(2)}) collective-permute-start(bf16[144,1920]{1,0:T(8,128)(2,1)} %get-tuple-element.167), channel_id=1, source_target_pairs={{0,12},{4,0},{8,4},{12,8},{1,13},{5,1},{9,5},{13,9},{2,14},{6,2},{... | collective-permute-start | bytes 1658888 | tf_op jit(solution)/shard_map/ppermute | solution.py:963
  281.2 15.3 %collective-permute-start.36 = (bf16[16,1024]{1,0:T(8,128)(2,1)}, bf16[16,1024]{1,0:T(8,128)(2,1)S(1)}, u32[]{:S(2)}, u32[]{:S(2)}) collective-permute-start(bf16[16,1024]{1,0:T(8,128)(2,1)} %get-tuple-element.162.refs_2_), channel_id=1, source_target_pairs={{7,3},{11,7},{15,11},{23,19},{27,23},{31,27}} | collective-permute-start | bytes 98312 | tf_op jit(solution)/shard_map/ppermute | solution.py:1110
  283.9 16.9 %collective-permute-start.44 = (bf16[192,768]{1,0:T(8,128)(2,1)}, bf16[192,768]{1,0:T(8,128)(2,1)S(1)}, u32[]{:S(2)}, u32[]{:S(2)}) collective-permute-start(bf16[192,768]{1,0:T(8,128)(2,1)} %get-tuple-element.181), channel_id=1, source_target_pairs={{0,1},{1,0},{2,3},{3,2},{4,5},{5,4},{6,7},{7,6},{8,9},{9,8},{10,11... | collective-permute-start | bytes 884744 | tf_op jit(solution)/shard_map/ppermute | solution.py:957
  290.1 11.5 %collective-permute-start.43 = (bf16[192,768]{1,0:T(8,128)(2,1)}, bf16[192,768]{1,0:T(8,128)(2,1)S(1)}, u32[]{:S(2)}, u32[]{:S(2)}) collective-permute-start(bf16[192,768]{1,0:T(8,128)(2,1)} %get-tuple-element.180.refs_1_), channel_id=1, source_target_pairs={{0,16},{16,0},{1,17},{17,1},{2,18},{18,2},{3,19},{19,3},{4,20},{20... | collective-permute-start | bytes 884744 | tf_op jit(solution)/shard_map/ppermute | solution.py:957
  (62 other events, 300.2 us)
Sparse Core Ops, SparseCore 0:
  149.7 56.4 reduce-scatter.2
  208.4 36.6 reduce-scatter.4
